TPU v7x, 32 devices: a whole 2x2x4 slice. The times are simulated.
32 devices in a mesh: dp: 4 (over y, x), fsdp: 8 (over z, core).
Axes of the slice: x: 2, y: 2, z: 4, core: 2. Of those that a mesh axis runs over, the one named last changes fastest.
Arguments:
- layer_entering_state: bfloat16 [24576, 1024], P(('dp', 'fsdp')), may hold values from -6 to 6
- exit_cotangent: bfloat16 [24576, 1024], P(('dp', 'fsdp')), may hold values from -6 to 6
- attend_norm_scaling: bfloat16 [1024], P('fsdp'), may hold values from 0.5 to 1.5
- branch_norm_scaling: bfloat16 [1024], P('fsdp'), may hold values from 0.5 to 1.5
- triple_coefficients: bfloat16 [1024, 2048], P('fsdp'), may hold values from -0.1875 to 0.1875
- attend_exit_coefficients: bfloat16 [1024, 1024], P('fsdp'), may hold values from -1.5 to 1.5
- dispatch_coefficients: bfloat16 [1024, 32], P('fsdp'), may hold values from -0.09375 to 0.09375
- branch_widen_coefficients: bfloat16 [32, 1024, 1024], P('dp', 'fsdp'), may hold values from -0.1875 to 0.1875
- branch_contract_coefficients: bfloat16 [32, 512, 1024], P('dp', 'fsdp'), may hold values from -1.5 to 1.5
- triple_plugin_source: bfloat16 [1024, 384], P('fsdp'), may hold values from -0.1875 to 0.1875
- asking_plugin_target: bfloat16 [128, 1024], P(None, 'fsdp'), may hold values from -0.75 to 0.75
- lookup_plugin_target: bfloat16 [128, 512], P(None, 'fsdp'), may hold values from -0.75 to 0.75
- content_plugin_target: bfloat16 [128, 512], P(None, 'fsdp'), may hold values from -0.75 to 0.75
- merge_plugin_source: bfloat16 [1024, 128], P('fsdp'), may hold values from -1.5 to 1.5
- merge_plugin_target: bfloat16 [128, 1024], P(None, 'fsdp'), may hold values from -0.75 to 0.75
- dispatch_plugin_source: bfloat16 [1024, 128], P('fsdp'), may hold values from -0.1875 to 0.1875
- dispatch_plugin_target: bfloat16 [128, 32], P('fsdp'), may hold values from -0.375 to 0.375
- branch_plugin_source: bfloat16 [32, 1024, 256], P('dp', 'fsdp'), may hold values from -0.1875 to 0.1875
- branch_plugin_target: bfloat16 [32, 2, 128, 512], P('dp', None, None, 'fsdp'), may hold values from -0.75 to 0.75
- contract_plugin_source: bfloat16 [32, 512, 128], P('dp', 'fsdp'), may hold values from -0.25 to 0.25
- contract_plugin_target: bfloat16 [32, 128, 1024], P('dp', None, 'fsdp'), may hold values from -4 to 4
- branch_choice_labels: int32 [24576, 8], P(('dp', 'fsdp')), may hold values from 0 to 31, all different within a row; in each aligned block of 384 rows (0 to 383, 384 to 767, ...) at most 108 rows name the same one
- plugin_choice_per_text: int32 [4, 16], P(None, 'fsdp'), may hold values from 0 to 7
- section_labels: int32 [64, 384], P(('dp', 'fsdp')), may hold values from 0 to 2, never falling along the last dimension, each value on 1 to 256 neighbouring positions
Outputs:
- block_out: bfloat16 [24576, 1024], P(('dp', 'fsdp'))
- grad_input: bfloat16 [24576, 1024], P(('dp', 'fsdp'))
- qkv_reduce_grad: float32 [1024, 384], P('fsdp')
- q_expand_grad: float32 [128, 1024], P(None, 'fsdp')
- k_expand_grad: float32 [128, 512], P(None, 'fsdp')
- v_expand_grad: float32 [128, 512], P(None, 'fsdp')
- out_reduce_grad: float32 [1024, 128], P('fsdp')
- out_expand_grad: float32 [128, 1024], P(None, 'fsdp')
- route_reduce_grad: float32 [1024, 128], P('fsdp')
- route_expand_grad: float32 [128, 32], P('fsdp')
- expert_reduce_grad: float32 [32, 1024, 256], P('dp', 'fsdp')
- expert_expand_grad: float32 [32, 2, 128, 512], P('dp', None, None, 'fsdp')
- down_reduce_grad: float32 [32, 512, 128], P('dp', 'fsdp')
- down_expand_grad: float32 [32, 128, 1024], P('dp', None, 'fsdp')
Inputs may be any that keep to these rules, and one draw needn't show every extreme that they name: `branch_choice_labels`: each row names 8 different experts. Within the 384 rows of one sequence no expert is named more than 108 times, and in every draw some expert is named exactly 108 times in some sequence. `section_labels`: within each sequence the block numbers never fall, every number from 0 to 2 occurs, and each block holds 1 to 256 positions.
All inputs are finite; a program needn't handle non-finite values.
Results may differ from a plain program's by a relative error of at most 0.023.
Values may be sent and summed in bfloat16 or wider, within the bound.
No kernel may reach another device: no remote copies, remote signals or barrier semaphores. Data moves between devices by JAX's collectives and lax.ppermute only.
A program may use at most 384 MiB of HBM per device.

v0:
```python
import jax
import jax.numpy as jnp
from jax import lax
from jax.sharding import PartitionSpec as P

H = 16
KVH = 8
HD = 64
FEEDFORWARD_SIZE = 512
PLUGIN_CHOICES = 8
REDUCED_DIM = 16


eps_norm = 1e-06
rope_base = 10000.0


def matrix_product(operand, factor):
    return jnp.dot(operand, factor, preferred_element_type=jnp.float32)


def matrix_product_transposed(operand, factor):
    return lax.dot_general(
        operand, factor, (((1,), (1,)), ((), ())), preferred_element_type=jnp.float32
    )


def outer_product_sum(operand, factor):
    return lax.dot_general(
        operand, factor, (((0,), (0,)), ((), ())), preferred_element_type=jnp.float32
    )


def layered_times_effect(pattern, operand, factor):
    return jnp.einsum(pattern, operand, factor, preferred_element_type=jnp.float32)


def norm_scale(values, gain_vec):
    inverse = lax.rsqrt(jnp.mean(values * values, axis=-1, keepdims=True) + eps_norm)
    return (values * inverse * gain_vec, inverse)


def norm_back(values, inverse, gain_vec, upstream):
    scaled = gain_vec * upstream
    feature_count = values.shape[-1]
    weighted_sum = jnp.sum(values * scaled, axis=-1, keepdims=True)
    return inverse * scaled - values * (inverse * inverse * inverse) * weighted_sum / feature_count


def rotation(length, head_size):
    half_size = head_size // 2
    frequency = rope_base ** (-(2.0 * jnp.arange(half_size, dtype=jnp.float32)) / head_size)
    angles = jnp.arange(length, dtype=jnp.float32)[:, None] * frequency[None, :]
    return (jnp.cos(angles)[:, None, :], jnp.sin(angles)[:, None, :])


def rotate(values, cos_table, sin_table):
    half_size = values.shape[-1] // 2
    leading = values[..., :half_size]
    trailing = values[..., half_size:]
    return jnp.concatenate(
        [leading * cos_table - trailing * sin_table, trailing * cos_table + leading * sin_table],
        axis=-1,
    )


def rotate_back(values, cos_table, sin_table):
    half_size = values.shape[-1] // 2
    leading = values[..., :half_size]
    trailing = values[..., half_size:]
    return jnp.concatenate(
        [leading * cos_table + trailing * sin_table, trailing * cos_table - leading * sin_table],
        axis=-1,
    )


def to_owners(rows_block):
    return lax.all_to_all(rows_block, "dp", split_axis=1, concat_axis=1, tiled=True)


def from_owners(rows_block):
    return lax.all_to_all(rows_block, "dp", split_axis=1, concat_axis=1, tiled=True)


def local(
    layer_entering_state,
    exit_cotangent,
    attend_norm_scaling,
    branch_norm_scaling,
    triple_coefficients,
    attend_exit_coefficients,
    dispatch_coefficients,
    branch_widen_coefficients,
    branch_contract_coefficients,
    triple_plugin_source,
    asking_plugin_target,
    lookup_plugin_target,
    content_plugin_target,
    merge_plugin_source,
    merge_plugin_target,
    dispatch_plugin_source,
    dispatch_plugin_target,
    branch_plugin_source,
    branch_plugin_target,
    contract_plugin_source,
    contract_plugin_target,
    branch_choice_labels,
    plugin_choice_per_text,
    section_labels,
):
    data_parallel_count = lax.axis_size("dp")
    dp_rank = lax.axis_index("dp")
    micro_count = section_labels.shape[0]
    seq_len = section_labels.shape[1]
    local_experts = branch_widen_coefficients.shape[0]
    expert_count = local_experts * data_parallel_count
    top_count = branch_choice_labels.shape[1]
    expert_capacity = seq_len * top_count * 9 // (expert_count * 8)
    model_width = layer_entering_state.shape[1]
    adapter_width = PLUGIN_CHOICES * REDUCED_DIM
    query_width = H * HD
    key_value_width = KVH * HD
    repeat = H // KVH
    score_scale = HD ** (-0.5)
    pair_count = seq_len * top_count
    receive_buffer_rows = data_parallel_count * expert_capacity
    cos_table, sin_table = rotation(seq_len, HD)
    column_holder = jnp.arange(adapter_width, dtype=jnp.int32) // REDUCED_DIM
    expert_range = jnp.arange(expert_count, dtype=jnp.int32)

    def fetch_attention():
        return (
            lax.all_gather(attend_norm_scaling, "fsdp", axis=0, tiled=True),
            lax.all_gather(branch_norm_scaling, "fsdp", axis=0, tiled=True),
            lax.all_gather(triple_coefficients, "fsdp", axis=0, tiled=True),
            lax.all_gather(attend_exit_coefficients, "fsdp", axis=0, tiled=True),
            lax.all_gather(dispatch_coefficients, "fsdp", axis=0, tiled=True),
            lax.all_gather(triple_plugin_source, "fsdp", axis=0, tiled=True),
            lax.all_gather(asking_plugin_target, "fsdp", axis=1, tiled=True),
            lax.all_gather(lookup_plugin_target, "fsdp", axis=1, tiled=True),
            lax.all_gather(content_plugin_target, "fsdp", axis=1, tiled=True),
            lax.all_gather(merge_plugin_source, "fsdp", axis=0, tiled=True),
            lax.all_gather(merge_plugin_target, "fsdp", axis=1, tiled=True),
            lax.all_gather(dispatch_plugin_source, "fsdp", axis=0, tiled=True),
            lax.all_gather(dispatch_plugin_target, "fsdp", axis=0, tiled=True),
        )

    def fetch_experts():
        return (
            lax.all_gather(branch_widen_coefficients, "fsdp", axis=1, tiled=True),
            lax.all_gather(branch_contract_coefficients, "fsdp", axis=1, tiled=True),
            lax.all_gather(branch_plugin_source, "fsdp", axis=1, tiled=True),
            lax.all_gather(branch_plugin_target, "fsdp", axis=3, tiled=True),
            lax.all_gather(contract_plugin_source, "fsdp", axis=1, tiled=True),
            lax.all_gather(contract_plugin_target, "fsdp", axis=2, tiled=True),
        )

    outputs = []
    input_grads = []
    grad_sums = None
    for micro_step in range(micro_count):
        first_row = micro_step * seq_len
        hidden_rows = layer_entering_state[first_row : first_row + seq_len]
        grad_bf = exit_cotangent[first_row : first_row + seq_len]
        grad_rows = grad_bf.astype(jnp.float32)
        route_rows = branch_choice_labels[first_row : first_row + seq_len]
        block_rows = section_labels[micro_step]
        own_adapter = plugin_choice_per_text[dp_rank, micro_step]
        owned_adapter_mask = (column_holder == own_adapter).astype(jnp.float32)
        query_key_value_mask = jnp.tile(owned_adapter_mask, 3)
        sender_mask = (
            column_holder[None, :] == plugin_choice_per_text[:, micro_step][:, None]
        ).astype(jnp.float32)
        slot_legit_filter = jnp.broadcast_to(
            sender_mask[:, None, :], (data_parallel_count, expert_capacity, adapter_width)
        ).reshape(receive_buffer_rows, adapter_width)
        token_pair_mask = jnp.tile(slot_legit_filter, (1, 2))[None]
        attn_full = fetch_attention()
        expert_full = fetch_experts()
        (
            gain_attn,
            gain_moe,
            gathered_query_key_value,
            gathered_attention_output,
            gathered_router_weight,
            gathered_query_key_value_input,
            gathered_query_output,
            gathered_key_output,
            gathered_value_output,
            gathered_projection_input,
            gathered_projection_output,
            gathered_router_input,
            gathered_router_output,
        ) = attn_full
        (
            full_gateup,
            full_down,
            gathered_expert_input,
            gathered_expert_output,
            gathered_down_input,
            gathering_contracted_parts,
        ) = expert_full
        hidden_float = hidden_rows.astype(jnp.float32)
        attn_gain_f = gain_attn.astype(jnp.float32)
        moe_gain_f = gain_moe.astype(jnp.float32)
        normed_f, inverse_attn = norm_scale(hidden_float, attn_gain_f)
        normalized_input = normed_f.astype(jnp.bfloat16)
        query_key_value_adapter = (
            matrix_product(normalized_input, gathered_query_key_value_input) * query_key_value_mask
        ).astype(jnp.bfloat16)
        adapter_pieces = jnp.concatenate(
            [
                matrix_product(query_key_value_adapter[:, :adapter_width], gathered_query_output),
                matrix_product(
                    query_key_value_adapter[:, adapter_width : 2 * adapter_width],
                    gathered_key_output,
                ),
                matrix_product(
                    query_key_value_adapter[:, 2 * adapter_width :], gathered_value_output
                ),
            ],
            axis=1,
        )
        projected_rows = matrix_product(normalized_input, gathered_query_key_value) + adapter_pieces
        queries = rotate(
            projected_rows[:, :query_width].reshape(seq_len, H, HD), cos_table, sin_table
        ).astype(jnp.bfloat16)
        keys_rot = rotate(
            projected_rows[:, query_width : query_width + key_value_width].reshape(
                seq_len, KVH, HD
            ),
            cos_table,
            sin_table,
        ).astype(jnp.bfloat16)
        values_b = (
            projected_rows[:, query_width + key_value_width :]
            .reshape(seq_len, KVH, HD)
            .astype(jnp.bfloat16)
        )
        grouped = queries.reshape(seq_len, KVH, repeat, HD)
        allowed = block_rows[None, :] <= block_rows[:, None]

        def masked_scores():
            raw_scores = layered_times_effect("qnrd,knd->nrqk", grouped, keys_rot) * score_scale
            return jnp.where(allowed, raw_scores, -1e30)

        scores = masked_scores()
        row_peak = jnp.max(scores, axis=-1, keepdims=True)
        shifted_exp = jnp.exp(scores - row_peak)
        row_total = jnp.sum(shifted_exp, axis=-1, keepdims=True)
        attn_probs = shifted_exp / row_total
        log_total = row_peak + jnp.log(row_total)
        probs_b = attn_probs.astype(jnp.bfloat16)
        attention_output = (
            layered_times_effect("nrqk,knd->qnrd", probs_b, values_b)
            .reshape(seq_len, query_width)
            .astype(jnp.bfloat16)
        )
        projection_adapter_result = (
            matrix_product(attention_output, gathered_projection_input) * owned_adapter_mask
        ).astype(jnp.bfloat16)
        residual_stream = (
            hidden_float
            + matrix_product(attention_output, gathered_attention_output)
            + matrix_product(projection_adapter_result, gathered_projection_output)
        )
        moe_f, inverse_moe = norm_scale(residual_stream, moe_gain_f)
        mixture_input = moe_f.astype(jnp.bfloat16)
        router_adapter_result = (
            matrix_product(mixture_input, gathered_router_input) * owned_adapter_mask
        ).astype(jnp.bfloat16)
        router_logits = matrix_product(mixture_input, gathered_router_weight) + matrix_product(
            router_adapter_result, gathered_router_output
        )
        picked = route_rows[:, :, None] == expert_range[None, None, :]
        chosen = jnp.sum(jnp.where(picked, router_logits[:, None, :], 0.0), axis=2)
        gate_weights = jax.nn.softmax(chosen, axis=-1)
        flat_ids = route_rows.reshape(pair_count)
        hit_table = (flat_ids[:, None] == expert_range[None, :]).astype(jnp.int32)
        slot_index = jnp.sum((jnp.cumsum(hit_table, axis=0) - hit_table) * hit_table, axis=1)
        target = (
            flat_ids % local_experts * receive_buffer_rows
            + flat_ids // local_experts * expert_capacity
            + slot_index
        )
        source_pair = (
            jnp.full((expert_count * expert_capacity,), pair_count, jnp.int32)
            .at[target]
            .set(jnp.arange(pair_count, dtype=jnp.int32))
        )
        padded_in = jnp.concatenate(
            [mixture_input, jnp.zeros((1, model_width), jnp.bfloat16)], axis=0
        )
        send_rows = padded_in[source_pair // top_count].reshape(
            local_experts, receive_buffer_rows, model_width
        )
        received_rows = to_owners(send_rows)
        expert_adapter_result = (
            layered_times_effect("gom,gms->gos", received_rows, gathered_expert_input)
            * token_pair_mask
        ).astype(jnp.bfloat16)
        gate_up_product = layered_times_effect(
            "erd,edf->erf", received_rows, full_gateup
        ) + jnp.concatenate(
            [
                layered_times_effect(
                    "dwa,dat->dwt",
                    expert_adapter_result[..., :adapter_width],
                    gathered_expert_output[:, 0],
                ),
                layered_times_effect(
                    "dwa,dat->dwt",
                    expert_adapter_result[..., adapter_width:],
                    gathered_expert_output[:, 1],
                ),
            ],
            axis=-1,
        )
        gate_part = gate_up_product[..., :FEEDFORWARD_SIZE]
        up_part = gate_up_product[..., FEEDFORWARD_SIZE:]
        sigmoid_gate = jax.nn.sigmoid(gate_part)
        between_curved_array = (gate_part * sigmoid_gate * up_part).astype(jnp.bfloat16)
        contracted_thin_effect = (
            layered_times_effect("uri,uih->urh", between_curved_array, gathered_down_input)
            * slot_legit_filter[None]
        ).astype(jnp.bfloat16)
        branch_produced_parts = (
            layered_times_effect("bqn,bnw->bqw", between_curved_array, full_down)
            + layered_times_effect(
                "acn,anp->acp", contracted_thin_effect, gathering_contracted_parts
            )
        ).astype(jnp.bfloat16)
        back_rows = from_owners(branch_produced_parts)
        returned = (
            back_rows.reshape(expert_count * expert_capacity, model_width)[target]
            .reshape(seq_len, top_count, model_width)
            .astype(jnp.float32)
        )
        mixture = jnp.sum(gate_weights[:, :, None] * returned, axis=1)
        gate_grad = jnp.sum(grad_rows[:, None, :] * returned, axis=2)
        outputs.append((residual_stream + mixture).astype(jnp.bfloat16))
        attn_full = fetch_attention()
        expert_full = fetch_experts()
        (
            gain_attn,
            gain_moe,
            gathered_query_key_value,
            gathered_attention_output,
            gathered_router_weight,
            gathered_query_key_value_input,
            gathered_query_output,
            gathered_key_output,
            gathered_value_output,
            gathered_projection_input,
            gathered_projection_output,
            gathered_router_input,
            gathered_router_output,
        ) = attn_full
        (
            full_gateup,
            full_down,
            gathered_expert_input,
            gathered_expert_output,
            gathered_down_input,
            gathering_contracted_parts,
        ) = expert_full
        row_grad = (
            (gate_weights[:, :, None] * grad_rows[:, None, :])
            .astype(jnp.bfloat16)
            .reshape(pair_count, model_width)
        )
        padded_grad = jnp.concatenate([row_grad, jnp.zeros((1, model_width), jnp.bfloat16)], axis=0)
        send_grads = padded_grad[source_pair].reshape(
            local_experts, receive_buffer_rows, model_width
        )
        arrived_cotangents = to_owners(send_grads)
        down_adapter_gradient = (
            layered_times_effect("erd,ecd->erc", arrived_cotangents, gathering_contracted_parts)
            * slot_legit_filter[None]
        ).astype(jnp.bfloat16)
        inner_grad = layered_times_effect(
            "erd,efd->erf", arrived_cotangents, full_down
        ) + layered_times_effect("mlz,miz->mli", down_adapter_gradient, gathered_down_input)
        gate_grad_rows = (
            inner_grad * up_part * sigmoid_gate * (1.0 + gate_part * (1.0 - sigmoid_gate))
        )
        up_grad_rows = inner_grad * gate_part * sigmoid_gate
        gate_up_gradient = jnp.concatenate([gate_grad_rows, up_grad_rows], axis=-1).astype(
            jnp.bfloat16
        )
        expert_adapter_gradient = (
            jnp.concatenate(
                [
                    layered_times_effect(
                        "erf,ecf->erc",
                        gate_up_gradient[..., :FEEDFORWARD_SIZE],
                        gathered_expert_output[:, 0],
                    ),
                    layered_times_effect(
                        "erf,ecf->erc",
                        gate_up_gradient[..., FEEDFORWARD_SIZE:],
                        gathered_expert_output[:, 1],
                    ),
                ],
                axis=-1,
            )
            * token_pair_mask
        ).astype(jnp.bfloat16)
        rows_grad = (
            layered_times_effect("erf,edf->erd", gate_up_gradient, full_gateup)
            + layered_times_effect("xlt,xqt->xlq", expert_adapter_gradient, gathered_expert_input)
        ).astype(jnp.bfloat16)
        back_grads = from_owners(rows_grad)
        pair_grads = back_grads.reshape(expert_count * expert_capacity, model_width)[
            target
        ].reshape(seq_len, top_count, model_width)
        moe_grad = jnp.sum(pair_grads.astype(jnp.float32), axis=1)
        input_map_term = layered_times_effect(
            "igf,igo->ifo", received_rows, expert_adapter_gradient
        )
        expand_term = jnp.stack(
            [
                layered_times_effect(
                    "yzp,yzo->ypo",
                    expert_adapter_result[..., :adapter_width],
                    gate_up_gradient[..., :FEEDFORWARD_SIZE],
                ),
                layered_times_effect(
                    "yzp,yzo->ypo",
                    expert_adapter_result[..., adapter_width:],
                    gate_up_gradient[..., FEEDFORWARD_SIZE:],
                ),
            ],
            axis=1,
        )
        down_input_term = layered_times_effect(
            "xdj,xda->xja", between_curved_array, down_adapter_gradient
        )
        down_output_term = layered_times_effect(
            "syr,sya->sra", contracted_thin_effect, arrived_cotangents
        )
        select_grad = gate_weights * (
            gate_grad - jnp.sum(gate_weights * gate_grad, axis=-1, keepdims=True)
        )
        router_logit_gradient = jnp.sum(
            jnp.where(picked, select_grad[:, :, None], 0.0), axis=1
        ).astype(jnp.bfloat16)
        router_adapter_gradient = (
            matrix_product_transposed(router_logit_gradient, gathered_router_output)
            * owned_adapter_mask
        ).astype(jnp.bfloat16)
        moe_grad = (
            moe_grad
            + matrix_product_transposed(router_logit_gradient, gathered_router_weight)
            + matrix_product_transposed(router_adapter_gradient, gathered_router_input)
        )
        residual_grad = grad_rows + norm_back(residual_stream, inverse_moe, moe_gain_f, moe_grad)
        attention_gradient = residual_grad.astype(jnp.bfloat16)
        projection_adapter_gradient = (
            matrix_product_transposed(attention_gradient, gathered_projection_output)
            * owned_adapter_mask
        ).astype(jnp.bfloat16)
        attended_grad = (
            matrix_product_transposed(attention_gradient, gathered_attention_output)
            + matrix_product_transposed(projection_adapter_gradient, gathered_projection_input)
        ).astype(jnp.bfloat16)
        head_grad = attended_grad.reshape(seq_len, KVH, repeat, HD)
        attn_probs = jnp.exp(masked_scores() - log_total)
        probs_b = attn_probs.astype(jnp.bfloat16)
        prob_grad = layered_times_effect("qnrd,knd->nrqk", head_grad, values_b)
        score_grad = (
            attn_probs * (prob_grad - jnp.sum(attn_probs * prob_grad, axis=-1, keepdims=True))
        ).astype(jnp.bfloat16)
        query_grad = (
            layered_times_effect("nrqk,knd->qnrd", score_grad, keys_rot).reshape(seq_len, H, HD)
            * score_scale
        )
        key_grad = layered_times_effect("nrqk,qnrd->knd", score_grad, grouped) * score_scale
        value_grad = layered_times_effect("nrqk,qnrd->knd", probs_b, head_grad)
        projection_gradient = jnp.concatenate(
            [
                rotate_back(query_grad, cos_table, sin_table).reshape(seq_len, query_width),
                rotate_back(key_grad, cos_table, sin_table).reshape(seq_len, key_value_width),
                value_grad.reshape(seq_len, key_value_width),
            ],
            axis=1,
        ).astype(jnp.bfloat16)
        query_key_value_adapter_gradient = (
            jnp.concatenate(
                [
                    matrix_product_transposed(
                        projection_gradient[:, :query_width], gathered_query_output
                    ),
                    matrix_product_transposed(
                        projection_gradient[:, query_width : query_width + key_value_width],
                        gathered_key_output,
                    ),
                    matrix_product_transposed(
                        projection_gradient[:, query_width + key_value_width :],
                        gathered_value_output,
                    ),
                ],
                axis=1,
            )
            * query_key_value_mask
        ).astype(jnp.bfloat16)
        normalized_gradient = matrix_product_transposed(
            projection_gradient, gathered_query_key_value
        ) + matrix_product_transposed(
            query_key_value_adapter_gradient, gathered_query_key_value_input
        )
        input_grads.append(
            (
                residual_grad
                + norm_back(hidden_float, inverse_attn, attn_gain_f, normalized_gradient)
            ).astype(jnp.bfloat16)
        )
        grad_terms = (
            outer_product_sum(normalized_input, query_key_value_adapter_gradient),
            outer_product_sum(
                query_key_value_adapter[:, :adapter_width], projection_gradient[:, :query_width]
            ),
            outer_product_sum(
                query_key_value_adapter[:, adapter_width : 2 * adapter_width],
                projection_gradient[:, query_width : query_width + key_value_width],
            ),
            outer_product_sum(
                query_key_value_adapter[:, 2 * adapter_width :],
                projection_gradient[:, query_width + key_value_width :],
            ),
            outer_product_sum(attention_output, projection_adapter_gradient),
            outer_product_sum(projection_adapter_result, attention_gradient),
            outer_product_sum(mixture_input, router_adapter_gradient),
            outer_product_sum(router_adapter_result, router_logit_gradient),
            input_map_term,
            expand_term,
            down_input_term,
            down_output_term,
        )
        grad_sums = (
            grad_terms
            if grad_sums is None
            else tuple(
                (held_sum + fresh_term for held_sum, fresh_term in zip(grad_sums, grad_terms))
            )
        )
    reduced = (
        lax.psum_scatter(grad_sums[0], "fsdp", scatter_dimension=0, tiled=True),
        lax.psum_scatter(grad_sums[1], "fsdp", scatter_dimension=1, tiled=True),
        lax.psum_scatter(grad_sums[2], "fsdp", scatter_dimension=1, tiled=True),
        lax.psum_scatter(grad_sums[3], "fsdp", scatter_dimension=1, tiled=True),
        lax.psum_scatter(grad_sums[4], "fsdp", scatter_dimension=0, tiled=True),
        lax.psum_scatter(grad_sums[5], "fsdp", scatter_dimension=1, tiled=True),
        lax.psum_scatter(grad_sums[6], "fsdp", scatter_dimension=0, tiled=True),
        lax.psum_scatter(grad_sums[7], "fsdp", scatter_dimension=0, tiled=True),
        lax.psum_scatter(grad_sums[8], "fsdp", scatter_dimension=1, tiled=True),
        lax.psum_scatter(grad_sums[9], "fsdp", scatter_dimension=3, tiled=True),
        lax.psum_scatter(grad_sums[10], "fsdp", scatter_dimension=1, tiled=True),
        lax.psum_scatter(grad_sums[11], "fsdp", scatter_dimension=2, tiled=True),
    )
    summed = (
        lax.psum(reduced[0].astype(jnp.bfloat16), "dp").astype(jnp.float32),
        lax.psum(reduced[1].astype(jnp.bfloat16), "dp").astype(jnp.float32),
        lax.psum(reduced[2].astype(jnp.bfloat16), "dp").astype(jnp.float32),
        lax.psum(reduced[3].astype(jnp.bfloat16), "dp").astype(jnp.float32),
        lax.psum(reduced[4].astype(jnp.bfloat16), "dp").astype(jnp.float32),
        lax.psum(reduced[5].astype(jnp.bfloat16), "dp").astype(jnp.float32),
        lax.psum(reduced[6].astype(jnp.bfloat16), "dp").astype(jnp.float32),
        lax.psum(reduced[7].astype(jnp.bfloat16), "dp").astype(jnp.float32),
    )
    return (
        jnp.concatenate(outputs, axis=0),
        jnp.concatenate(input_grads, axis=0),
        summed[0],
        summed[1],
        summed[2],
        summed[3],
        summed[4],
        summed[5],
        summed[6],
        summed[7],
        reduced[8],
        reduced[9],
        reduced[10],
        reduced[11],
    )


def solution(mesh):
    placed = (
        P(("dp", "fsdp"), None),
        P(("dp", "fsdp"), None),
        P("fsdp"),
        P("fsdp"),
        P("fsdp", None),
        P("fsdp", None),
        P("fsdp", None),
        P("dp", "fsdp", None),
        P("dp", "fsdp", None),
        P("fsdp", None),
        P(None, "fsdp"),
        P(None, "fsdp"),
        P(None, "fsdp"),
        P("fsdp", None),
        P(None, "fsdp"),
        P("fsdp", None),
        P("fsdp", None),
        P("dp", "fsdp", None),
        P("dp", None, None, "fsdp"),
        P("dp", "fsdp", None),
        P("dp", None, "fsdp"),
        P(("dp", "fsdp"), None),
        P(None, "fsdp"),
        P(("dp", "fsdp"), None),
    )
    return jax.shard_map(
        local,
        mesh=mesh,
        in_specs=placed,
        out_specs=(
            P(("dp", "fsdp"), None),
            P(("dp", "fsdp"), None),
            P("fsdp", None),
            P(None, "fsdp"),
            P(None, "fsdp"),
            P(None, "fsdp"),
            P("fsdp", None),
            P(None, "fsdp"),
            P("fsdp", None),
            P("fsdp", None),
            P("dp", "fsdp", None),
            P("dp", None, None, "fsdp"),
            P("dp", "fsdp", None),
            P("dp", None, "fsdp"),
        ),
        check_vma=False,
    )
```

profile of v0, /device:TPU:0, one launch (start us, length us, event | category | flops | bytes accessed | tf_op | source)
XLA Modules:
  0.0 1782.7 jit_solution(6615289789643616006)
XLA Ops:
  278.5 19.9 %gather_fusion.6 = bf16[3456,1024]{1,0:T(8,128)(2,1)} fusion(bf16[3073,1024]{1,0:T(8,128)(2,1)} %concatenate.122, s32[4096]{0:T(1024)S(1)} %copy-done.172), kind=kCustom, calls=%fused_computation.6 | custom fusion | bytes 14169600 | tf_op jit(solution)/shard_map/gather | solution.py:373
  336.0 57.2 %all-to-all-done.6 = bf16[8,432,1024]{2,0,1:T(8,128)(2,1)} async-done(((bf16[8,432,1024]{2,0,1:T(8,128)(2,1)}), bf16[8,432,1024]{2,0,1:T(8,128)(2,1)}, u32[]{:S(2)}, u32[]{:S(2)}) %all-to-all-start.6) | async-done | bytes 7077920 | tf_op jit(solution)/shard_map/all_to_all | solution.py:78
  444.4 32.3 %all-to-all-done.2 = bf16[8,432,1024]{2,0,1:T(8,128)(2,1)} async-done(((bf16[8,432,1024]{2,0,1:T(8,128)(2,1)}), bf16[8,432,1024]{2,0,1:T(8,128)(2,1)}, u32[]{:S(2)}, u32[]{:S(2)}) %all-to-all-start.2) | async-done | bytes 7077920 | tf_op jit(solution)/shard_map/all_to_all | solution.py:78
  489.1 19.9 %gather_fusion.4 = bf16[3456,1024]{1,0:T(8,128)(2,1)} fusion(bf16[3073,1024]{1,0:T(8,128)(2,1)} %concatenate.115, s32[4096]{0:T(1024)S(1)} %get-tuple-element.186), kind=kCustom, calls=%fused_computation.4 | custom fusion | bytes 14169600 | tf_op jit(solution)/shard_map/gather | solution.py:373
  518.9 41.4 %all-to-all-done = bf16[8,432,1024]{2,0,1:T(8,128)(2,1)} async-done(((bf16[8,432,1024]{2,0,1:T(8,128)(2,1)}), bf16[8,432,1024]{2,0,1:T(8,128)(2,1)}, u32[]{:S(2)}, u32[]{:S(2)}) %all-to-all-start) | async-done | bytes 7077920 | tf_op jit(solution)/shard_map/all_to_all | solution.py:78
  617.2 26.3 %all-to-all-done.4 = bf16[8,432,1024]{2,0,1:T(8,128)(2,1)} async-done(((bf16[8,432,1024]{2,0,1:T(8,128)(2,1)}), bf16[8,432,1024]{2,0,1:T(8,128)(2,1)}, u32[]{:S(2)}, u32[]{:S(2)}) %all-to-all-start.4) | async-done | bytes 7077920 | tf_op jit(solution)/shard_map/all_to_all | solution.py:78
  655.5 26.7 %maximum_add_fusion.1 = f32[8,432,1024]{2,1,0:T(8,128)} fusion(f32[8,432,512]{2,1,0:T(8,128)} %fusion.136, f32[8,432,512]{2,1,0:T(8,128)} %fusion.144, bf16[8,1024,1024]{2,1,0:T(8,128)(2,1)} %all-gather.15.cloned.1.call-done, bf16[8,432,1024]{2,0,1:T(8,128)(2,1)} %all-to-all-done.2), kind=kOutput, calls=%fused_computation.15 | convolution fusion | flops 7254835200 | bytes 52166656 | tf_op jit(solution)/shard_map/erd,edf->erf/dot_general | solution.py:35
  682.2 22.0 %multiply_convert_fusion.1 = (bf16[8,432,512]{2,1,0:T(8,128)(2,1)}, bf16[8,432,512]{2,1,0:T(8,128)(2,1)}, bf16[8,432,512]{2,1,0:T(8,128)(2,1)S(1)}) fusion(f32[8,432,1024]{2,1,0:T(8,128)} %maximum_add_fusion.1, f32[8,432,512]{2,1,0:T(8,128)} %fusion.270, bf16[8,512,1024]{2,1,0:T(8,128)(2,1)} %all-gather.21.cloned.1.call-done, ...), kind=kOutput, calls=%fused_computation.61 | convolution fusion | flops 3653959680 | bytes 47316992 | tf_op jit(solution)/shard_map/erd,efd->erf/dot_general | solution.py:35
  738.7 26.3 %maximum_add_fusion = f32[8,432,1024]{2,1,0:T(8,128)} fusion(f32[8,432,512]{2,1,0:T(8,128)} %fusion.138, f32[8,432,512]{2,1,0:T(8,128)} %fusion.146, bf16[8,1024,1024]{2,1,0:T(8,128)(2,1)} %all-gather.15.cloned.1.call-done, bf16[8,432,1024]{2,0,1:T(8,128)(2,1)} %all-to-all-done), kind=kOutput, calls=%fused_computation.14 | convolution fusion | flops 7254835200 | bytes 52166656 | tf_op jit(solution)/shard_map/erd,edf->erf/dot_general | solution.py:35
  765.0 21.9 %multiply_convert_fusion.3 = (bf16[8,432,512]{2,1,0:T(8,128)(2,1)}, bf16[8,432,512]{2,1,0:T(8,128)(2,1)}, bf16[8,432,512]{2,1,0:T(8,128)(2,1)S(1)}) fusion(f32[8,432,1024]{2,1,0:T(8,128)} %maximum_add_fusion, f32[8,432,512]{2,1,0:T(8,128)} %fusion.264, bf16[8,512,1024]{2,1,0:T(8,128)(2,1)} %all-gather.21.cloned.1.call-done, ...), kind=kOutput, calls=%fused_computation.63 | convolution fusion | flops 3653959680 | bytes 47316992 | tf_op jit(solution)/shard_map/erd,efd->erf/dot_general | solution.py:35
  866.1 33.7 %all-to-all-done.1 = bf16[8,432,1024]{2,0,1:T(8,128)(2,1)} async-done(((bf16[8,432,1024]{2,0,1:T(8,128)(2,1)}), bf16[8,432,1024]{2,0,1:T(8,128)(2,1)}, u32[]{:S(2)}, u32[]{:S(2)}) %all-to-all-start.1) | async-done | bytes 7077920 | tf_op jit(solution)/shard_map/all_to_all | solution.py:82
  947.2 36.2 %all-to-all-done.7 = bf16[8,432,1024]{2,0,1:T(8,128)(2,1)} async-done(((bf16[8,432,1024]{2,0,1:T(8,128)(2,1)}), bf16[8,432,1024]{2,0,1:T(8,128)(2,1)}, u32[]{:S(2)}, u32[]{:S(2)}) %all-to-all-start.7) | async-done | bytes 7077920 | tf_op jit(solution)/shard_map/all_to_all | solution.py:82
  1000.2 20.0 %gather_fusion.3 = bf16[3072,1024]{1,0:T(8,128)(2,1)} fusion(bf16[3456,1024]{1,0:T(8,128)(2,1)} %bitcast.422, s32[3072]{0:T(1024)S(1)} %broadcast_clamp_fusion), kind=kCustom, calls=%fused_computation.3 | custom fusion | bytes 12595200 | tf_op jit(solution)/shard_map/gather | solution.py:335
  1038.1 19.9 %gather_fusion.1 = bf16[3072,1024]{1,0:T(8,128)(2,1)} fusion(bf16[3456,1024]{1,0:T(8,128)(2,1)} %bitcast.423, s32[3072]{0:T(1024)S(1)} %broadcast_clamp_fusion.1), kind=kCustom, calls=%fused_computation.1 | custom fusion | bytes 12595200 | tf_op jit(solution)/shard_map/gather | solution.py:335
  1076.5 19.9 %gather_fusion.7 = bf16[3072,1024]{1,0:T(8,128)(2,1)} fusion(bf16[3456,1024]{1,0:T(8,128)(2,1)} %bitcast.420, s32[3072]{0:T(1024)S(1)} %broadcast_clamp_fusion), kind=kCustom, calls=%fused_computation.7 | custom fusion | bytes 12595200 | tf_op jit(solution)/shard_map/gather | solution.py:414
  1116.3 20.4 %gather_fusion.5 = bf16[3072,1024]{1,0:T(8,128)(2,1)} fusion(bf16[3456,1024]{1,0:T(8,128)(2,1)} %bitcast.421, s32[3072]{0:T(1024)} %copy-done.159), kind=kCustom, calls=%fused_computation.5 | custom fusion | bytes 12595200 | tf_op jit(solution)/shard_map/gather | solution.py:414
  1290.5 30.0 %reduce-scatter.25.cloned.1.call-done = f32[128,128]{1,0:T(8,128)} async-done(((f32[1024,128]{1,0:T(8,128)}), f32[128,128]{1,0:T(8,128)}) %reduce-scatter.25.cloned.1.call-update) | async-done | bytes 65552 | tf_op jit(solution)/shard_map/reduce_scatter | solution.py:554
  1321.9 30.5 %reduce-scatter.23.cloned.1.call-done = f32[128,128]{1,0:T(8,128)} async-done(((f32[128,1024]{1,0:T(8,128)}), f32[128,128]{1,0:T(8,128)}) %reduce-scatter.23.cloned.1.call-update) | async-done | bytes 65552 | tf_op jit(solution)/shard_map/reduce_scatter | solution.py:553
  1353.9 30.5 %reduce-scatter.21.cloned.1.call-done = f32[128,128]{1,0:T(8,128)} async-done(((f32[1024,128]{1,0:T(8,128)}), f32[128,128]{1,0:T(8,128)}) %reduce-scatter.21.cloned.1.call-update) | async-done | bytes 65552 | tf_op jit(solution)/shard_map/reduce_scatter | solution.py:552
  1385.8 30.4 %reduce-scatter.15.cloned.1.call-done = f32[128,128]{1,0:T(8,128)} async-done(((f32[128,1024]{1,0:T(8,128)}), f32[128,128]{1,0:T(8,128)}) %reduce-scatter.15.cloned.1.call-update) | async-done | bytes 65552 | tf_op jit(solution)/shard_map/reduce_scatter | solution.py:549
  1553.5 40.9 %all-reduce.8.cloned.1.call-done = bf16[128,384]{1,0:T(8,128)(2,1)} async-done(((bf16[128,384]{1,0:T(8,128)(2,1)}), bf16[128,384]{1,0:T(8,128)(2,1)}) %all-reduce.8.cloned.1.call-update) | async-done | bytes 98320 | tf_op jit(solution)/shard_map/psum | solution.py:562
  1596.0 37.1 %reduce-scatter.33.cloned.1.call-done = f32[8,64,128]{2,1,0:T(8,128)} async-done(((f32[8,512,128]{2,1,0:T(8,128)}), f32[8,64,128]{2,1,0:T(8,128)}) %reduce-scatter.33.cloned.1.call-update) | async-done | bytes 262160 | tf_op jit(solution)/shard_map/reduce_scatter | solution.py:558
  1633.1 51.7 %reduce-scatter.35.cloned.1.call-done = f32[8,128,128]{2,1,0:T(8,128)} async-done(((f32[8,128,1024]{2,1,0:T(8,128)}), f32[8,128,128]{2,1,0:T(8,128)}) %reduce-scatter.35.cloned.1.call-update) | async-done | bytes 524304 | tf_op jit(solution)/shard_map/reduce_scatter | solution.py:559
  1684.8 90.8 %reduce-scatter.29.cloned.1.call-done = f32[8,128,256]{2,1,0:T(8,128)} async-done(((f32[8,1024,256]{2,1,0:T(8,128)}), f32[8,128,256]{2,1,0:T(8,128)}) %reduce-scatter.29.cloned.1.call-update) | async-done | bytes 1048592 | tf_op jit(solution)/shard_map/reduce_scatter | solution.py:556
  (811 shorter events, 979.4 us)
Async XLA Ops:
  7.2 202.1 %all-gather.11.cloned.1.call-start = ((), (), s32[]{:S(2)}) async-start(), calls=%async_computation.20 | async-start | bytes 4718592 | tf_op jit(solution)/shard_map/all_gather | solution.py:135
  7.9 245.8 %all-gather.13.cloned.1.call-start = ((), (), s32[]{:S(2)}) async-start(), calls=%async_computation.21 | async-start | bytes 2359296 | tf_op jit(solution)/shard_map/all_gather | solution.py:136
  8.7 559.1 %all-gather.19.cloned.1.call-start = ((), (), s32[]{:S(2)}) async-start(), calls=%async_computation.24 | async-start | bytes 2359296 | tf_op jit(solution)/shard_map/all_gather | solution.py:153
  10.6 560.5 %all-gather.17.cloned.1.call-start = ((), (), s32[]{:S(2)}) async-start(), calls=%async_computation.23 | async-start | bytes 4718592 | tf_op jit(solution)/shard_map/all_gather | solution.py:152
  11.2 592.0 %all-gather.25.cloned.1.call-start = ((), (), s32[]{:S(2)}) async-start(), calls=%async_computation.27 | async-start | bytes 2359296 | tf_op jit(solution)/shard_map/all_gather | solution.py:155
  11.8 599.2 %all-gather.23.cloned.1.call-start = ((), (), s32[]{:S(2)}) async-start(), calls=%async_computation.26 | async-start | bytes 1179648 | tf_op jit(solution)/shard_map/all_gather | solution.py:154
  12.4 643.0 %all-gather.15.cloned.1.call-start = ((), (), s32[]{:S(2)}) async-start(), calls=%async_computation.22 | async-start | bytes 18874368 | tf_op jit(solution)/shard_map/all_gather | solution.py:150
  308.4 84.8 %all-to-all-start.6 = ((bf16[8,432,1024]{2,0,1:T(8,128)(2,1)}), bf16[8,432,1024]{2,0,1:T(8,128)(2,1)}, u32[]{:S(2)}, u32[]{:S(2)}) async-start(bf16[8,432,1024]{2,0,1:T(8,128)(2,1)} %copy.300), calls=%async_computation.6 | async-start | bytes 14155776 | tf_op jit(solution)/shard_map/all_to_all | solution.py:78
  398.5 283.7 %all-gather.21.cloned.1.call-start = ((), (), s32[]{:S(2)}) async-start(), calls=%async_computation.25 | async-start | bytes 9437184 | tf_op jit(solution)/shard_map/all_gather | solution.py:151
  476.7 83.6 %all-to-all-start = ((bf16[8,432,1024]{2,0,1:T(8,128)(2,1)}), bf16[8,432,1024]{2,0,1:T(8,128)(2,1)}, u32[]{:S(2)}, u32[]{:S(2)}) async-start(bf16[8,432,1024]{2,0,1:T(8,128)(2,1)} %copy.261), calls=%async_computation | async-start | bytes 14155776 | tf_op jit(solution)/shard_map/all_to_all | solution.py:78
  983.4 123.0 %all-to-all-start.5 = ((bf16[8,432,1024]{2,0,1:T(8,128)(2,1)}), bf16[8,432,1024]{2,0,1:T(8,128)(2,1)}, u32[]{:S(2)}, u32[]{:S(2)}) async-start(bf16[8,432,1024]{2,0,1:T(8,128)(2,1)} %copy.288), calls=%async_computation.5 | async-start | bytes 14155776 | tf_op jit(solution)/shard_map/all_to_all | solution.py:82
  988.8 292.6 %reduce-scatter.27.cloned.1.call-start = ((), (), s32[]{:S(2)}) async-start(), calls=%async_computation.36 | async-start | bytes 73728 | tf_op jit(solution)/shard_map/reduce_scatter | solution.py:555
  1191.3 91.3 %reduce-scatter.19.cloned.1.call-start = ((), (), s32[]{:S(2)}) async-start(), calls=%async_computation.32 | async-start | bytes 294912 | tf_op jit(solution)/shard_map/reduce_scatter | solution.py:551
  1232.0 88.5 %reduce-scatter.25.cloned.1.call-start = ((), (), s32[]{:S(2)}) async-start(), calls=%async_computation.35 | async-start | bytes 589824 | tf_op jit(solution)/shard_map/reduce_scatter | solution.py:554
  1234.8 117.6 %reduce-scatter.23.cloned.1.call-start = ((), (), s32[]{:S(2)}) async-start(), calls=%async_computation.34 | async-start | bytes 589824 | tf_op jit(solution)/shard_map/reduce_scatter | solution.py:553
  1242.2 142.2 %reduce-scatter.21.cloned.1.call-start = ((), (), s32[]{:S(2)}) async-start(), calls=%async_computation.33 | async-start | bytes 589824 | tf_op jit(solution)/shard_map/reduce_scatter | solution.py:552
  1253.3 162.9 %reduce-scatter.15.cloned.1.call-start = ((), (), s32[]{:S(2)}) async-start(), calls=%async_computation.30 | async-start | bytes 589824 | tf_op jit(solution)/shard_map/reduce_scatter | solution.py:549
  1260.4 191.1 %reduce-scatter.13.cloned.1.call-start = ((), (), s32[]{:S(2)}) async-start(), calls=%async_computation.28 | async-start | bytes 1769472 | tf_op jit(solution)/shard_map/reduce_scatter | solution.py:548
  1268.6 265.1 %all-reduce.10.cloned.1.call-start = ((), (), s32[]{:S(2)}) async-start(), calls=%async_computation.41 | async-start | bytes 335872 | tf_op jit(solution)/shard_map/psum | solution.py:563
  1417.7 133.8 %reduce-scatter.31.cloned.1.call-start = ((), (), s32[]{:S(2)}) async-start(), calls=%async_computation.38 | async-start | bytes 4718592 | tf_op jit(solution)/shard_map/reduce_scatter | solution.py:557
  1429.8 164.6 %all-reduce.8.cloned.1.call-start = ((), (), s32[]{:S(2)}) async-start(), calls=%async_computation.29 | async-start | bytes 196608 | tf_op jit(solution)/shard_map/psum | solution.py:562
  1453.1 180.0 %reduce-scatter.33.cloned.1.call-start = ((), (), s32[]{:S(2)}) async-start(), calls=%async_computation.39 | async-start | bytes 2359296 | tf_op jit(solution)/shard_map/reduce_scatter | solution.py:558
  1458.8 225.9 %reduce-scatter.35.cloned.1.call-start = ((), (), s32[]{:S(2)}) async-start(), calls=%async_computation.40 | async-start | bytes 4718592 | tf_op jit(solution)/shard_map/reduce_scatter | solution.py:559
  1484.5 291.0 %reduce-scatter.29.cloned.1.call-start = ((), (), s32[]{:S(2)}) async-start(), calls=%async_computation.37 | async-start | bytes 9437184 | tf_op jit(solution)/shard_map/reduce_scatter | solution.py:556
  (238 other events, 5383.6 us)
Sparse Core Ops, SparseCore 0:
  9.6 49.9 all-gather.10
  61.2 28.4 all-gather.12
  91.9 29.5 all-gather.18
  123.0 52.6 all-gather.16
  177.2 34.6 all-gather.24
  213.4 20.2 all-gather.22
  235.3 150.7 all-gather.14
  400.9 82.1 all-gather.20
  1191.4 30.4 reduce-scatter.26
  1226.9 30.7 reduce-scatter.18
  1260.5 28.5 reduce-scatter.16
  1291.3 29.0 reduce-scatter.24
  1323.3 29.0 reduce-scatter.22
  1355.2 29.0 reduce-scatter.20
  1387.0 29.1 reduce-scatter.14
  1419.0 32.4 reduce-scatter.12
  1456.7 41.4 all-reduce.9
  1500.3 51.0 reduce-scatter.30
  1554.4 39.9 all-reduce.7
  1597.2 35.7 reduce-scatter.32
  1636.0 48.6 reduce-scatter.34
  1687.7 87.7 reduce-scatter.28
where the time goes:
time: 1790 us; the launch traced here: 1780 us
  waiting for transfers between devices  604 us (34%)
  matrix products  465 us (26%)
  local copies, waits for them, and re-layouts  357 us (20%)
  blocking collectives  155 us (9%)
  other arithmetic  138 us (8%)
  starting transfers between devices  46.7 us (3%)
    dot_general x50, matrix products, layered_times_effect(): jnp.einsum(pattern, operand, factor, preferred_element_type=jnp.float32)  389 us
    all_to_all x4, waiting for transfers between devices, to_owners(): lax.all_to_all(rows_block, 'dp', split_axis=1, concat_axis=1, tiled=True)  157 us
    reduce_scatter x1, waiting for transfers between devices, local(): lax.psum_scatter(grad_sums[8], 'fsdp', scatter_dimension=1, tiled=True)  90.8 us
    all_to_all x4, waiting for transfers between devices, from_owners(): lax.all_to_all(rows_block, 'dp', split_axis=1, concat_axis=1, tiled=True)  70.3 us
    reduce_scatter x1, waiting for transfers between devices, local(): lax.psum_scatter(grad_sums[11], 'fsdp', scatter_dimension=2, tiled=True)  51.7 us
    psum x1, waiting for transfers between devices, local(): lax.psum(reduced[0].astype(jnp.bfloat16), 'dp').astype(jnp.float32)  40.9 us
    gather x2, local copies, waits for them, and re-layouts, local(): back_grads.reshape(expert_count * expert_capacity, model_width)[target]  40.3 us
    gather x2, local copies, waits for them, and re-layouts, local(): back_rows.reshape(expert_count * expert_capacity, model_width)[target]  40 us
  transfers between devices with their start and end apart: 30, of which 18 were waited for; matrix products, arithmetic and copies ran while one was open for 45% of the time, Pallas kernels for 0%

commit v1 on v0

v1 whole, which is shorter than its diff:
```python
import functools

import jax
import jax.numpy as jnp
from jax import lax
from jax.experimental import pallas as pl
from jax.experimental.pallas import tpu as pltpu
from jax.sharding import PartitionSpec as P

H = 16
KVH = 8
HD = 64
FEEDFORWARD_SIZE = 512
PLUGIN_CHOICES = 8
REDUCED_DIM = 16

eps_norm = 1e-06
rope_base = 10000.0

LANES = 128
SHARDS = 8
CHUNKS = (2, 2, 2, 2)
VMEM = 60 * 1024 * 1024

f32 = jnp.float32
bf16 = jnp.bfloat16


def nn(a, b):
    return lax.dot_general(a, b, (((1,), (0,)), ((), ())), preferred_element_type=f32)


def nt(a, b):
    return lax.dot_general(a, b, (((1,), (1,)), ((), ())), preferred_element_type=f32)


def tn(a, b):
    return lax.dot_general(a, b, (((0,), (0,)), ((), ())), preferred_element_type=f32)


matrix_product = nn
matrix_product_transposed = nt
outer_product_sum = tn


def layered_times_effect(pattern, operand, factor):
    return jnp.einsum(pattern, operand, factor, preferred_element_type=f32)


def norm_scale(values, gain_vec):
    inverse = lax.rsqrt(jnp.mean(values * values, axis=-1, keepdims=True) + eps_norm)
    return (values * inverse * gain_vec, inverse)


def norm_back(values, inverse, gain_vec, upstream):
    scaled = gain_vec * upstream
    feature_count = values.shape[-1]
    weighted_sum = jnp.sum(values * scaled, axis=-1, keepdims=True)
    return inverse * scaled - values * (inverse * inverse * inverse) * weighted_sum / feature_count


def rotation(length, head_size):
    half_size = head_size // 2
    frequency = rope_base ** (-(2.0 * jnp.arange(half_size, dtype=f32)) / head_size)
    angles = jnp.arange(length, dtype=f32)[:, None] * frequency[None, :]
    return (jnp.cos(angles)[:, None, :], jnp.sin(angles)[:, None, :])


def rotate(values, cos_table, sin_table):
    half_size = values.shape[-1] // 2
    leading = values[..., :half_size]
    trailing = values[..., half_size:]
    return jnp.concatenate(
        [leading * cos_table - trailing * sin_table, trailing * cos_table + leading * sin_table],
        axis=-1,
    )


def rotate_back(values, cos_table, sin_table):
    half_size = values.shape[-1] // 2
    leading = values[..., :half_size]
    trailing = values[..., half_size:]
    return jnp.concatenate(
        [leading * cos_table + trailing * sin_table, trailing * cos_table - leading * sin_table],
        axis=-1,
    )


def columns_to_rows(a):
    r, c = a.shape[-2:]
    b = c // LANES
    a = a.reshape(a.shape[:-1] + (b, LANES))
    return jnp.swapaxes(a, -3, -2).reshape(a.shape[:-3] + (b * r, LANES))


def rows_to_columns(a, blocks):
    n, br, _ = a.shape
    r = br // blocks
    return a.reshape(n, blocks, r, LANES).transpose(0, 2, 1, 3).reshape(n * r, blocks * LANES)


def pad_lanes(a):
    return jnp.pad(a, ((0, 0), (0, LANES - a.shape[-1])))


def expert_segments(width, inner):
    ru, rd = width // SHARDS, inner // SHARDS
    return (ru * width // LANES, rd * width // LANES, 2 * ru, 2 * rd, rd, ru)


def pack_experts(widen, contract, up_source, up_target, down_source, down_target):
    count = widen.shape[0]
    return jnp.concatenate(
        [
            columns_to_rows(widen),
            columns_to_rows(contract),
            columns_to_rows(up_source),
            jnp.swapaxes(up_target, 2, 3).reshape(count, -1, LANES),
            down_source,
            jnp.swapaxes(down_target, 1, 2),
        ],
        axis=1,
    )


def regroup(gathered, width, inner):
    n, count = gathered.shape[:2]
    if n == SHARDS:
        return gathered
    per = n // SHARDS
    pieces, at = [], 0
    ru, rd = width // n, inner // n
    blocks = ((width // LANES, ru), (width // LANES, rd), (2, ru), (2, rd), (1, rd), (1, ru))
    for b, r in blocks:
        piece = gathered[:, :, at : at + b * r].reshape(SHARDS, per, count, b, r, LANES)
        at += b * r
        pieces.append(piece.transpose(0, 2, 3, 1, 4, 5).reshape(SHARDS, count, b * per * r, LANES))
    return jnp.concatenate(pieces, axis=2)


def hits_of(rank_row, capacity):
    rows = lax.broadcasted_iota(jnp.int32, (capacity, rank_row.shape[1]), 0)
    return rows == rank_row


def dispatch_kernel(capacity, x_ref, c_ref, rank_ref, gate_ref, xs_ref, cs_ref, gs_ref):
    count = rank_ref.shape[1]
    hot = []
    for e in range(count):
        hits = hits_of(rank_ref[0, e : e + 1, :], capacity)
        hot.append(jnp.where(hits, 1.0, 0.0).astype(bf16))
        gate = jnp.sum(jnp.where(hits, gate_ref[0, e : e + 1, :], 0.0), axis=1, keepdims=True)
        gs_ref[0, e] = jnp.broadcast_to(gate, (capacity, LANES))
    hot = jnp.concatenate(hot, axis=0)
    shape = xs_ref.shape[1:]
    xs_ref[0] = nn(hot, x_ref[...]).astype(bf16).reshape(shape)
    cs_ref[0] = nn(hot, c_ref[...]).astype(bf16).reshape(shape)


def dispatch(rows, cotangent, rank, gate, capacity):
    micro, count, length = rank.shape
    width = rows.shape[1]
    row_spec = pl.BlockSpec((length, width), lambda m: (m, 0))
    table = pl.BlockSpec((1, count, length), lambda m: (m, 0, 0))
    out_spec = pl.BlockSpec((1, count, capacity, width), lambda m: (m, 0, 0, 0))
    slots = micro * count * capacity
    return pl.pallas_call(
        functools.partial(dispatch_kernel, capacity),
        grid=(micro,),
        in_specs=[row_spec, row_spec, table, table],
        out_specs=[
            out_spec,
            out_spec,
            pl.BlockSpec((1, count, capacity, LANES), lambda m: (m, 0, 0, 0)),
        ],
        out_shape=[
            jax.ShapeDtypeStruct((micro, count, capacity, width), bf16),
            jax.ShapeDtypeStruct((micro, count, capacity, width), bf16),
            jax.ShapeDtypeStruct((micro, count, capacity, LANES), f32),
        ],
        compiler_params=pltpu.CompilerParams(vmem_limit_bytes=VMEM),
        cost_estimate=pl.CostEstimate(
            flops=4 * slots * length * width, bytes_accessed=8 * slots * width, transcendentals=0
        ),
        name="dispatch",
    )(rows, cotangent, rank, gate)


def expert_kernel(groups, *refs):
    n = groups
    x_refs, c_refs, g_refs = refs[:n], refs[n : 2 * n], refs[2 * n : 3 * n]
    w_ref, mask_ref = refs[3 * n : 3 * n + 2]
    outs = refs[3 * n + 2 :]
    y_refs, m_refs, gg_refs = outs[:n], outs[n : 2 * n], outs[2 * n : 3 * n]
    grad_ref = outs[3 * n]
    wide, deep, source, sums_a, sums_b, sums_c, sums_d, sums_e = outs[3 * n + 1 :]
    micro, _, capacity, width = x_refs[0].shape
    inner_width = deep.shape[0]
    ru, rd = width // SHARDS, inner_width // SHARDS
    blocks = width // LANES
    at = 0

    def part(rows):
        nonlocal at
        value = w_ref[:, 0, at : at + rows, :].reshape(SHARDS * rows, LANES)
        at += rows
        return value

    for j in range(blocks):
        wide[:, j * LANES : (j + 1) * LANES] = part(ru)
    for j in range(blocks):
        deep[:, j * LANES : (j + 1) * LANES] = part(rd)
    for j in range(2):
        source[:, j * LANES : (j + 1) * LANES] = part(ru)
    target_gate, target_up = part(rd), part(rd)
    down_source = part(rd)
    down_target = part(ru)

    step = 2
    for first in range(0, n, step):
        ks = range(first, first + step)

        def rows_of(rs):
            return jnp.concatenate(
                [rs[k][:, 0].reshape(micro * capacity, rs[k].shape[3]) for k in ks], axis=0
            )

        x = rows_of(x_refs)
        cot = rows_of(c_refs)
        gate_of_slot = rows_of(g_refs)[:, :1]
        mask = jnp.concatenate(
            [
                jnp.broadcast_to(mask_ref[k, m : m + 1, :], (capacity, LANES))
                for k in ks
                for m in range(micro)
            ],
            axis=0,
        )
        mask2 = jnp.concatenate([mask, mask], axis=1)
        lora = (nn(x, source[...]) * mask2).astype(bf16)
        gate_up = nn(x, wide[...])
        gate = gate_up[:, :inner_width] + nt(lora[:, :LANES], target_gate)
        up = gate_up[:, inner_width:] + nt(lora[:, LANES:], target_up)
        sig = jax.nn.sigmoid(gate)
        silu = gate * sig
        inner = (silu * up).astype(bf16)
        down_lora = (nn(inner, down_source) * mask).astype(bf16)
        rows = (nn(inner, deep[...]) + nt(down_lora, down_target)).astype(bf16)
        rows_f = rows.astype(f32)
        cot_f = cot.astype(f32)
        product = jnp.sum(rows_f * cot_f, axis=1, keepdims=True)
        weighted = (rows_f * gate_of_slot).astype(bf16)
        row_grad = (cot_f * gate_of_slot).astype(bf16)
        down_lora_grad = (nn(row_grad, down_target) * mask).astype(bf16)
        inner_grad = nt(row_grad, deep[...]) + nt(down_lora_grad, down_source)
        gate_grad = (inner_grad * up * (sig * (1.0 + gate * (1.0 - sig)))).astype(bf16)
        up_grad = (inner_grad * silu).astype(bf16)
        lora_grad = (
            jnp.concatenate([nn(gate_grad, target_gate), nn(up_grad, target_up)], axis=1) * mask2
        ).astype(bf16)
        back = (
            nt(gate_grad, wide[:, :inner_width])
            + nt(up_grad, wide[:, inner_width:])
            + nt(lora_grad, source[...])
        ).astype(bf16)
        for i, k in enumerate(ks):
            size = micro * capacity
            here = slice(i * size, (i + 1) * size)
            y_refs[k][:, 0] = weighted[here].reshape(micro, capacity, width)
            m_refs[k][:, 0] = back[here].reshape(micro, capacity, width)
            gg_refs[k][:, 0] = jnp.broadcast_to(product[here], (size, LANES)).reshape(
                micro, capacity, LANES
            )
        terms = (
            tn(lora_grad, x),
            tn(lora[:, :LANES], gate_grad),
            tn(lora[:, LANES:], up_grad),
            tn(down_lora_grad, inner),
            tn(down_lora, row_grad),
        )
        held = (sums_a, sums_b, sums_c, sums_d, sums_e)
        for ref, term in zip(held, terms):
            ref[...] = term if first == 0 else ref[...] + term
    out = 0
    for s in range(SHARDS):
        grad_ref[s, 0, : 2 * LANES] = sums_a[:, s * ru : (s + 1) * ru].astype(bf16)
    out = 2 * LANES
    for ref in (sums_b, sums_c, sums_d):
        turned = ref[...].T.astype(bf16).reshape(SHARDS, rd, LANES)
        grad_ref[:, 0, out : out + rd] = turned
        out += rd
    for s in range(SHARDS):
        grad_ref[s, 0, out : out + LANES] = sums_e[:, s * ru : (s + 1) * ru].astype(bf16)


def expert_chunk(xs, cs, gs, weights, masks, first, inner_width):
    n = len(xs)
    micro, _, capacity, width = xs[0].shape
    count = weights.shape[1]
    rows = weights.shape[2]
    rd = inner_width // SHARDS
    grad_rows = 2 * LANES + 3 * rd + LANES

    def slot_spec(lanes, at):
        return pl.BlockSpec((micro, 1, capacity, lanes), lambda e: (0, at + e, 0, 0))

    slots = n * micro * capacity
    return pl.pallas_call(
        functools.partial(expert_kernel, n),
        grid=(count,),
        in_specs=[slot_spec(width, first)] * (2 * n)
        + [slot_spec(LANES, first)] * n
        + [
            pl.BlockSpec((SHARDS, 1, rows, LANES), lambda e: (0, e, 0, 0)),
            pl.BlockSpec(masks.shape, lambda e: (0, 0, 0)),
        ],
        out_specs=[slot_spec(width, 0)] * (2 * n)
        + [slot_spec(LANES, 0)] * n
        + [pl.BlockSpec((SHARDS, 1, grad_rows, LANES), lambda e: (0, e, 0, 0))],
        out_shape=[jax.ShapeDtypeStruct((micro, count, capacity, width), bf16)] * (2 * n)
        + [jax.ShapeDtypeStruct((micro, count, capacity, LANES), f32)] * n
        + [jax.ShapeDtypeStruct((SHARDS, count, grad_rows, LANES), bf16)],
        scratch_shapes=[
            pltpu.VMEM((width, 2 * inner_width), bf16),
            pltpu.VMEM((inner_width, width), bf16),
            pltpu.VMEM((width, 2 * LANES), bf16),
            pltpu.VMEM((2 * LANES, width), f32),
            pltpu.VMEM((LANES, inner_width), f32),
            pltpu.VMEM((LANES, inner_width), f32),
            pltpu.VMEM((LANES, inner_width), f32),
            pltpu.VMEM((LANES, width), f32),
        ],
        compiler_params=pltpu.CompilerParams(vmem_limit_bytes=VMEM),
        cost_estimate=pl.CostEstimate(
            flops=10 * 1000 * 1000 * slots * count,
            bytes_accessed=count * (8 * slots * width + 6 * rows * LANES * SHARDS),
            transcendentals=slots * count * inner_width,
        ),
        name="experts",
    )(*xs, *cs, *gs, weights, masks)


def combine_kernel(chunks, with_product, *refs):
    n = chunks
    row_refs = refs[:n]
    gg_refs = refs[n : 2 * n] if with_product else ()
    rank_ref = refs[2 * n if with_product else n]
    outs = refs[(2 * n if with_product else n) + 1 :]
    capacity, width = row_refs[0].shape[2:]
    total = None
    e = 0
    for c in range(n):
        hot = []
        here = row_refs[c].shape[1]
        for i in range(here):
            hits = hits_of(rank_ref[0, e : e + 1, :], capacity)
            hot.append(jnp.where(hits, 1.0, 0.0).astype(bf16))
            if with_product:
                outs[1][0, e : e + 1, :] = jnp.sum(
                    jnp.where(hits, gg_refs[c][0, i, :, :1], 0.0), axis=0, keepdims=True
                )
            e += 1
        term = tn(jnp.concatenate(hot, axis=0), row_refs[c][0].reshape(here * capacity, width))
        total = term if total is None else total + term
    outs[0][...] = total.astype(bf16)


def combine(rows, products, rank):
    micro, count, length = rank.shape
    capacity, width = rows[0].shape[2:]
    with_product = products is not None

    def chunk_spec(a):
        return pl.BlockSpec((1,) + a.shape[1:], lambda m: (m, 0, 0, 0))

    table = pl.BlockSpec((1, count, length), lambda m: (m, 0, 0))
    out_specs = [pl.BlockSpec((length, width), lambda m: (m, 0))]
    out_shape = [jax.ShapeDtypeStruct((micro * length, width), bf16)]
    operands = list(rows)
    if with_product:
        operands += list(products)
        out_specs.append(table)
        out_shape.append(jax.ShapeDtypeStruct((micro, count, length), f32))
    slots = micro * count * capacity
    return pl.pallas_call(
        functools.partial(combine_kernel, len(rows), with_product),
        grid=(micro,),
        in_specs=[chunk_spec(a) for a in operands] + [table],
        out_specs=out_specs,
        out_shape=out_shape,
        compiler_params=pltpu.CompilerParams(vmem_limit_bytes=VMEM),
        cost_estimate=pl.CostEstimate(
            flops=2 * slots * length * width, bytes_accessed=3 * slots * width, transcendentals=0
        ),
        name="combine",
    )(*operands, rank)


def exchange(a, k):
    if k == 0:
        return a
    size = lax.axis_size("dp")
    return lax.ppermute(a, "dp", [(i, i ^ k) for i in range(size)])


def local(
    layer_entering_state,
    exit_cotangent,
    attend_norm_scaling,
    branch_norm_scaling,
    triple_coefficients,
    attend_exit_coefficients,
    dispatch_coefficients,
    branch_widen_coefficients,
    branch_contract_coefficients,
    triple_plugin_source,
    asking_plugin_target,
    lookup_plugin_target,
    content_plugin_target,
    merge_plugin_source,
    merge_plugin_target,
    dispatch_plugin_source,
    dispatch_plugin_target,
    branch_plugin_source,
    branch_plugin_target,
    contract_plugin_source,
    contract_plugin_target,
    branch_choice_labels,
    plugin_choice_per_text,
    section_labels,
):
    dp_count = lax.axis_size("dp")
    shard_count = lax.axis_size("fsdp")
    dp_rank = lax.axis_index("dp")
    micro_count, seq_len = section_labels.shape
    local_experts = branch_widen_coefficients.shape[0]
    expert_count = local_experts * dp_count
    top_count = branch_choice_labels.shape[1]
    most = seq_len * top_count * 9 // (expert_count * 8)
    capacity = -(-most // 16) * 16
    model_width = layer_entering_state.shape[1]
    inner_width = contract_plugin_source.shape[1] * shard_count
    adapter_width = PLUGIN_CHOICES * REDUCED_DIM
    query_width = H * HD
    key_value_width = KVH * HD
    repeat = H // KVH
    score_scale = HD ** (-0.5)
    cos_table, sin_table = rotation(seq_len, HD)
    column_holder = jnp.arange(adapter_width, dtype=jnp.int32) // REDUCED_DIM
    peers = range(dp_count)

    ru = model_width // shard_count
    packed_parts = [
        (columns_to_rows(triple_coefficients), query_width // LANES + 2 * key_value_width // LANES),
        (columns_to_rows(attend_exit_coefficients), model_width // LANES),
        (columns_to_rows(triple_plugin_source), 3),
        (asking_plugin_target.T, 1),
        (lookup_plugin_target.T, 1),
        (content_plugin_target.T, 1),
        (merge_plugin_source, 1),
        (merge_plugin_target.T, 1),
        (dispatch_plugin_source, 1),
        (pad_lanes(dispatch_coefficients), 1),
        (pad_lanes(dispatch_plugin_target), 1),
        (pad_lanes(attend_norm_scaling[None]), 1),
        (pad_lanes(branch_norm_scaling[None]), 1),
    ]
    attn_packed = jnp.concatenate([a for a, _ in packed_parts], axis=0)
    attn_all = lax.all_gather(attn_packed, "fsdp", axis=0)
    full = []
    at = 0
    for a, blocks in packed_parts:
        full.append(rows_to_columns(attn_all[:, at : at + a.shape[0]], blocks))
        at += a.shape[0]
    (
        full_qkv,
        full_exit,
        full_qkv_in,
        q_out_t,
        k_out_t,
        v_out_t,
        full_merge_in,
        merge_out_t,
        full_route_in,
        route_padded,
        route_out_padded,
        gain_attn,
        gain_moe,
    ) = full
    full_route = route_padded[:, :expert_count]
    full_route_out = route_out_padded[:, :expert_count]
    attn_gain_f = gain_attn[:, :ru].reshape(model_width).astype(f32)
    moe_gain_f = gain_moe[:, :ru].reshape(model_width).astype(f32)

    chunk_weights = []
    first = 0
    for size in CHUNKS:
        here = slice(first, first + size)
        packed = pack_experts(
            branch_widen_coefficients[here],
            branch_contract_coefficients[here],
            branch_plugin_source[here],
            branch_plugin_target[here],
            contract_plugin_source[here],
            contract_plugin_target[here],
        )
        chunk_weights.append(
            regroup(lax.all_gather(packed, "fsdp", axis=0), model_width, inner_width)
        )
        first += size

    labels = branch_choice_labels.reshape(micro_count, seq_len, top_count)
    expert_range = jnp.arange(expert_count, dtype=jnp.int32)
    picked = labels[..., None] == expert_range
    chosen = jnp.any(picked, axis=2)
    before = jnp.tril(jnp.ones((seq_len, seq_len), bf16), -1)
    rank = jnp.einsum("mse,ts->met", chosen.astype(bf16), before, preferred_element_type=f32)
    chosen_t = jnp.swapaxes(chosen, 1, 2)
    rank = jnp.where(chosen_t, rank.astype(jnp.int32), -1)

    def of_group(a, k):
        return lax.dynamic_slice_in_dim(a, (dp_rank ^ k) * local_experts, local_experts, 1)

    rank_from = [exchange(of_group(rank, k), k) for k in peers]
    cot_from = [exchange(exit_cotangent, k) for k in peers]

    adapters = [plugin_choice_per_text[dp_rank ^ k] for k in peers]
    masks = jnp.stack(
        [(column_holder[None, :] == own[:, None]).astype(f32) for own in adapters]
    )

    saved = []
    for m in range(micro_count):
        rows_here = slice(m * seq_len, (m + 1) * seq_len)
        hidden_float = layer_entering_state[rows_here].astype(f32)
        block_rows = section_labels[m]
        mask = masks[0, m]
        mask3 = jnp.tile(mask, 3)
        normed_f, inverse_attn = norm_scale(hidden_float, attn_gain_f)
        normed = normed_f.astype(bf16)
        qkv_lora = (nn(normed, full_qkv_in) * mask3).astype(bf16)
        adapter_pieces = jnp.concatenate(
            [
                nt(qkv_lora[:, :adapter_width], q_out_t),
                nt(qkv_lora[:, adapter_width : 2 * adapter_width], k_out_t),
                nt(qkv_lora[:, 2 * adapter_width :], v_out_t),
            ],
            axis=1,
        )
        projected = nn(normed, full_qkv) + adapter_pieces
        queries = rotate(
            projected[:, :query_width].reshape(seq_len, H, HD), cos_table, sin_table
        ).astype(bf16)
        keys = rotate(
            projected[:, query_width : query_width + key_value_width].reshape(seq_len, KVH, HD),
            cos_table,
            sin_table,
        ).astype(bf16)
        values = projected[:, query_width + key_value_width :].reshape(seq_len, KVH, HD)
        values = values.astype(bf16)
        grouped = queries.reshape(seq_len, KVH, repeat, HD)
        allowed = block_rows[None, :] <= block_rows[:, None]
        raw = layered_times_effect("qnrd,knd->nrqk", grouped, keys) * score_scale
        scores = jnp.where(allowed, raw, -1e30)
        row_peak = jnp.max(scores, axis=-1, keepdims=True)
        shifted_exp = jnp.exp(scores - row_peak)
        row_total = jnp.sum(shifted_exp, axis=-1, keepdims=True)
        log_total = row_peak + jnp.log(row_total)
        probs_b = (shifted_exp / row_total).astype(bf16)
        attended = (
            layered_times_effect("nrqk,knd->qnrd", probs_b, values)
            .reshape(seq_len, query_width)
            .astype(bf16)
        )
        out_lora = (nn(attended, full_merge_in) * mask).astype(bf16)
        residual = hidden_float + nn(attended, full_exit) + nt(out_lora, merge_out_t)
        moe_f, inverse_moe = norm_scale(residual, moe_gain_f)
        moe_in = moe_f.astype(bf16)
        route_lora = (nn(moe_in, full_route_in) * mask).astype(bf16)
        logits = nn(moe_in, full_route) + nn(route_lora, full_route_out)
        shown = jnp.where(chosen[m], logits, -jnp.inf)
        weight = jnp.exp(shown - jnp.max(shown, axis=1, keepdims=True))
        gates = weight / jnp.sum(weight, axis=1, keepdims=True)
        saved.append(
            (normed, inverse_attn, qkv_lora, queries, keys, values, allowed, log_total, attended)
            + (out_lora, residual, inverse_moe, moe_in, route_lora, gates)
        )
    moe_rows = jnp.concatenate([s[12] for s in saved], axis=0)
    gates_t = jnp.stack([s[14].T for s in saved])

    gate_from = [exchange(of_group(gates_t, k), k) for k in peers]
    rows_from = [exchange(moe_rows, k) for k in peers]
    sent = [
        dispatch(rows_from[k], cot_from[k], rank_from[k], gate_from[k], capacity) for k in peers
    ]
    xs, cs, gs = [s[0] for s in sent], [s[1] for s in sent], [s[2] for s in sent]
    outs = []
    first = 0
    for size, weights in zip(CHUNKS, chunk_weights):
        outs.append(expert_chunk(xs, cs, gs, weights, masks, first, inner_width))
        first += size
    n = dp_count
    order = [3, 1, 2, 0] if n == 4 else list(peers)[::-1]
    grads_home, products_home, mixture_home = {}, {}, {}
    for k in order:
        back, product = combine([o[n + k] for o in outs], [o[2 * n + k] for o in outs], rank_from[k])
        products_home[k] = exchange(product, k)
        grads_home[k] = exchange(back, k)
    for k in order:
        (mix,) = combine([o[k] for o in outs], None, rank_from[k])
        mixture_home[k] = exchange(mix, k)

    adapter_sums = []
    for o in outs:
        g = o[3 * n]
        if shard_count == SHARDS:
            adapter_sums.append(lax.psum_scatter(g, "fsdp", scatter_dimension=0, tiled=False))
        else:
            adapter_sums.append(g)
    rd = inner_width // SHARDS
    wide_rows = 2 * LANES
    if shard_count == SHARDS:
        g = jnp.concatenate(adapter_sums, axis=0).astype(f32)
        cuts = [wide_rows + i * rd for i in range(4)]
        expert_reduce = jnp.swapaxes(g[:, :wide_rows], 1, 2)
        expert_expand = jnp.stack(
            [jnp.swapaxes(g[:, cuts[i] : cuts[i + 1]], 1, 2) for i in range(2)], axis=1
        )
        down_reduce = g[:, cuts[2] : cuts[3]]
        down_expand = g[:, cuts[3] :]
    else:
        g = jnp.concatenate(adapter_sums, axis=1).astype(f32)
        cuts = [wide_rows + i * rd for i in range(4)]

        def rows_joined(a):
            return jnp.swapaxes(a, 0, 1).reshape(a.shape[1], -1, LANES)

        wide = g[:, :, :wide_rows].transpose(1, 0, 3, 2).reshape(local_experts, -1, wide_rows)
        expand = jnp.stack(
            [jnp.swapaxes(rows_joined(g[:, :, cuts[i] : cuts[i + 1]]), 1, 2) for i in range(2)],
            axis=1,
        )
        deep = rows_joined(g[:, :, cuts[2] : cuts[3]])
        last = g[:, :, cuts[3] :].transpose(1, 2, 0, 3).reshape(local_experts, LANES, -1)
        expert_reduce = lax.psum_scatter(wide, "fsdp", scatter_dimension=1, tiled=True)
        expert_expand = lax.psum_scatter(expand, "fsdp", scatter_dimension=3, tiled=True)
        down_reduce = lax.psum_scatter(deep, "fsdp", scatter_dimension=1, tiled=True)
        down_expand = lax.psum_scatter(last, "fsdp", scatter_dimension=2, tiled=True)

    product_t = jnp.stack([products_home[k] for k in peers])
    product_t = jnp.take(product_t, dp_rank ^ jnp.arange(dp_count), axis=0)
    product_t = jnp.swapaxes(product_t, 0, 1).reshape(micro_count, expert_count, seq_len)
    weighted = gates_t * product_t
    select_t = weighted - gates_t * jnp.sum(weighted, axis=1, keepdims=True)
    logit_grads = jnp.swapaxes(select_t, 1, 2).astype(bf16)

    outputs, input_grads, grad_sums = [], [], None
    for m in range(micro_count):
        rows_here = slice(m * seq_len, (m + 1) * seq_len)
        (
            normed,
            inverse_attn,
            qkv_lora,
            queries,
            keys,
            values,
            allowed,
            log_total,
            attended,
            out_lora,
            residual,
            inverse_moe,
            moe_in,
            route_lora,
            gates,
        ) = saved[m]
        mask = masks[0, m]
        mask3 = jnp.tile(mask, 3)
        hidden_float = layer_entering_state[rows_here].astype(f32)
        grad_rows = exit_cotangent[rows_here].astype(f32)
        grouped = queries.reshape(seq_len, KVH, repeat, HD)
        mixture = sum(mixture_home[k][rows_here].astype(f32) for k in peers)
        outputs.append((residual + mixture).astype(bf16))
        logit_grad = logit_grads[m]
        route_lora_grad = (nt(logit_grad, full_route_out) * mask).astype(bf16)
        moe_grad = (
            sum(grads_home[k][rows_here].astype(f32) for k in peers)
            + nt(logit_grad, full_route)
            + nt(route_lora_grad, full_route_in)
        )
        residual_grad = grad_rows + norm_back(residual, inverse_moe, moe_gain_f, moe_grad)
        att_grad = residual_grad.astype(bf16)
        out_lora_grad = (nn(att_grad, merge_out_t) * mask).astype(bf16)
        attended_grad = (nt(att_grad, full_exit) + nt(out_lora_grad, full_merge_in)).astype(bf16)
        head_grad = attended_grad.reshape(seq_len, KVH, repeat, HD)
        raw = layered_times_effect("qnrd,knd->nrqk", grouped, keys) * score_scale
        probs = jnp.exp(jnp.where(allowed, raw, -1e30) - log_total)
        probs_b = probs.astype(bf16)
        prob_grad = layered_times_effect("qnrd,knd->nrqk", head_grad, values)
        score_grad = (
            probs * (prob_grad - jnp.sum(probs * prob_grad, axis=-1, keepdims=True))
        ).astype(bf16)
        query_grad = (
            layered_times_effect("nrqk,knd->qnrd", score_grad, keys).reshape(seq_len, H, HD)
            * score_scale
        )
        key_grad = layered_times_effect("nrqk,qnrd->knd", score_grad, grouped) * score_scale
        value_grad = layered_times_effect("nrqk,qnrd->knd", probs_b, head_grad)
        proj_grad = jnp.concatenate(
            [
                rotate_back(query_grad, cos_table, sin_table).reshape(seq_len, query_width),
                rotate_back(key_grad, cos_table, sin_table).reshape(seq_len, key_value_width),
                value_grad.reshape(seq_len, key_value_width),
            ],
            axis=1,
        ).astype(bf16)
        q_grad = proj_grad[:, :query_width]
        k_grad = proj_grad[:, query_width : query_width + key_value_width]
        v_grad = proj_grad[:, query_width + key_value_width :]
        qkv_lora_grad = (
            jnp.concatenate([nn(q_grad, q_out_t), nn(k_grad, k_out_t), nn(v_grad, v_out_t)], axis=1)
            * mask3
        ).astype(bf16)
        normed_grad = nt(proj_grad, full_qkv) + nt(qkv_lora_grad, full_qkv_in)
        input_grads.append(
            (
                residual_grad + norm_back(hidden_float, inverse_attn, attn_gain_f, normed_grad)
            ).astype(bf16)
        )
        terms = (
            tn(normed, qkv_lora_grad),
            tn(qkv_lora[:, :adapter_width], q_grad),
            tn(k_grad, qkv_lora[:, adapter_width : 2 * adapter_width]),
            tn(v_grad, qkv_lora[:, 2 * adapter_width :]),
            tn(attended, out_lora_grad),
            tn(out_lora, att_grad),
            tn(moe_in, route_lora_grad),
            tn(route_lora, logit_grad),
        )
        grad_sums = terms if grad_sums is None else tuple(a + b for a, b in zip(grad_sums, terms))

    def by_rows(a):
        return columns_to_rows(a.reshape(shard_count, -1, a.shape[1]))

    def by_columns(a):
        part = a.reshape(a.shape[0], shard_count, -1).transpose(1, 0, 2)
        return jnp.pad(part, ((0, 0), (0, 0), (0, LANES - part.shape[2])))

    sizes = [3 * ru, adapter_width, key_value_width // shard_count, key_value_width // shard_count]
    sizes += [ru, adapter_width, ru, adapter_width // shard_count]
    to_sum = jnp.concatenate(
        [
            by_rows(grad_sums[0]),
            by_columns(grad_sums[1]),
            by_rows(grad_sums[2]),
            by_rows(grad_sums[3]),
            by_rows(grad_sums[4]),
            by_columns(grad_sums[5]),
            by_rows(grad_sums[6]),
            by_rows(pad_lanes(grad_sums[7])),
        ],
        axis=1,
    ).astype(bf16)
    shard_sum = lax.psum_scatter(to_sum, "fsdp", scatter_dimension=0, tiled=False)
    total = sum(exchange(shard_sum, k).astype(f32) for k in peers)
    pieces, at = [], 0
    for size in sizes:
        pieces.append(total[at : at + size])
        at += size
    query_cols = query_width // shard_count
    return (
        jnp.concatenate(outputs, axis=0),
        jnp.concatenate(input_grads, axis=0),
        pieces[0].reshape(3, ru, LANES).transpose(1, 0, 2).reshape(ru, 3 * LANES),
        pieces[1][:, :query_cols],
        pieces[2].T,
        pieces[3].T,
        pieces[4],
        pieces[5][:, :ru],
        pieces[6],
        pieces[7][:, :expert_count],
        expert_reduce,
        expert_expand,
        down_reduce,
        down_expand,
    )


def solution(mesh):
    placed = (
        P(("dp", "fsdp"), None),
        P(("dp", "fsdp"), None),
        P("fsdp"),
        P("fsdp"),
        P("fsdp", None),
        P("fsdp", None),
        P("fsdp", None),
        P("dp", "fsdp", None),
        P("dp", "fsdp", None),
        P("fsdp", None),
        P(None, "fsdp"),
        P(None, "fsdp"),
        P(None, "fsdp"),
        P("fsdp", None),
        P(None, "fsdp"),
        P("fsdp", None),
        P("fsdp", None),
        P("dp", "fsdp", None),
        P("dp", None, None, "fsdp"),
        P("dp", "fsdp", None),
        P("dp", None, "fsdp"),
        P(("dp", "fsdp"), None),
        P(None, "fsdp"),
        P(("dp", "fsdp"), None),
    )
    return jax.shard_map(
        local,
        mesh=mesh,
        in_specs=placed,
        out_specs=(
            P(("dp", "fsdp"), None),
            P(("dp", "fsdp"), None),
            P("fsdp", None),
            P(None, "fsdp"),
            P(None, "fsdp"),
            P(None, "fsdp"),
            P("fsdp", None),
            P(None, "fsdp"),
            P("fsdp", None),
            P("fsdp", None),
            P("dp", "fsdp", None),
            P("dp", None, None, "fsdp"),
            P("dp", "fsdp", None),
            P("dp", None, "fsdp"),
        ),
        check_vma=False,
    )
```

time: 1790 us -> 803 us (0.45)
  matrix products: 465 us -> 102 us
  waiting for transfers between devices: 604 us -> 323 us
  local copies, waits for them, and re-layouts: 357 us -> 90.9 us
  Pallas kernels: 0 us -> 182 us
  blocking collectives: 155 us -> 0 us
  other arithmetic: 138 us -> 48.7 us
    dot_general x110 -> x73, matrix products: 465 us -> 102 us  [the longest x12 52.1 us: layered_times_effect(): return jnp.einsum(pattern, operand, factor, preferred_element_type=f32)]
    reduce_scatter x12 -> x5, waiting for transfers between devices: 331 us -> 17.5 us  [the longest x1 17.5 us: local(): lax.psum_scatter(to_sum, 'fsdp', scatter_dimension=0, tiled=False)]
    all_to_all x8 -> x0, waiting for transfers between devices: 227 us -> none  [the longest x4 157 us: to_owners(): lax.all_to_all(rows_block, 'dp', split_axis=1, concat_axis=1, tiled=True)]
    ppermute x0 -> x24, waiting for transfers between devices: none -> 213 us  [exchange(): return lax.ppermute(a, 'dp', [(i, i ^ k) for i in range(size)])]
    pallas_call x0 -> x16, Pallas kernels: none -> 182 us  [the longest x4 117 us: expert_chunk(): pl.pallas_call(functools.partial(expert_kernel, n), grid=(count,), in_spe...]
    all_gather x11 -> x0, blocking collectives: 155 us -> none  [the longest x1 18.9 us: fetch_attention(): lax.all_gather(triple_plugin_source, 'fsdp', axis=0, tiled=True)]
    gather x8 -> x1, local copies, waits for them, and re-layouts: 144 us -> 0.56 us  [local(): product_t = jnp.take(product_t, dp_rank ^ jnp.arange(dp_count), axis=0)]
    all_gather x8 -> x5, waiting for transfers between devices: 0.05 us -> 92.3 us  [the longest x1 64.4 us: local(): attn_all = lax.all_gather(attn_packed, 'fsdp', axis=0)]
  transfers between devices with their start and end apart: 30 -> 34, of which waited for: 18 -> 13; matrix products, arithmetic and copies ran while one was open for 45% -> 26% of each run, Pallas kernels for 0% -> 23%
where the time goes in v1:
time: 803 us; the launch traced here: 798 us
  waiting for transfers between devices  323 us (40%)
  Pallas kernels  182 us (23%)
  matrix products  102 us (13%)
  local copies, waits for them, and re-layouts  90.9 us (11%)
  other arithmetic  48.7 us (6%)
  starting transfers between devices  34.7 us (4%)
  between operations  17.3 us (2%)
    ppermute x24, waiting for transfers between devices, exchange(): return lax.ppermute(a, 'dp', [(i, i ^ k) for i in range(size)])  213 us
    pallas_call x4, Pallas kernels, expert_chunk(): pl.pallas_call(functools.partial(expert_kernel, n), grid=(count,), in_spe...  117 us
    all_gather x1, waiting for transfers between devices, local(): attn_all = lax.all_gather(attn_packed, 'fsdp', axis=0)  64.4 us
    dot_general x12, matrix products, layered_times_effect(): return jnp.einsum(pattern, operand, factor, preferred_element_type=f32)  52.1 us
    pallas_call x8, Pallas kernels, combine(): pl.pallas_call(functools.partial(combine_kernel, len(rows), with_product)...  36.4 us
    unnamed x436, local copies, waits for them, and re-layouts  36 us
    ppermute x24, starting transfers between devices, exchange(): return lax.ppermute(a, 'dp', [(i, i ^ k) for i in range(size)])  34.1 us
    pallas_call x4, Pallas kernels, dispatch(): pl.pallas_call(functools.partial(dispatch_kernel, capacity), grid=(micro,...  28.3 us
  transfers between devices with their start and end apart: 34, of which 13 were waited for; matrix products, arithmetic and copies ran while one was open for 26% of the time, Pallas kernels for 23%

profile of v1, /device:TPU:0, one launch (start us, length us, event | category | flops | bytes accessed | tf_op | source)
XLA Modules:
  0.0 797.7 jit_solution(14708224605502434768)
XLA Ops:
  10.2 8.3 %concatenate.94 = bf16[4242,128]{1,0:T(8,128)(2,1)} concatenate(bf16[2048,128]{1,0:T(8,128)(2,1)S(1)} %bitcast.642, bf16[1024,128]{1,0:T(8,128)(2,1)S(1)} %bitcast.667, bf16[384,128]{1,0:T(8,128)(2,1)S(1)} %bitcast.686, bf16[128,128]{1,0:T(8,128)(2,1)S(1)} %bitcast.702, bf16[64,128]{1,0:T(8,128)(2,1)S(1)} %bitcast.724, bf16[64,128]{1,0:T(8,128)(2,1)S(1)} %bitcast.725, ...), dimensions={0} | concatenate | bytes 2171904 | tf_op jit(solution)/shard_map/concatenate | solution.py:468
  41.6 64.4 %all-gather.20.cloned.1.call-done = bf16[8,4242,128]{2,1,0:T(8,128)(2,1)} async-done(((bf16[1,4242,128]{2,1,0:T(8,128)(2,1)}), bf16[8,4242,128]{2,1,0:T(8,128)(2,1)}) %all-gather.20.cloned.1.call-update) | async-done | bytes 8687632 | tf_op jit(solution)/shard_map/all_gather | solution.py:469
  180.6 64.6 %collective-permute-done.6.rank_ref.refs_4_.refs_8_ = s32[2,8,384]{2,1,0:T(8,128)S(1)} collective-permute-done((s32[2,8,384]{2,1,0:T(8,128)S(1)}, s32[2,8,384]{2,1,0:T(8,128)S(1)}, u32[]{:S(2)}, u32[]{:S(2)}) %collective-permute-start.6) | collective-permute-done | bytes 24608 | tf_op jit(solution)/shard_map/ppermute | solution.py:403
  252.2 7.4 dispatch.4
  260.4 7.0 dispatch.7
  269.5 7.0 dispatch.6
  276.5 41.1 %collective-permute-done.2.rank_ref.refs_4_.refs_8_ = s32[2,8,384]{2,1,0:T(8,128)S(1)} collective-permute-done((s32[2,8,384]{2,1,0:T(8,128)S(1)}, s32[2,8,384]{2,1,0:T(8,128)S(1)}, u32[]{:S(2)}, u32[]{:S(2)}) %collective-permute-start.2) | collective-permute-done | bytes 24608 | tf_op jit(solution)/shard_map/ppermute | solution.py:403
  318.5 7.0 dispatch.5
  325.4 29.2 %experts.7 = (bf16[2,2,112,1024]{3,2,1,0:T(8,128)(2,1)}, bf16[2,2,112,1024]{3,2,1,0:T(8,128)(2,1)}, bf16[2,2,112,1024]{3,2,1,0:T(8,128)(2,1)}, bf16[2,2,112,1024...) custom-call(bf16[2,8,112,1024]{3,2,1,0:T(8,128)(2,1)} %get-tuple-ele, ...), custom_call_target="tpu_custom_call" | custom-call | flops 17920000000 | bytes 40632320 | tf_op jit(solution)/shard_map/experts/pallas_call | solution.py:308
  354.7 29.2 %experts.6 = (bf16[2,2,112,1024]{3,2,1,0:T(8,128)(2,1)}, bf16[2,2,112,1024]{3,2,1,0:T(8,128)(2,1)}, bf16[2,2,112,1024]{3,2,1,0:T(8,128)(2,1)}, bf16[2,2,112,1024...) custom-call(bf16[2,8,112,1024]{3,2,1,0:T(8,128)(2,1)} %get-tuple-ele, ...), custom_call_target="tpu_custom_call" | custom-call | flops 17920000000 | bytes 40632320 | tf_op jit(solution)/shard_map/experts/pallas_call | solution.py:308
  384.0 29.5 %experts.5 = (bf16[2,2,112,1024]{3,2,1,0:T(8,128)(2,1)}, bf16[2,2,112,1024]{3,2,1,0:T(8,128)(2,1)}, bf16[2,2,112,1024]{3,2,1,0:T(8,128)(2,1)}, bf16[2,2,112,1024...) custom-call(bf16[2,8,112,1024]{3,2,1,0:T(8,128)(2,1)} %get-tuple-ele, ...), custom_call_target="tpu_custom_call" | custom-call | flops 17920000000 | bytes 40632320 | tf_op jit(solution)/shard_map/experts/pallas_call | solution.py:308
  415.6 27.9 %all-gather.12.cloned.1.call-done = bf16[16,2112,128]{2,1,0:T(8,128)(2,1)} async-done(((bf16[2,2112,128]{2,1,0:T(8,128)(2,1)}), bf16[16,2112,128]{2,1,0:T(8,128)(2,1)}) %all-gather.12.cloned.1.call-update) | async-done | bytes 8650768 | tf_op jit(solution)/shard_map/all_gather | solution.py:508
  443.4 29.1 %experts.4 = (bf16[2,2,112,1024]{3,2,1,0:T(8,128)(2,1)}, bf16[2,2,112,1024]{3,2,1,0:T(8,128)(2,1)}, bf16[2,2,112,1024]{3,2,1,0:T(8,128)(2,1)}, bf16[2,2,112,1024...) custom-call(bf16[2,8,112,1024]{3,2,1,0:T(8,128)(2,1)} %get-tuple-ele, ...), custom_call_target="tpu_custom_call" | custom-call | flops 17920000000 | bytes 40632320 | tf_op jit(solution)/shard_map/experts/pallas_call | solution.py:308
  521.1 6.6 collective-permute-done.15
  534.2 28.7 %collective-permute-done.16 = bf16[768,1024]{1,0:T(8,128)(2,1)} collective-permute-done((bf16[768,1024]{1,0:T(8,128)(2,1)}, bf16[768,1024]{1,0:T(8,128)(2,1)}, u32[]{:S(2)}, u32[]{:S(2)}) %collective-permute-start.16) | collective-permute-done | bytes 1572896 | tf_op jit(solution)/shard_map/ppermute | solution.py:403
  565.9 29.3 %collective-permute-done.12 = bf16[768,1024]{1,0:T(8,128)(2,1)} collective-permute-done((bf16[768,1024]{1,0:T(8,128)(2,1)}, bf16[768,1024]{1,0:T(8,128)(2,1)}, u32[]{:S(2)}, u32[]{:S(2)}) %collective-permute-start.12) | collective-permute-done | bytes 1572896 | tf_op jit(solution)/shard_map/ppermute | solution.py:403
  595.2 33.5 %collective-permute-done.13 = bf16[768,1024]{1,0:T(8,128)(2,1)} collective-permute-done((bf16[768,1024]{1,0:T(8,128)(2,1)}, bf16[768,1024]{1,0:T(8,128)(2,1)}, u32[]{:S(2)}, u32[]{:S(2)}) %collective-permute-start.13) | collective-permute-done | bytes 1572896 | tf_op jit(solution)/shard_map/ppermute | solution.py:403
  639.9 6.8 fusion.98
  646.8 8.5 %fusion = (f32[8,2,384]{2,1,0:T(2,128)}, f32[8,384,384,2]{2,1,3,0:T(8,128)}) fusion(f32[8,2,384]{2,1,0:T(2,128)S(1)} %bitcast.699, f32[8,384,384,2]{2,1,3,0:T(8,128)} %copy-done, pred[384,384]{0,1:T(8,128)(4,1)S(1)} %copy-done.60, bf16[384,8,64,1]{0,2,3,1:T(8,128)(2,1)S(1)} %bitcast.665, bf16[384,8,2,64]{0,3,2,1:T(8,128)(2,1)S(1)} %bitcast.616), kind=kOutput, calls=%fused_computation.3 | convolution fusion | flops 313780224 | bytes 20250624 | tf_op jit(solution)/shard_map/qnrd,knd->nrqk/dot_general | solution.py:47
  662.8 7.1 fusion.101
  669.9 8.3 %fusion.3 = (f32[8,2,384]{2,1,0:T(2,128)}, f32[8,384,384,2]{2,1,3,0:T(8,128)}) fusion(f32[8,2,384]{2,1,0:T(2,128)S(1)} %bitcast.696, f32[8,384,384,2]{2,1,3,0:T(8,128)} %copy-done.1, pred[384,384]{0,1:T(8,128)(4,1)S(1)} %get-tuple-element.381, bf16[384,8,64,1]{0,2,3,1:T(8,128)(2,1)S(1)} %bitcast.663, bf16[384,8,2,64]{0,3,2,1:T(8,128)(2,1)S(1)} %bitcast.618), kind=kOutput, calls=%fused_computation.8 | convolution fusion | flops 313780224 | bytes 20250624 | tf_op jit(solution)/shard_map/qnrd,knd->nrqk/dot_general | solution.py:47
  678.2 11.1 %fusion.2 = bf16[8,2,384,384]{2,3,1,0:T(8,128)(2,1)} fusion(f32[8,384,384,2]{2,1,3,0:T(8,128)} %get-tuple-element.374, f32[8,2,384]{2,1,0:T(2,128)S(1)} %copy-done.128, f32[8,2,384]{2,1,0:T(2,128)S(1)} %bitcast.700, f32[8,384,384,2]{2,1,3,0:T(8,128)} %copy-done, pred[384,384]{0,1:T(8,128)(4,1)S(1)} %copy-done.61), kind=kLoop, calls=%fused_computation.5 | loop fusion | flops 14155776 | bytes 23789568 | tf_op jit(solution)/shard_map/convert_element_type | solution.py:702
  696.5 11.1 %fusion.5 = bf16[8,2,384,384]{2,3,1,0:T(8,128)(2,1)} fusion(f32[8,384,384,2]{2,1,3,0:T(8,128)} %get-tuple-element.372, f32[8,2,384]{2,1,0:T(2,128)S(1)} %copy-done.129, f32[8,2,384]{2,1,0:T(2,128)S(1)} %bitcast.697, f32[8,384,384,2]{2,1,3,0:T(8,128)} %copy-done.1, pred[384,384]{0,1:T(8,128)(4,1)S(1)} %get-tuple-element.381), kind=kLoop, calls=%fused_computation.10 | loop fusion | flops 14155776 | bytes 23789568 | tf_op jit(solution)/shard_map/convert_element_type | solution.py:702
  756.5 17.5 %reduce-scatter.6.cloned.1.call-done = bf16[1,1040,128]{2,1,0:T(8,128)(2,1)} async-done(((bf16[8,1040,128]{2,1,0:T(8,128)(2,1)}), bf16[1,1040,128]{2,1,0:T(8,128)(2,1)}) %reduce-scatter.6.cloned.1.call-update) | async-done | bytes 266256 | tf_op jit(solution)/shard_map/reduce_scatter | solution.py:764
  (690 shorter events, 260.3 us)
Async XLA Ops:
  7.2 98.8 %all-gather.20.cloned.1.call-start = ((), (), s32[]{:S(2)}) async-start(), calls=%async_computation.14 | async-start | bytes 9787392 | tf_op jit(solution)/shard_map/all_gather | solution.py:469
  18.6 306.9 %all-gather.18.cloned.1.call-start = ((), (), s32[]{:S(2)}) async-start(), calls=%async_computation.13 | async-start | bytes 9732096 | tf_op jit(solution)/shard_map/all_gather | solution.py:508
  27.4 327.4 %all-gather.16.cloned.1.call-start = ((), (), s32[]{:S(2)}) async-start(), calls=%async_computation.12 | async-start | bytes 9732096 | tf_op jit(solution)/shard_map/all_gather | solution.py:508
  28.6 355.4 %all-gather.14.cloned.1.call-start = ((), (), s32[]{:S(2)}) async-start(), calls=%async_computation.11 | async-start | bytes 9732096 | tf_op jit(solution)/shard_map/all_gather | solution.py:508
  29.4 414.0 %all-gather.12.cloned.1.call-start = ((), (), s32[]{:S(2)}) async-start(), calls=%async_computation.10 | async-start | bytes 9732096 | tf_op jit(solution)/shard_map/all_gather | solution.py:508
  29.5 217.5 %collective-permute-start.9 = (bf16[768,1024]{1,0:T(8,128)(2,1)}, bf16[768,1024]{1,0:T(8,128)(2,1)}, u32[]{:S(2)}, u32[]{:S(2)}) collective-permute-start(bf16[768,1024]{1,0:T(8,128)(2,1)} %c_ref.1), channel_id=1, source_target_pairs={{0,24},{8,16},{16,8},{24,0},{1,25},{9,17},{17,9},{25,1},{2,26},{10... | collective-permute-start | bytes 4718600 | tf_op jit(solution)/shard_map/ppermute | solution.py:403
  33.4 233.9 %collective-permute-start.5 = (bf16[768,1024]{1,0:T(8,128)(2,1)}, bf16[768,1024]{1,0:T(8,128)(2,1)}, u32[]{:S(2)}, u32[]{:S(2)}) collective-permute-start(bf16[768,1024]{1,0:T(8,128)(2,1)} %c_ref.1), channel_id=1, source_target_pairs={{0,16},{8,24},{16,0},{24,8},{1,17},{9,25},{17,1},{25,9},{2,18},{10... | collective-permute-start | bytes 4718600 | tf_op jit(solution)/shard_map/ppermute | solution.py:403
  35.1 143.4 %collective-permute-start.10 = (s32[2,8,384]{2,1,0:T(8,128)}, s32[2,8,384]{2,1,0:T(8,128)}, u32[]{:S(2)}, u32[]{:S(2)}) collective-permute-start(s32[2,8,384]{2,1,0:T(8,128)} %get-tuple-element.326), channel_id=1, source_target_pairs={{0,24},{8,16},{16,8},{24,0},{1,25},{9,17},{17,9},{25,1},{2,26},{10... | collective-permute-start | bytes 73736 | tf_op jit(solution)/shard_map/ppermute | solution.py:403
  37.7 715.8 %reduce-scatter.14.cloned.1.call-start = ((), (), s32[]{:S(2)}) async-start(), calls=%async_computation.9 | async-start | bytes 2654208 | tf_op jit(solution)/shard_map/reduce_scatter | solution.py:617
  173.3 86.3 %collective-permute-start.8 = (bf16[768,1024]{1,0:T(8,128)(2,1)}, bf16[768,1024]{1,0:T(8,128)(2,1)}, u32[]{:S(2)}, u32[]{:S(2)}) collective-permute-start(bf16[768,1024]{1,0:T(8,128)(2,1)} %pad_maximum_fusion.x_ref), channel_id=1, source_target_pairs={{0,24},{8,16},{16,8},{24,0},{1,25},{9,17},{17,9},{25,1},{2,26},{10... | collective-permute-start | bytes 4718600 | tf_op jit(solution)/shard_map/ppermute | solution.py:403
  175.8 93.7 %collective-permute-start.4 = (bf16[768,1024]{1,0:T(8,128)(2,1)}, bf16[768,1024]{1,0:T(8,128)(2,1)}, u32[]{:S(2)}, u32[]{:S(2)}) collective-permute-start(bf16[768,1024]{1,0:T(8,128)(2,1)} %pad_maximum_fusion.x_ref), channel_id=1, source_target_pairs={{0,16},{8,24},{16,0},{24,8},{1,17},{9,25},{17,1},{25,9},{2,18},{10... | collective-permute-start | bytes 4718600 | tf_op jit(solution)/shard_map/ppermute | solution.py:403
  178.4 66.8 %collective-permute-start.6 = (s32[2,8,384]{2,1,0:T(8,128)S(1)}, s32[2,8,384]{2,1,0:T(8,128)S(1)}, u32[]{:S(2)}, u32[]{:S(2)}) collective-permute-start(s32[2,8,384]{2,1,0:T(8,128)S(1)} %copy-done.148), channel_id=1, source_target_pairs={{0,16},{8,24},{16,0},{24,8},{1,17},{9,25},{17,1},{25,9},{2,18},{10... | collective-permute-start | bytes 73736 | tf_op jit(solution)/shard_map/ppermute | solution.py:403
  247.0 70.7 %collective-permute-start.1 = (bf16[768,1024]{1,0:T(8,128)(2,1)}, bf16[768,1024]{1,0:T(8,128)(2,1)}, u32[]{:S(2)}, u32[]{:S(2)}) collective-permute-start(bf16[768,1024]{1,0:T(8,128)(2,1)} %c_ref.1), channel_id=1, source_target_pairs={{0,8},{8,0},{16,24},{24,16},{1,9},{9,1},{17,25},{25,17},{2,10},{10... | collective-permute-start | bytes 4718600 | tf_op jit(solution)/shard_map/ppermute | solution.py:403
  249.9 68.0 %collective-permute-start = (bf16[768,1024]{1,0:T(8,128)(2,1)}, bf16[768,1024]{1,0:T(8,128)(2,1)}, u32[]{:S(2)}, u32[]{:S(2)}) collective-permute-start(bf16[768,1024]{1,0:T(8,128)(2,1)} %pad_maximum_fusion.x_ref), channel_id=1, source_target_pairs={{0,8},{8,0},{16,24},{24,16},{1,9},{9,1},{17,25},{25,17},{2,10},{10... | collective-permute-start | bytes 4718600 | tf_op jit(solution)/shard_map/ppermute | solution.py:403
  267.4 50.2 %collective-permute-start.2 = (s32[2,8,384]{2,1,0:T(8,128)S(1)}, s32[2,8,384]{2,1,0:T(8,128)S(1)}, u32[]{:S(2)}, u32[]{:S(2)}) collective-permute-start(s32[2,8,384]{2,1,0:T(8,128)S(1)} %copy-done.147), channel_id=1, source_target_pairs={{0,8},{8,0},{16,24},{24,16},{1,9},{9,1},{17,25},{25,17},{2,10},{10... | collective-permute-start | bytes 73736 | tf_op jit(solution)/shard_map/ppermute | solution.py:403
  268.9 49.0 %collective-permute-start.3 = (f32[2,8,384]{2,1,0:T(8,128)S(1)}, f32[2,8,384]{2,1,0:T(8,128)S(1)}, u32[]{:S(2)}, u32[]{:S(2)}) collective-permute-start(f32[2,8,384]{2,1,0:T(8,128)S(1)} %get-tuple-element.324), channel_id=1, source_target_pairs={{0,8},{8,0},{16,24},{24,16},{1,9},{9,1},{17,25},{25,17},{2,10},{10... | collective-permute-start | bytes 73736 | tf_op jit(solution)/shard_map/ppermute | solution.py:403
  354.6 398.9 %reduce-scatter.12.cloned.1.call-start = ((), (), s32[]{:S(2)}) async-start(), calls=%async_computation.8 | async-start | bytes 2654208 | tf_op jit(solution)/shard_map/reduce_scatter | solution.py:617
  384.0 369.5 %reduce-scatter.10.cloned.1.call-start = ((), (), s32[]{:S(2)}) async-start(), calls=%async_computation.7 | async-start | bytes 2654208 | tf_op jit(solution)/shard_map/reduce_scatter | solution.py:617
  413.6 339.9 %reduce-scatter.8.cloned.1.call-start = ((), (), s32[]{:S(2)}) async-start(), calls=%async_computation.6 | async-start | bytes 2654208 | tf_op jit(solution)/shard_map/reduce_scatter | solution.py:617
  491.6 71.4 %collective-permute-start.16 = (bf16[768,1024]{1,0:T(8,128)(2,1)}, bf16[768,1024]{1,0:T(8,128)(2,1)}, u32[]{:S(2)}, u32[]{:S(2)}) collective-permute-start(bf16[768,1024]{1,0:T(8,128)(2,1)} %get-tuple-element.140), channel_id=1, source_target_pairs={{0,16},{8,24},{16,0},{24,8},{1,17},{9,25},{17,1},{25,9},{2,18},{10... | collective-permute-start | bytes 4718600 | tf_op jit(solution)/shard_map/ppermute | solution.py:403
  493.1 280.8 %reduce-scatter.6.cloned.1.call-start = ((), (), s32[]{:S(2)}) async-start(), calls=%async_computation.5 | async-start | bytes 2396160 | tf_op jit(solution)/shard_map/reduce_scatter | solution.py:764
  516.2 79.0 %collective-permute-start.12 = (bf16[768,1024]{1,0:T(8,128)(2,1)}, bf16[768,1024]{1,0:T(8,128)(2,1)}, u32[]{:S(2)}, u32[]{:S(2)}) collective-permute-start(bf16[768,1024]{1,0:T(8,128)(2,1)} %combine.9), channel_id=1, source_target_pairs={{0,8},{8,0},{16,24},{24,16},{1,9},{9,1},{17,25},{25,17},{2,10},{10... | collective-permute-start | bytes 4718600 | tf_op jit(solution)/shard_map/ppermute | solution.py:403
  517.7 111.0 %collective-permute-start.13 = (bf16[768,1024]{1,0:T(8,128)(2,1)}, bf16[768,1024]{1,0:T(8,128)(2,1)}, u32[]{:S(2)}, u32[]{:S(2)}) collective-permute-start(bf16[768,1024]{1,0:T(8,128)(2,1)} %combine.10), channel_id=1, source_target_pairs={{0,16},{8,24},{16,0},{24,8},{1,17},{9,25},{17,1},{25,9},{2,18},{10... | collective-permute-start | bytes 4718600 | tf_op jit(solution)/shard_map/ppermute | solution.py:403
  527.7 101.0 %collective-permute-start.14 = (bf16[768,1024]{1,0:T(8,128)(2,1)}, bf16[768,1024]{1,0:T(8,128)(2,1)}, u32[]{:S(2)}, u32[]{:S(2)}) collective-permute-start(bf16[768,1024]{1,0:T(8,128)(2,1)} %combine.11), channel_id=1, source_target_pairs={{0,24},{8,16},{16,8},{24,0},{1,25},{9,17},{17,9},{25,1},{2,26},{10... | collective-permute-start | bytes 4718600 | tf_op jit(solution)/shard_map/ppermute | solution.py:403
  (211 other events, 2658.7 us)
Sparse Core Ops, SparseCore 0:
  18.7 87.3 all-gather.19
  107.7 82.7 all-gather.17
  192.1 82.7 all-gather.15
  276.4 82.7 all-gather.13
  360.6 82.7 all-gather.11
  445.6 34.7 reduce-scatter.13
  482.7 35.7 reduce-scatter.11
  520.8 35.6 reduce-scatter.9
  558.8 35.4 reduce-scatter.7
  740.5 33.4 reduce-scatter.5

commit v2 on v1

v2 whole, which is shorter than its diff:
```python
import functools

import jax
import jax.numpy as jnp
from jax import lax
from jax.experimental import pallas as pl
from jax.experimental.pallas import tpu as pltpu
from jax.sharding import PartitionSpec as P

H = 16
KVH = 8
HD = 64
FEEDFORWARD_SIZE = 512
PLUGIN_CHOICES = 8
REDUCED_DIM = 16

eps_norm = 1e-06
rope_base = 10000.0

LANES = 128
SHARDS = 8
CHUNKS = (4, 2, 2)
EXTRA = 16
VMEM = 60 * 1024 * 1024

f32 = jnp.float32
bf16 = jnp.bfloat16


def nn(a, b):
    return lax.dot_general(a, b, (((1,), (0,)), ((), ())), preferred_element_type=f32)


def nt(a, b):
    return lax.dot_general(a, b, (((1,), (1,)), ((), ())), preferred_element_type=f32)


def tn(a, b):
    return lax.dot_general(a, b, (((0,), (0,)), ((), ())), preferred_element_type=f32)


def rotation(length):
    half_size = HD // 2
    frequency = rope_base ** (-(2.0 * jnp.arange(half_size, dtype=f32)) / HD)
    angles = jnp.arange(length, dtype=f32)[:, None] * frequency[None, :]
    return tuple(jnp.tile(f(angles), (1, LANES // half_size)) for f in (jnp.cos, jnp.sin))


def columns_to_rows(a):
    r, c = a.shape[-2:]
    b = c // LANES
    a = a.reshape(a.shape[:-1] + (b, LANES))
    return jnp.swapaxes(a, -3, -2).reshape(a.shape[:-3] + (b * r, LANES))


def pad_lanes(a):
    return jnp.pad(a, ((0, 0), (0, LANES - a.shape[-1])))


def pack_experts(widen, contract, up_source, up_target, down_source, down_target):
    count = widen.shape[0]
    return jnp.concatenate(
        [
            columns_to_rows(widen),
            columns_to_rows(contract),
            columns_to_rows(up_source),
            jnp.swapaxes(up_target, 2, 3).reshape(count, -1, LANES),
            down_source,
            jnp.swapaxes(down_target, 1, 2),
        ],
        axis=1,
    )


def regroup(gathered, width, inner):
    n, count = gathered.shape[:2]
    if n == SHARDS:
        return gathered
    per = n // SHARDS
    pieces, at = [], 0
    ru, rd = width // n, inner // n
    blocks = ((width // LANES, ru), (width // LANES, rd), (2, ru), (2, rd), (1, rd), (1, ru))
    for b, r in blocks:
        piece = gathered[:, :, at : at + b * r].reshape(SHARDS, per, count, b, r, LANES)
        at += b * r
        pieces.append(piece.transpose(0, 2, 3, 1, 4, 5).reshape(SHARDS, count, b * per * r, LANES))
    return jnp.concatenate(pieces, axis=2)


def hits_of(rank_row, capacity):
    rows = lax.broadcasted_iota(jnp.int32, (capacity, rank_row.shape[1]), 0)
    return rows == rank_row.astype(jnp.int32)


def pieces_of(value):
    high = value.astype(bf16).astype(f32)
    rest = value - high
    middle = rest.astype(bf16).astype(f32)
    return [high, middle, rest - middle]


def put_extra(ref, rows, length, value):
    spare = 2 * EXTRA - value.shape[0]
    if spare:
        value = jnp.concatenate([value, jnp.zeros((spare, length), f32)], axis=0)
    value = value.astype(bf16)
    for i in range(2):
        ref[rows : rows + EXTRA, i * length : (i + 1) * length] = value[i * EXTRA : (i + 1) * EXTRA]
    ref[rows : rows + EXTRA, 2 * length :] = jnp.zeros((EXTRA, ref.shape[1] - 2 * length), bf16)


def get_extra(ref, rows, length):
    return jnp.concatenate(
        [ref[rows : rows + EXTRA, i * length : (i + 1) * length] for i in range(2)], axis=0
    ).astype(f32)


def dispatch_kernel(peers, capacity, *refs):
    x_refs, cots = refs[:peers], refs[peers : 2 * peers]
    xs_ref, cs_ref, gs_ref, rank_ref = refs[2 * peers :]
    count, _, width = xs_ref.shape[1:]
    length = cots[0].shape[0]
    shape = xs_ref.shape[1:]
    for i in range(peers):

        @pl.when(pl.program_id(0) == i)
        def _():
            table = get_extra(x_refs[i], length, length)
            rank_ref[0] = table[:count]
            gates = table[count : 2 * count] + table[2 * count : 3 * count] + table[3 * count :]
            hot = []
            for e in range(count):
                hits = hits_of(table[e : e + 1], capacity)
                hot.append(jnp.where(hits, 1.0, 0.0).astype(bf16))
                gate = jnp.sum(jnp.where(hits, gates[e : e + 1], 0.0), axis=1, keepdims=True)
                gs_ref[0, e] = jnp.broadcast_to(gate, (capacity, LANES))
            hot = jnp.concatenate(hot, axis=0)
            xs_ref[0] = nn(hot, x_refs[i][:length]).astype(bf16).reshape(shape)
            cs_ref[0] = nn(hot, cots[i][...]).astype(bf16).reshape(shape)


def dispatch(rows, cots, count, capacity):
    peers = len(rows)
    length, width = cots[0].shape

    def out_spec(lanes):
        return pl.BlockSpec((1, count, capacity, lanes), lambda k: (k, 0, 0, 0))

    def shaped(lanes, dtype):
        return jax.ShapeDtypeStruct((peers, count, capacity, lanes), dtype)

    slots = peers * count * capacity
    return pl.pallas_call(
        functools.partial(dispatch_kernel, peers, capacity),
        grid=(peers,),
        in_specs=[pl.BlockSpec(a.shape, lambda k: (0, 0)) for a in (*rows, *cots)],
        out_specs=[
            out_spec(width),
            out_spec(width),
            out_spec(LANES),
            pl.BlockSpec((1, count, length), lambda k: (k, 0, 0)),
        ],
        out_shape=[
            shaped(width, bf16),
            shaped(width, bf16),
            shaped(LANES, f32),
            jax.ShapeDtypeStruct((peers, count, length), f32),
        ],
        compiler_params=pltpu.CompilerParams(vmem_limit_bytes=VMEM),
        cost_estimate=pl.CostEstimate(
            flops=4 * slots * length * width, bytes_accessed=8 * slots * width, transcendentals=0
        ),
        name="dispatch",
    )(*rows, *cots)


def expert_kernel(first, micro, held, add, final, *refs):
    tables, x_refs, c_refs, g_refs = (refs[i * micro : (i + 1) * micro] for i in range(4))
    w_ref, mask_ref = refs[4 * micro : 4 * micro + 2]
    n, _, capacity, width = x_refs[0].shape
    at = 4 * micro + 2
    old_products = refs[at : at + held]
    old_grads = refs[at + held]
    outs = refs[at + held + 1 :]
    y_refs, m_refs = outs[:n], outs[n : 2 * n]
    grad_ref = outs[2 * n]
    prod_refs = outs[2 * n + 1 : 2 * n + 1 + micro]
    wide, deep, source, sums_a, sums_b, sums_c, sums_d, sums_e = outs[2 * n + 1 + micro :]
    expert = pl.program_id(0)
    if held:

        @pl.when(expert == 0)
        def _():
            for old, new in zip(old_products, prod_refs):
                new[...] = old[...]

    inner_width = deep.shape[0]
    ru, rd = width // SHARDS, inner_width // SHARDS
    blocks = width // LANES
    at = 0

    def part(rows):
        nonlocal at
        value = w_ref[:, 0, at : at + rows, :].reshape(SHARDS * rows, LANES)
        at += rows
        return value

    for j in range(blocks):
        wide[:, j * LANES : (j + 1) * LANES] = part(ru)
    for j in range(blocks):
        deep[:, j * LANES : (j + 1) * LANES] = part(rd)
    for j in range(2):
        source[:, j * LANES : (j + 1) * LANES] = part(ru)
    target_gate, target_up = part(rd), part(rd)
    down_source = part(rd)
    down_target = part(ru)

    size = n * capacity
    for m in range(micro):
        x = x_refs[m][:, 0].reshape(size, width)
        cot = c_refs[m][:, 0].reshape(size, width)
        gate_of_slot = g_refs[m][:, 0].reshape(size, LANES)[:, :1]
        mask = jnp.concatenate(
            [jnp.broadcast_to(mask_ref[m, k : k + 1, :], (capacity, LANES)) for k in range(n)],
            axis=0,
        )
        mask2 = jnp.concatenate([mask, mask], axis=1)
        lora = (nn(x, source[...]) * mask2).astype(bf16)
        gate_up = nn(x, wide[...])
        gate = gate_up[:, :inner_width] + nt(lora[:, :LANES], target_gate)
        up = gate_up[:, inner_width:] + nt(lora[:, LANES:], target_up)
        sig = jax.nn.sigmoid(gate)
        silu = gate * sig
        inner = (silu * up).astype(bf16)
        down_lora = (nn(inner, down_source) * mask).astype(bf16)
        rows = (nn(inner, deep[...]) + nt(down_lora, down_target)).astype(bf16)
        rows_f = rows.astype(f32)
        cot_f = cot.astype(f32)
        product = jnp.sum(rows_f * cot_f, axis=1, keepdims=True)
        weighted = (rows_f * gate_of_slot).astype(bf16)
        row_grad = (cot_f * gate_of_slot).astype(bf16)
        down_lora_grad = (nn(row_grad, down_target) * mask).astype(bf16)
        inner_grad = nt(row_grad, deep[...]) + nt(down_lora_grad, down_source)
        gate_grad = (inner_grad * up * (sig * (1.0 + gate * (1.0 - sig)))).astype(bf16)
        up_grad = (inner_grad * silu).astype(bf16)
        lora_grad = (
            jnp.concatenate([nn(gate_grad, target_gate), nn(up_grad, target_up)], axis=1) * mask2
        ).astype(bf16)
        back = (
            nt(gate_grad, wide[:, :inner_width])
            + nt(up_grad, wide[:, inner_width:])
            + nt(lora_grad, source[...])
        ).astype(bf16)
        for k in range(n):
            here = slice(k * capacity, (k + 1) * capacity)
            y_refs[k][m, 0] = weighted[here]
            if final:
                place = pl.ds(pl.multiple_of(expert * capacity, EXTRA), capacity)
                m_refs[k][place, :] = back[here]
            else:
                m_refs[k][m, 0] = back[here]
            hits = hits_of(tables[m][k, pl.ds(first + expert, 1), :], capacity)
            prod_refs[m][k, pl.ds(first + expert, 1), :] = jnp.sum(
                jnp.where(hits, product[here], 0.0), axis=0, keepdims=True
            )
        terms = (
            tn(lora_grad, x),
            tn(lora[:, :LANES], gate_grad),
            tn(lora[:, LANES:], up_grad),
            tn(down_lora_grad, inner),
            tn(down_lora, row_grad),
        )
        for ref, term in zip((sums_a, sums_b, sums_c, sums_d, sums_e), terms):
            ref[...] = term if m == 0 else ref[...] + term
    if final:

        @pl.when(expert == pl.num_programs(0) - 1)
        def _():
            for k in range(n):
                rows = m_refs[k].shape[0] - EXTRA
                value = jnp.concatenate(pieces_of(prod_refs[0][k]), axis=0)
                put_extra(m_refs[k], rows, value.shape[1], value)

    def put(place, value):
        if add:
            value = value + old_grads[place].astype(f32)
        grad_ref[place] = value.astype(bf16)

    for s in range(SHARDS):
        put((s, 0, slice(0, 2 * LANES)), sums_a[:, s * ru : (s + 1) * ru])
    out = 2 * LANES
    for ref in (sums_b, sums_c, sums_d):
        put((slice(None), 0, slice(out, out + rd)), ref[...].T.reshape(SHARDS, rd, LANES))
        out += rd
    for s in range(SHARDS):
        put((s, 0, slice(out, out + LANES)), sums_e[:, s * ru : (s + 1) * ru])


def expert_chunk(
    slots, weights, masks, first, inner_width, grad_at, grad_count, grads, products, add, final
):
    micro = len(slots)
    tables = [t[3] for t in slots]
    n, local_count, capacity, width = slots[0][0].shape
    count, rows = weights.shape[1:3]
    rd = inner_width // SHARDS
    grad_rows = 2 * LANES + 3 * rd + LANES
    prod_shape = (n, local_count, tables[0].shape[2])

    def slot_spec(lanes):
        return pl.BlockSpec((n, 1, capacity, lanes), lambda e: (0, first + e, 0, 0))

    out_spec = pl.BlockSpec((micro, 1, capacity, width), lambda e: (0, e, 0, 0))
    out_shape = jax.ShapeDtypeStruct((micro, count, capacity, width), bf16)
    back_spec, back_shape = out_spec, out_shape
    if final:
        back_shape = jax.ShapeDtypeStruct((count * capacity + EXTRA, width), bf16)
        back_spec = pl.BlockSpec(back_shape.shape, lambda e: (0, 0))
    grad_spec = pl.BlockSpec((SHARDS, 1, grad_rows, LANES), lambda e: (0, grad_at + e, 0, 0))
    prod_spec = pl.BlockSpec(prod_shape, lambda e: (0, 0, 0))
    work = n * micro * capacity * count
    held = products or []
    kept = jnp.zeros((8, LANES), f32) if grads is None else grads
    return pl.pallas_call(
        functools.partial(expert_kernel, first, micro, len(held), add, final),
        grid=(count,),
        in_specs=[pl.BlockSpec(tables[0].shape, lambda e: (0, 0, 0))] * micro
        + [slot_spec(width)] * (2 * micro)
        + [slot_spec(LANES)] * micro
        + [
            pl.BlockSpec((SHARDS, 1, rows, LANES), lambda e: (0, e, 0, 0)),
            pl.BlockSpec(masks.shape, lambda e: (0, 0, 0)),
        ]
        + [prod_spec] * len(held)
        + [grad_spec if add else pl.BlockSpec(memory_space=pl.ANY)],
        out_specs=[out_spec] * n + [back_spec] * n + [grad_spec] + [prod_spec] * micro,
        out_shape=[out_shape] * n
        + [back_shape] * n
        + [jax.ShapeDtypeStruct((SHARDS, grad_count, grad_rows, LANES), bf16)]
        + [jax.ShapeDtypeStruct(prod_shape, f32)] * micro,
        scratch_shapes=[
            pltpu.VMEM((width, 2 * inner_width), bf16),
            pltpu.VMEM((inner_width, width), bf16),
            pltpu.VMEM((width, 2 * LANES), bf16),
            pltpu.VMEM((2 * LANES, width), f32),
            pltpu.VMEM((LANES, inner_width), f32),
            pltpu.VMEM((LANES, inner_width), f32),
            pltpu.VMEM((LANES, inner_width), f32),
            pltpu.VMEM((LANES, width), f32),
        ],
        compiler_params=pltpu.CompilerParams(vmem_limit_bytes=VMEM),
        cost_estimate=pl.CostEstimate(
            flops=10 * 1000 * 1000 * work,
            bytes_accessed=8 * work * width + 6 * count * rows * LANES * SHARDS,
            transcendentals=work * inner_width,
        ),
        input_output_aliases={} if grads is None else {2 + 4 * micro + len(held): 2 * n},
        name="experts",
    )(
        *tables, *[t[0] for t in slots], *[t[1] for t in slots], *[t[2] for t in slots],
        weights, masks, *held, kept,
    )


def combine_kernel(peer, chunks, micro, added, *refs):
    tables, row_refs = refs[:micro], refs[micro : micro + chunks]
    outs = refs[micro + chunks + (added is not None) :]
    capacity, width = row_refs[0].shape[2:]
    length = tables[0].shape[2]
    for m in range(micro):
        total = None
        e = 0
        for ref in row_refs:
            hot = []
            here = ref.shape[1]
            for i in range(here):
                hits = hits_of(tables[m][peer, e : e + 1, :], capacity)
                hot.append(jnp.where(hits, 1.0, 0.0).astype(bf16))
                e += 1
            term = tn(jnp.concatenate(hot, axis=0), ref[m].reshape(here * capacity, width))
            total = term if total is None else total + term
        if added == m:
            total = total + refs[micro + chunks][...].astype(f32)
        if len(outs) > 1:
            outs[m][...] = total.astype(bf16)
        else:
            outs[0][m * length : (m + 1) * length, :] = total.astype(bf16)


def combine(slots, rows, peer, apart=False, added=None, add=None):
    tables = [t[3] for t in slots]
    micro, length = len(tables), tables[0].shape[2]
    capacity, width = rows[0].shape[2:]
    work = micro * sum(a.shape[1] for a in rows) * capacity
    whole = pl.BlockSpec(memory_space=pltpu.VMEM)
    shapes = [(length, width)] * micro if apart else [(micro * length, width)]
    operands = [*tables, *rows] + ([] if add is None else [add])
    out = pl.pallas_call(
        functools.partial(combine_kernel, peer, len(rows), micro, added),
        in_specs=[whole] * len(operands),
        out_specs=[whole] * len(shapes),
        out_shape=[jax.ShapeDtypeStruct(shape, bf16) for shape in shapes],
        compiler_params=pltpu.CompilerParams(vmem_limit_bytes=VMEM),
        cost_estimate=pl.CostEstimate(
            flops=2 * work * length * width, bytes_accessed=3 * work * width, transcendentals=0
        ),
        name="combine",
    )(*operands)
    return out if apart else out[0]


GROUP = 4
HALF = HD // 2
SPAN = GROUP * HD
REPEAT = H // KVH
NGROUPS = KVH // GROUP


def query_order():
    return [
        (g * GROUP + n) * REPEAT + r
        for g in range(NGROUPS)
        for r in range(REPEAT)
        for n in range(GROUP)
    ]


def halves_order(heads_in_group):
    return [
        heads[n] * 2 + t for heads in heads_in_group for t in range(2) for n in range(GROUP)
    ]


def query_halves():
    order = query_order()
    return halves_order([order[i : i + GROUP] for i in range(0, H, GROUP)])


def key_halves():
    return halves_order([list(range(g * GROUP, (g + 1) * GROUP)) for g in range(NGROUPS)])


def take_rows(a, order, size):
    return jnp.concatenate([a[o * size : (o + 1) * size] for o in order], axis=0)


def put_rows(a, order, size):
    inverse = sorted(range(len(order)), key=lambda i: order[i])
    return take_rows(a, inverse, size)


def lay_out_columns(a):
    rows = a.shape[0]
    q = a[:, : H * HD].reshape(rows, NGROUPS, GROUP, REPEAT, 2, HALF)
    k = a[:, H * HD : (H + KVH) * HD].reshape(rows, NGROUPS, GROUP, 2, HALF)
    q = q.transpose(0, 1, 3, 4, 2, 5).reshape(rows, H * HD)
    k = k.transpose(0, 1, 3, 2, 4).reshape(rows, KVH * HD)
    return jnp.concatenate([q, k, a[:, (H + KVH) * HD :]], axis=1)


def rope(a, cos, sin, sign):
    out = []
    for at in range(0, a.shape[1], SPAN):
        lead, trail = a[:, at : at + LANES], a[:, at + LANES : at + SPAN]
        out.append(lead * cos - sign * (trail * sin))
        out.append(trail * cos + sign * (lead * sin))
    return jnp.concatenate(out, axis=1)


def lanes_like(a):
    return lax.broadcasted_iota(jnp.int32, a.shape, 1)


def key_of(a, n):
    return jnp.where((lanes_like(a) % LANES) // HALF == n, a, jnp.zeros_like(a))


def value_of(a, n):
    return jnp.where(lanes_like(a) // HD == n, a, jnp.zeros_like(a))


def unpack_kernel(peers, me_ref, *refs):
    own, near, far = refs[0], refs[1:peers], refs[peers : 2 * peers - 1]
    qkv_ref, exit_ref, other_ref = refs[2 * peers - 1 :]
    width = qkv_ref.shape[0]
    shards = own.shape[0]
    ru, half = width // shards, width // 2
    a, b = qkv_ref.shape[1] // LANES // peers, exit_ref.shape[1] // LANES // peers
    c = other_ref.shape[0] // peers
    order = [n * REPEAT + r for r in range(REPEAT) for n in range(GROUP)]

    def place(part, h, q):
        def block(j):
            return part[:, j * ru : (j + 1) * ru, :].reshape(half, LANES)

        rows = pl.ds(pl.multiple_of(h * half, half), half)
        for j in range(a):
            columns = pl.ds(pl.multiple_of((q * a + j) * LANES, LANES), LANES)
            qkv_ref[rows, columns] = block(j)
        for j in range(b):
            columns = pl.ds(pl.multiple_of((q * b + j) * LANES, LANES), LANES)
            exit_ref[rows, columns] = take_rows(block(a + j), order, HD)
        for j in range(c):
            other_ref[q * c + j, rows, :] = block(a + b + j)

    me, core = me_ref[0], me_ref[1]
    for h in range(2):
        place(own.at[h * shards // 2 : (h + 1) * shards // 2], h, me)
    for k in range(1, peers):
        place(near[k - 1], core, me ^ k)
        place(far[k - 1], 1 - core, me ^ k)


def unpack(me, own, near, far, width, qkv_width, others):
    whole = pl.BlockSpec(memory_space=pltpu.VMEM)
    packed = [own, *near, *far]
    return pl.pallas_call(
        functools.partial(unpack_kernel, len(near) + 1),
        in_specs=[pl.BlockSpec(memory_space=pltpu.SMEM)] + [whole] * len(packed),
        out_specs=[whole] * 3,
        out_shape=[
            jax.ShapeDtypeStruct((width, qkv_width), bf16),
            jax.ShapeDtypeStruct((width, width), bf16),
            jax.ShapeDtypeStruct((others, width, LANES), bf16),
        ],
        compiler_params=pltpu.CompilerParams(vmem_limit_bytes=VMEM),
        name="unpack",
    )(me, *packed)


def scale_rows(values):
    return lax.rsqrt(jnp.mean(values * values, axis=-1, keepdims=True) + eps_norm)


def attn_forward_kernel(
    me_ref, x_ref, chosen_ref, rank_ref, row_ref, col_ref, mask_ref, cos_ref, sin_ref, qkv_ref,
    exit_ref, oth_ref, kout_ref, vout_ref, rout_ref, gain_ref,
    res_ref, q_ref, k_ref, v_ref, lse_ref, att_ref, lora_ref, olora_ref, rlora_ref, gate_ref,
    *sent_refs,
):
    length, width = x_ref.shape
    qw, kw = H * HD, KVH * HD
    mask = mask_ref[0]
    cos, sin = cos_ref[...], sin_ref[...]
    hidden = x_ref[...].astype(f32)
    normed = (hidden * scale_rows(hidden) * gain_ref[0:1, :]).astype(bf16)
    lora = [(nn(normed, oth_ref[i]) * mask).astype(bf16) for i in range(3)]
    for i in range(3):
        lora_ref[:, i * LANES : (i + 1) * LANES] = lora[i]
    q_out = take_rows(oth_ref[3], query_halves(), HALF)
    k_out = take_rows(kout_ref[...], key_halves(), HALF)
    q = nn(normed, qkv_ref[:, :qw]) + nt(lora[0], q_out)
    q_ref[...] = (rope(q, cos, sin, 1.0) * HD ** (-0.5)).astype(bf16)
    k = nn(normed, qkv_ref[:, qw : qw + kw]) + nt(lora[1], k_out)
    k_ref[...] = rope(k, cos, sin, 1.0).astype(bf16)
    v_ref[...] = (nn(normed, qkv_ref[:, qw + kw :]) + nt(lora[2], vout_ref[...])).astype(bf16)
    shut = jnp.where(row_ref[0] <= col_ref[0], 0.0, -1e30)
    lane = lax.broadcasted_iota(jnp.int32, (length, LANES), 1)
    logs = jnp.zeros((length, LANES), f32)
    for g in range(NGROUPS):
        kg = k_ref[:, g * SPAN : (g + 1) * SPAN]
        vg = v_ref[:, g * SPAN : (g + 1) * SPAN]
        totals = [None] * REPEAT
        for n in range(GROUP):
            kn, vn = key_of(kg, n), value_of(vg, n)
            for r in range(REPEAT):
                at = g * REPEAT + r
                s = nt(q_ref[:, at * SPAN : (at + 1) * SPAN], kn) + shut
                peak = jnp.max(s, axis=-1, keepdims=True)
                p = jnp.exp(s - peak)
                total = jnp.sum(p, axis=-1, keepdims=True)
                logs = jnp.where(lane == at * GROUP + n, peak + jnp.log(total), logs)
                probs = (p * (1.0 / total)).astype(bf16)
                term = nn(probs, vn)
                totals[r] = term if n == 0 else totals[r] + term
        for r in range(REPEAT):
            at = g * REPEAT + r
            att_ref[:, at * SPAN : (at + 1) * SPAN] = totals[r].astype(bf16)
    lse_ref[...] = logs
    att = att_ref[...]
    merge_in = take_rows(oth_ref[5], query_order(), HD)
    out_lora = (nn(att, merge_in) * mask).astype(bf16)
    olora_ref[...] = out_lora
    residual = hidden + nn(att, exit_ref[...]) + nt(out_lora, oth_ref[6])
    res_ref[...] = residual
    moe = (residual * scale_rows(residual) * gain_ref[1:2, :]).astype(bf16)
    for ref in sent_refs:
        ref[:length] = moe
    route_lora = (nn(moe, oth_ref[7]) * mask).astype(bf16)
    rlora_ref[...] = route_lora
    logits = nn(moe, oth_ref[8]) + nn(route_lora, rout_ref[...])
    shown = jnp.where(chosen_ref[...] > 0, logits, -1e30)
    weight = jnp.where(
        chosen_ref[...] > 0, jnp.exp(shown - jnp.max(shown, axis=1, keepdims=True)), 0.0
    )
    gates = weight / jnp.sum(weight, axis=1, keepdims=True)
    gate_ref[0] = gates.T[: gate_ref.shape[1]]
    own = gate_ref.shape[1] // len(sent_refs)
    for k, ref in enumerate(sent_refs):
        group = pl.ds(pl.multiple_of((me_ref[0] ^ k) * own, own), own)
        value = jnp.concatenate(
            [rank_ref[0, group, :], *pieces_of(gate_ref[0, group, :])], axis=0
        )
        put_extra(ref, length, length, value)


def attn_forward(step, me, hidden, chosen, rank, rows, cols, mask, cos, sin, weights, peers):
    _, experts, length = rank.shape
    width = hidden.shape[1]

    def by_row(a):
        return pl.BlockSpec((length, a.shape[1]), lambda i: (step, 0))

    def by_step(a):
        return pl.BlockSpec((1,) + a.shape[1:], lambda i: (step,) + (0,) * (a.ndim - 1))

    def whole(a):
        return pl.BlockSpec(a.shape, lambda i: (0,) * a.ndim)

    qw, kw = H * HD, KVH * HD
    shapes = [
        ((length, width), f32), ((length, qw), bf16), ((length, kw), bf16), ((length, kw), bf16),
         ((length, LANES), f32), ((length, qw), bf16), ((length, 3 * LANES), bf16),
        ((length, LANES), bf16), ((length, LANES), bf16), ((1, experts, length), f32),
    ] + [((length + EXTRA, width), bf16)] * peers
    shapes = [jax.ShapeDtypeStruct(*shape) for shape in shapes]
    return pl.pallas_call(
        attn_forward_kernel,
        grid=(1,),
        in_specs=[pl.BlockSpec(memory_space=pltpu.SMEM), by_row(hidden), by_row(chosen)]
        + [by_step(a) for a in (rank, rows, cols, mask)]
        + [whole(a) for a in (cos, sin, *weights)],
        out_specs=[whole(a) for a in shapes],
        out_shape=shapes,
        compiler_params=pltpu.CompilerParams(vmem_limit_bytes=VMEM),
        cost_estimate=pl.CostEstimate(
            flops=2 * length * (5 * width * width + 4 * H * HD * length),
            bytes_accessed=20 * width * width,
            transcendentals=H * length * length,
        ),
        name="attention_forward",
    )(me, hidden, chosen, rank, rows, cols, mask, cos, sin, *weights)


def last_hits(rank_ref, count, capacity):
    return [hits_of(rank_ref[0, i : i + 1, :], capacity) for i in range(count)]


def attn_backward_kernel(
    peers, last, parts, older, me_ref, x_ref, cot_ref, row_ref, col_ref, mask_ref, cos_ref, sin_ref,
    qkv_ref, exit_ref, oth_ref, kout_ref, vout_ref, rout_ref, gain_ref,
    res_ref, q_ref, k_ref, v_ref, lse_ref, att_ref, lora_ref, olora_ref, rlora_ref, gate_ref, moe_ref,
    rank_ref, *refs,
):
    part_refs, tail_refs = refs[:parts], refs[parts : parts + peers]
    at = parts + peers
    old_grads = refs[at : at + older]
    out_ref, grad_ref, product_ref, dq_ref, dk_ref, dv_ref = refs[at + 2 * older :]
    length, width = x_ref.shape
    experts = gate_ref.shape[1]
    own = experts // peers
    capacity = (tail_refs[0].shape[0] - EXTRA) // last
    qw, kw = H * HD, KVH * HD
    mask = mask_ref[0]
    cos, sin = cos_ref[...], sin_ref[...]

    hits = last_hits(rank_ref, peers * last, capacity)
    hot = jnp.concatenate([jnp.where(h, 1.0, 0.0).astype(bf16) for h in hits], axis=0)
    tails = jnp.concatenate([ref[: last * capacity] for ref in tail_refs], axis=0)
    upstream = tn(hot, tails)
    for ref in part_refs:
        upstream = upstream + ref[...].astype(f32)
    for k in range(peers):
        group = pl.ds(pl.multiple_of((me_ref[0] ^ k) * own, own), own)
        value = get_extra(tail_refs[k], last * capacity, length)
        product_ref[group, :] = value[:own] + value[own : 2 * own] + value[2 * own : 3 * own]
    product = product_ref[...]
    gates = gate_ref[0]
    weighted = gates * product
    select = weighted - gates * jnp.sum(weighted, axis=0, keepdims=True)
    select = jnp.concatenate([select, jnp.zeros((LANES - experts, length), f32)], axis=0)
    logit_grad = select.T.astype(bf16)

    route_lora_grad = (nt(logit_grad, rout_ref[...]) * mask).astype(bf16)
    upstream = upstream + nt(logit_grad, oth_ref[8]) + nt(route_lora_grad, oth_ref[7])
    residual = res_ref[...]
    scale = scale_rows(residual)
    scaled = gain_ref[1:2, :] * upstream
    inner = jnp.sum(residual * scaled, axis=-1, keepdims=True) * (1.0 / width)
    res_grad = cot_ref[...].astype(f32) + scale * scaled - residual * (scale * scale * scale * inner)
    att_grad = res_grad.astype(bf16)
    merge_out = oth_ref[6]
    merge_in = take_rows(oth_ref[5], query_order(), HD)
    out_lora_grad = (nn(att_grad, merge_out) * mask).astype(bf16)
    head_grad = (nt(att_grad, exit_ref[...]) + nt(out_lora_grad, merge_in)).astype(bf16)

    shut = jnp.where(row_ref[0] <= col_ref[0], 0.0, -1e30)
    logs = lse_ref[...]
    for g in range(NGROUPS):
        kg = k_ref[:, g * SPAN : (g + 1) * SPAN]
        vg = v_ref[:, g * SPAN : (g + 1) * SPAN]
        dq = [None] * REPEAT
        qs = [q_ref[:, (g * REPEAT + r) * SPAN : (g * REPEAT + r + 1) * SPAN] for r in range(REPEAT)]
        dos = [
            head_grad[:, (g * REPEAT + r) * SPAN : (g * REPEAT + r + 1) * SPAN]
            for r in range(REPEAT)
        ]
        qts = [a.T for a in qs]
        dots = [a.T for a in dos]
        lead, trail, dvs = [], [], []
        for n in range(GROUP):
            kn, vn = key_of(kg, n), value_of(vg, n)
            dk, dv = None, None
            for r in range(REPEAT):
                at = (g * REPEAT + r) * GROUP + n
                s = nt(qs[r], kn) + (shut - logs[:, at : at + 1])
                p = jnp.exp(s)
                dp = nt(dos[r], vn)
                weight = p * dp
                ds = (weight - p * jnp.sum(weight, axis=-1, keepdims=True)).astype(bf16)
                term = nn(ds, kn)
                dq[r] = term if n == 0 else dq[r] + term
                qt = jnp.concatenate(
                    [
                        qts[r][n * HALF : (n + 1) * HALF],
                        qts[r][LANES + n * HALF : LANES + (n + 1) * HALF],
                    ],
                    axis=0,
                )
                term = nn(qt, ds)
                dk = term if r == 0 else dk + term
                term = nn(dots[r][n * HD : (n + 1) * HD], p.astype(bf16))
                dv = term if r == 0 else dv + term
            lead.append(dk[:HALF])
            trail.append(dk[HALF:])
            dvs.append(dv)
        for r in range(REPEAT):
            at = g * REPEAT + r
            back = rope(dq[r] * HD ** (-0.5), cos, sin, -1.0)
            dq_ref[:, at * SPAN : (at + 1) * SPAN] = back.astype(bf16)
        dk = jnp.concatenate(lead + trail, axis=0).T
        dk_ref[:, g * SPAN : (g + 1) * SPAN] = rope(dk, cos, sin, -1.0).astype(bf16)
        dv_ref[:, g * SPAN : (g + 1) * SPAN] = jnp.concatenate(dvs, axis=0).T.astype(bf16)

    dq, dk, dv = dq_ref[...], dk_ref[...], dv_ref[...]
    q_out = take_rows(oth_ref[3], query_halves(), HALF)
    k_out = take_rows(kout_ref[...], key_halves(), HALF)
    lora_grads = [
        (nn(dq, q_out) * mask).astype(bf16),
        (nn(dk, k_out) * mask).astype(bf16),
        (nn(dv, vout_ref[...]) * mask).astype(bf16),
    ]
    back = (
        nt(dq, qkv_ref[:, :qw]) + nt(dk, qkv_ref[:, qw : qw + kw]) + nt(dv, qkv_ref[:, qw + kw :])
    )
    for i in range(3):
        back = back + nt(lora_grads[i], oth_ref[i])
    hidden = x_ref[...].astype(f32)
    scale = scale_rows(hidden)
    normed = (hidden * scale * gain_ref[0:1, :]).astype(bf16)
    scaled = gain_ref[0:1, :] * back
    inner = jnp.sum(hidden * scaled, axis=-1, keepdims=True) * (1.0 / width)
    out_ref[...] = (
        res_grad + scale * scaled - hidden * (scale * scale * scale * inner)
    ).astype(bf16)

    lora = [lora_ref[:, i * LANES : (i + 1) * LANES] for i in range(3)]
    terms = (
        tn(jnp.concatenate(lora_grads, axis=1), normed),
        tn(lora[0], dq),
        tn(lora[1], dk),
        tn(lora[2], dv),
        tn(out_lora_grad, att_ref[...]),
        tn(olora_ref[...], att_grad),
        tn(route_lora_grad, moe_ref[...]),
        tn(rlora_ref[...], logit_grad),
    )
    ru = width // SHARDS

    def put(place, value):
        if older:
            value = value + old_grads[0][place].astype(f32)
        grad_ref[place] = value.astype(bf16)

    def put_columns(at, value):
        for s in range(SHARDS):
            put((s, slice(at, at + value.shape[0])), value[:, s * ru : (s + 1) * ru])

    def put_rows_at(at, value):
        size = value.shape[0] // SHARDS
        put((slice(None), slice(at, at + size)), value.reshape(SHARDS, size, LANES))

    at = 0
    sizes = attn_grad_rows(width)
    turned = {
        1: lambda a: put_rows(a.T, query_halves(), HALF),
        2: lambda a: put_rows(a.T, key_halves(), HALF),
        3: lambda a: a.T,
        4: lambda a: put_rows(a.T, query_order(), HD),
        7: lambda a: a,
    }
    for i, (size, term) in enumerate(zip(sizes, terms)):
        if i in turned:
            put_rows_at(at, turned[i](term))
        else:
            put_columns(at, term)
        at += size


def attn_grad_rows(width):
    ru, qs, ks = width // SHARDS, H * HD // SHARDS, KVH * HD // SHARDS
    return (3 * LANES, qs, ks, ks, qs, LANES, LANES, LANES // SHARDS)


def attn_backward(
    step, last, me, hidden, cotangent, rows, cols, mask, cos, sin, weights, saved, moe, rank, parts, tails, older
):
    length = rows.shape[2]
    width = hidden.shape[1]
    peers = len(tails)
    experts = saved[-1].shape[1]
    grads = jax.ShapeDtypeStruct((SHARDS, sum(attn_grad_rows(width)), LANES), bf16)

    def by_row(a):
        return pl.BlockSpec((length, a.shape[1]), lambda i: (step, 0))

    def by_step(a):
        return pl.BlockSpec((1,) + a.shape[1:], lambda i: (step,) + (0,) * (a.ndim - 1))

    def whole(a):
        return pl.BlockSpec(a.shape, lambda i: (0,) * a.ndim)

    qw, kw = H * HD, KVH * HD
    ahead = 8 + len(weights) + len(saved) + 2 + len(parts) + peers
    return pl.pallas_call(
        functools.partial(attn_backward_kernel, peers, last, len(parts), len(older) // 2),
        grid=(1,),
        in_specs=[pl.BlockSpec(memory_space=pltpu.SMEM), by_row(hidden), by_row(cotangent)]
        + [by_step(a) for a in (rows, cols, mask)]
        + [whole(a) for a in (cos, sin, *weights, *saved)]
        + [pl.BlockSpec((length, width), lambda i: (0, 0)), by_step(rank)]
        + [by_row(a) for a in parts]
        + [whole(a) for a in tails]
        + ([whole(older[0]), pl.BlockSpec(memory_space=pl.ANY)] if older else []),
        out_specs=[by_row(hidden), whole(grads)],
        out_shape=[jax.ShapeDtypeStruct(hidden.shape, bf16), grads],
        scratch_shapes=[
            pltpu.VMEM((experts, length), f32),
            pltpu.VMEM((length, qw), bf16),
            pltpu.VMEM((length, kw), bf16),
            pltpu.VMEM((length, kw), bf16),
        ],
        compiler_params=pltpu.CompilerParams(vmem_limit_bytes=VMEM),
        cost_estimate=pl.CostEstimate(
            flops=2 * length * (6 * width * width + 10 * H * HD * length),
            bytes_accessed=30 * width * width,
            transcendentals=H * length * length,
        ),
        input_output_aliases={ahead + 1: 0} if older else {},
        name="attention_backward",
    )(
        me, hidden, cotangent, rows, cols, mask, cos, sin, *weights, *saved, moe, rank, *parts, *tails, *older
    )


def mixture_kernel(peers, count, last, res_ref, rank_ref, *refs):
    parts, tails, out_ref = refs[:count], refs[count : count + peers], refs[-1]
    capacity, width = tails[0].shape[2:]
    hits = last_hits(rank_ref, peers * last, capacity)
    hot = jnp.concatenate([jnp.where(h, 1.0, 0.0).astype(bf16) for h in hits], axis=0)
    rows = jnp.concatenate([ref[0].reshape(last * capacity, width) for ref in tails], axis=0)
    total = tn(hot, rows)
    for ref in parts:
        total = total + ref[...].astype(f32)
    out_ref[...] = (res_ref[...] + total).astype(bf16)


def add_mixture(step, residual, rank, parts, tails, older):
    length = rank.shape[2]
    width = residual.shape[1]

    def by_row(a):
        return pl.BlockSpec((length, a.shape[1]), lambda i: (step, 0))

    def by_step(a):
        return pl.BlockSpec((1,) + a.shape[1:], lambda i: (step,) + (0,) * (a.ndim - 1))

    def whole(a):
        return pl.BlockSpec(a.shape, lambda i: (0,) * a.ndim)

    return pl.pallas_call(
        functools.partial(mixture_kernel, len(tails), len(parts), tails[0].shape[1]),
        grid=(1,),
        in_specs=[whole(residual), by_step(rank)]
        + [by_row(a) for a in parts]
        + [whole(a) for a in tails]
        + [pl.BlockSpec(memory_space=pl.ANY)] * len(older),
        out_specs=by_row(parts[0]),
        out_shape=jax.ShapeDtypeStruct(parts[0].shape, bf16),
        compiler_params=pltpu.CompilerParams(vmem_limit_bytes=VMEM),
        cost_estimate=pl.CostEstimate(
            flops=2 * length * 1000 * width, bytes_accessed=20 * length * width, transcendentals=0
        ),
        input_output_aliases={2 + len(parts) + len(tails): 0} if older else {},
        name="mixture",
    )(residual, rank, *parts, *tails, *older)


def finish_experts_kernel(chunks, *refs):
    parts = refs[:chunks]
    reduce_ref, expand_ref, deep_ref, last_ref = refs[chunks:]
    wide = reduce_ref.shape[2]
    rd = deep_ref.shape[1]
    e = 0
    for ref in parts:
        for i in range(ref.shape[0]):
            g = ref[i].astype(f32)
            reduce_ref[e] = g[:wide].T
            for j in range(2):
                expand_ref[e, j] = g[wide + j * rd : wide + (j + 1) * rd].T
            deep_ref[e] = g[wide + 2 * rd : wide + 3 * rd]
            last_ref[e] = g[wide + 3 * rd :]
            e += 1


def finish_experts(parts, width, inner_width):
    count = sum(a.shape[0] for a in parts)
    ru, rd = width // SHARDS, inner_width // SHARDS
    whole = pl.BlockSpec(memory_space=pltpu.VMEM)
    return pl.pallas_call(
        functools.partial(finish_experts_kernel, len(parts)),
        in_specs=[whole] * len(parts),
        out_specs=[whole] * 4,
        out_shape=[
            jax.ShapeDtypeStruct((count, ru, 2 * LANES), f32),
            jax.ShapeDtypeStruct((count, 2, LANES, rd), f32),
            jax.ShapeDtypeStruct((count, rd, LANES), f32),
            jax.ShapeDtypeStruct((count, LANES, ru), f32),
        ],
        compiler_params=pltpu.CompilerParams(vmem_limit_bytes=VMEM),
        name="finish_experts",
    )(*parts)


def finish_attention_kernel(sizes, peers, *refs):
    parts, outs = refs[:peers], refs[peers:]
    total = parts[0][...].astype(f32)
    for ref in parts[1:]:
        total = total + ref[...].astype(f32)
    at = 0
    for i, (size, ref) in enumerate(zip(sizes, outs)):
        piece = total[at : at + size]
        at += size
        if i in (0, 1, 2, 3, 6):
            ref[...] = piece.T
        else:
            ref[...] = piece[:, : ref.shape[1]]


def finish_attention(parts, sizes, experts):
    shapes = [
        (LANES, sizes[0]), (LANES, sizes[1]), (LANES, sizes[2]), (LANES, sizes[3]),
        (sizes[4], LANES), (sizes[5], LANES), (LANES, sizes[6]), (sizes[7], experts),
    ]
    whole = pl.BlockSpec(memory_space=pltpu.VMEM)
    return pl.pallas_call(
        functools.partial(finish_attention_kernel, sizes, len(parts)),
        in_specs=[whole] * len(parts),
        out_specs=[whole] * len(shapes),
        out_shape=[jax.ShapeDtypeStruct(s, f32) for s in shapes],
        compiler_params=pltpu.CompilerParams(vmem_limit_bytes=VMEM),
        name="finish_attention",
    )(*parts)


def exchange(a, k):
    if k == 0:
        return a
    size = lax.axis_size("dp")
    return lax.ppermute(a, "dp", [(i, i ^ k) for i in range(size)])


def local(
    layer_entering_state,
    exit_cotangent,
    attend_norm_scaling,
    branch_norm_scaling,
    triple_coefficients,
    attend_exit_coefficients,
    dispatch_coefficients,
    branch_widen_coefficients,
    branch_contract_coefficients,
    triple_plugin_source,
    asking_plugin_target,
    lookup_plugin_target,
    content_plugin_target,
    merge_plugin_source,
    merge_plugin_target,
    dispatch_plugin_source,
    dispatch_plugin_target,
    branch_plugin_source,
    branch_plugin_target,
    contract_plugin_source,
    contract_plugin_target,
    branch_choice_labels,
    plugin_choice_per_text,
    section_labels,
):
    dp_count = lax.axis_size("dp")
    shard_count = lax.axis_size("fsdp")
    dp_rank = lax.axis_index("dp")
    micro_count, seq_len = section_labels.shape
    local_experts = branch_widen_coefficients.shape[0]
    expert_count = local_experts * dp_count
    top_count = branch_choice_labels.shape[1]
    most = seq_len * top_count * 9 // (expert_count * 8)
    capacity = -(-most // 16) * 16
    model_width = layer_entering_state.shape[1]
    inner_width = contract_plugin_source.shape[1] * shard_count
    adapter_width = PLUGIN_CHOICES * REDUCED_DIM
    cos_table, sin_table = rotation(seq_len)
    column_holder = jnp.arange(adapter_width, dtype=jnp.int32) // REDUCED_DIM
    peers = range(dp_count)
    last = CHUNKS[-1]
    core = lax.axis_index("fsdp") % 2
    me = jnp.stack([dp_rank, core]).astype(jnp.int32)
    cot_rows = [exit_cotangent[m * seq_len : (m + 1) * seq_len] for m in range(micro_count)]
    cot_from = [[exchange(cot_rows[0], k)] for k in peers]

    labels = branch_choice_labels.reshape(micro_count, seq_len, top_count)
    lane_range = jnp.arange(LANES, dtype=jnp.int32)
    chosen = jnp.any(labels[..., None] == lane_range, axis=2)
    before = jnp.tril(jnp.ones((seq_len, seq_len), bf16), -1)
    chosen_e = chosen[..., :expert_count]
    rank = jnp.einsum("mse,ts->met", chosen_e.astype(bf16), before, preferred_element_type=f32)
    rank = jnp.where(jnp.swapaxes(chosen_e, 1, 2), rank, -1.0)
    chosen = chosen.astype(f32).reshape(micro_count * seq_len, LANES)

    def of_group(a, k):
        return lax.dynamic_slice_in_dim(a, (dp_rank ^ k) * local_experts, local_experts, 1)

    rank_last = jnp.concatenate([of_group(rank, k)[:, -last:] for k in peers], axis=1)
    adapters = [plugin_choice_per_text[dp_rank ^ k] for k in peers]
    masks = jnp.stack(
        [(column_holder[None, :] == own[:, None]).astype(f32) for own in adapters], axis=1
    )
    own_mask = masks[:, :1]
    section_rows = section_labels[:, None, :]
    section_cols = section_labels[:, :, None]

    ru = model_width // shard_count
    kv_cols = lookup_plugin_target.shape[1]
    route_rows = dispatch_plugin_target.shape[0]
    small = jnp.concatenate(
        [
            pad_lanes(dispatch_plugin_target),
            pad_lanes(attend_norm_scaling[None]),
            pad_lanes(branch_norm_scaling[None]),
        ],
        axis=0,
    )
    small = jnp.pad(small, ((0, ru - small.shape[0]), (0, 0)))
    others = jnp.concatenate(
        [
            columns_to_rows(triple_plugin_source),
            asking_plugin_target.T,
            lookup_plugin_target.T,
            content_plugin_target.T,
            merge_plugin_source,
            merge_plugin_target.T,
            dispatch_plugin_source,
            pad_lanes(dispatch_coefficients),
            small,
        ],
        axis=0,
    )
    other_count = others.shape[0] // ru
    other_slots = -(-other_count // dp_count) * dp_count
    others = jnp.pad(others, ((0, (other_slots - other_count) * ru), (0, 0)))

    def own_part(a, axis):
        size = a.shape[axis] // dp_count
        return lax.dynamic_slice_in_dim(a, dp_rank * size, size, axis)

    part = jnp.concatenate(
        [
            columns_to_rows(own_part(lay_out_columns(triple_coefficients), 1)),
            columns_to_rows(own_part(attend_exit_coefficients, 1)),
            own_part(others, 0),
        ],
        axis=0,
    )
    part_all = lax.all_gather(part, "fsdp", axis=0)
    (part_all, cot_from, rank, chosen, masks, own_mask, section_cols, cos_table, sin_table) = (
        lax.optimization_barrier(
            (part_all, cot_from, rank, chosen, masks, own_mask, section_cols, cos_table, sin_table)
        )
    )
    mine = lax.dynamic_slice_in_dim(part_all, core * (shard_count // 2), shard_count // 2, 0)
    near = [exchange(mine, k) for k in peers[1:]]
    pairs = [(i, i ^ 1) for i in range(shard_count)]
    far = [lax.ppermute(a, "fsdp", pairs) for a in near]

    chunk_weights = []
    first = 0
    before_it = part
    for size in CHUNKS:
        here = slice(first, first + size)
        shards = (
            branch_widen_coefficients[here],
            branch_contract_coefficients[here],
            branch_plugin_source[here],
            branch_plugin_target[here],
            contract_plugin_source[here],
            contract_plugin_target[here],
        )
        if first:
            shards, cot_from = lax.optimization_barrier((shards, cot_from))
        shards, before_it = lax.optimization_barrier((shards, before_it))
        before_it = pack_experts(*shards)
        gathered = lax.all_gather(before_it, "fsdp", axis=0)
        chunk_weights.append(regroup(gathered, model_width, inner_width))
        first += size

    later, near = lax.optimization_barrier((cot_rows[1:], near))
    for k in peers:
        cot_from[k] += [exchange(a, k) for a in later]

    qkv, exit_full, other_full = unpack(
        me, part_all, near, far, model_width, triple_coefficients.shape[1], other_slots
    )
    kv_out = other_full[4].reshape(shard_count, 2, kv_cols, LANES)
    k_out = kv_out[:, 0].reshape(-1, LANES)
    v_out = kv_out[:, 1].reshape(-1, LANES)
    small_full = other_full[9].reshape(shard_count, ru, LANES)
    route_out = small_full[:, :route_rows].reshape(adapter_width, LANES)
    gains = jnp.stack(
        [small_full[:, route_rows + i, :ru].reshape(model_width) for i in range(2)]
    ).astype(f32)
    weights = (qkv, exit_full, other_full, k_out, v_out, route_out, gains)

    micro = range(micro_count)
    saved, sent, slots = [], [], []
    me_then = me
    for m in micro:
        if m > 0:
            me_then, sent[-1] = lax.optimization_barrier((me_then, sent[-1]))
        out = attn_forward(
            m, me_then, layer_entering_state, chosen, rank, section_rows, section_cols, own_mask,
            cos_table, sin_table, weights, dp_count,
        )
        saved.append(out[:-dp_count])
        sent.append(list(out[-dp_count:]))
    first_rows, cot_from = lax.optimization_barrier((sent[0], cot_from))
    sent[0] = first_rows
    rows_from = None
    for m in micro:
        if m > 0:
            sent[m], rows_from = lax.optimization_barrier((sent[m], rows_from))
        rows_from = [exchange(sent[m][k], k) for k in peers]
        cots = [cot_from[k][m] for k in peers]
        slots.append(dispatch(rows_from, cots, local_experts, capacity))

    n = dp_count
    head = CHUNKS[0]
    outs, first, grads, products = [], 0, None, None
    for size, chunk in zip(CHUNKS[:-1], chunk_weights):
        at = first if first < head else first - head
        count = head if first < head else local_experts - head
        outs.append(
            expert_chunk(
                slots, chunk, masks, first, inner_width, at, count, grads, products, False, False
            )
        )
        grads, products = outs[-1][2 * n], list(outs[-1][2 * n + 1 :])
        if first == 0:
            head_grads, grads = grads, None
        first += size
    if shard_count == SHARDS:
        head_sum = lax.psum_scatter(head_grads, "fsdp", scatter_dimension=0, tiled=False)
    else:
        head_sum = head_grads

    def rows_of(place):
        return [o[place] for o in outs]

    far_backs = combine(slots, rows_of(n + 3), 3, apart=True)
    passed = [exchange(far_backs[0], 1), exchange(far_backs[1], 2)]
    far_mixes = combine(slots, rows_of(3), 3, apart=True)
    far_mixes, passed = lax.optimization_barrier((far_mixes, passed))
    backs = {
        1: combine(slots, rows_of(n + 1), 1, added=1, add=passed[1]),
        2: combine(slots, rows_of(n + 2), 2, added=0, add=passed[0]),
    }
    passed_mixes = [exchange(far_mixes[0], 1), exchange(far_mixes[1], 2)]
    backs[0] = combine(slots, rows_of(n), 0)
    back_home = [backs[0], exchange(backs[1], 1), exchange(backs[2], 2)]
    mixes = {
        0: combine(slots, rows_of(0), 0),
        1: combine(slots, rows_of(1), 1, added=1, add=passed_mixes[1]),
        2: combine(slots, rows_of(2), 2, added=0, add=passed_mixes[0]),
    }
    chunk, _ = lax.optimization_barrier((chunk_weights[-1], (backs, mixes)))
    tails = []
    for m in micro:
        if m == micro_count - 1:
            chunk, back_home = lax.optimization_barrier((chunk, back_home))
        out = expert_chunk(
            [slots[m]], chunk, masks[m : m + 1], first, inner_width, first - head,
            local_experts - head, grads, [products[m]], m > 0, True,
        )
        grads = out[2 * n]
        tails.append(out)
    back_last = []
    for m in micro:
        tail = list(tails[m][n : 2 * n])
        if m == 0:
            tail, back_home = lax.optimization_barrier((tail, back_home))
        else:
            tail, back_last[-1] = lax.optimization_barrier((tail, back_last[-1]))
        back_last.append([exchange(tail[k], k) for k in peers])
    grads, back_last[0] = lax.optimization_barrier((grads, back_last[0]))
    if shard_count == SHARDS:
        tail_sum = lax.psum_scatter(grads, "fsdp", scatter_dimension=0, tiled=False)
    else:
        tail_sum = grads
    older = []
    for m in micro:
        if m == micro_count - 1:
            mixes, mix_tails, back_last[m], head_sum, older = lax.optimization_barrier(
                (mixes, [list(t[:n]) for t in tails], back_last[m], head_sum, older)
            )
        grad_input, attn_grads = attn_backward(
            m, last, me, layer_entering_state, exit_cotangent, section_rows, section_cols, own_mask,
            cos_table, sin_table, weights, saved[m], sent[m][0], rank_last, back_home, back_last[m],
            older,
        )
        older = [attn_grads, grad_input]
    mix_home = [mixes[0], exchange(mixes[1], 1), exchange(mixes[2], 2)]
    mix_last = [[exchange(t[k], k) for k in peers] for t in mix_tails]
    attn_grads, mix_home, tail_sum = lax.optimization_barrier((attn_grads, mix_home, tail_sum))
    block_out = []
    for m in micro:
        block_out = [add_mixture(m, saved[m][0], rank_last, mix_home, mix_last[m], block_out)]

    sizes = attn_grad_rows(model_width)
    if shard_count == SHARDS:
        expert_out = finish_experts([head_sum, tail_sum], model_width, inner_width)
        own_sum = lax.psum_scatter(attn_grads, "fsdp", scatter_dimension=0, tiled=False)
        attn_out = finish_attention([exchange(own_sum, k) for k in peers], sizes, expert_count)
    else:
        expert_out = scatter_experts([head_sum, tail_sum], inner_width)
        attn_out = scatter_attention(attn_grads, sizes, expert_count)
    return (*block_out, grad_input, *attn_out, *expert_out)


def scatter_experts(parts, inner_width):
    g = jnp.concatenate(parts, axis=1).astype(f32)
    count, rd, wide = g.shape[1], inner_width // SHARDS, 2 * LANES
    cuts = [wide + i * rd for i in range(4)]

    def rows_joined(a):
        return jnp.swapaxes(a, 0, 1).reshape(a.shape[1], -1, LANES)

    reduce = g[:, :, :wide].transpose(1, 0, 3, 2).reshape(count, -1, wide)
    expand = jnp.stack(
        [jnp.swapaxes(rows_joined(g[:, :, cuts[i] : cuts[i + 1]]), 1, 2) for i in range(2)],
        axis=1,
    )
    deep = rows_joined(g[:, :, cuts[2] : cuts[3]])
    last = g[:, :, cuts[3] :].transpose(1, 2, 0, 3).reshape(count, LANES, -1)
    return (
        lax.psum_scatter(reduce, "fsdp", scatter_dimension=1, tiled=True),
        lax.psum_scatter(expand, "fsdp", scatter_dimension=3, tiled=True),
        lax.psum_scatter(deep, "fsdp", scatter_dimension=1, tiled=True),
        lax.psum_scatter(last, "fsdp", scatter_dimension=2, tiled=True),
    )


def scatter_attention(packed, sizes, experts):
    pieces, at = [], 0
    for size in sizes:
        pieces.append(packed[:, at : at + size].astype(f32))
        at += size

    def by_rows(a):
        return a.reshape(-1, LANES)

    def by_columns(a):
        return jnp.swapaxes(a, 0, 1).reshape(a.shape[1], -1)

    full = (
        (by_columns(pieces[0]).T, 0),
        (by_rows(pieces[1]).T, 1),
        (by_rows(pieces[2]).T, 1),
        (by_rows(pieces[3]).T, 1),
        (by_rows(pieces[4]), 0),
        (by_columns(pieces[5]), 1),
        (by_columns(pieces[6]).T, 0),
        (by_rows(pieces[7])[:, :experts], 0),
    )
    return [
        lax.psum(lax.psum_scatter(a, "fsdp", scatter_dimension=d, tiled=True), "dp")
        for a, d in full
    ]


def solution(mesh):
    placed = (
        P(("dp", "fsdp"), None),
        P(("dp", "fsdp"), None),
        P("fsdp"),
        P("fsdp"),
        P("fsdp", None),
        P("fsdp", None),
        P("fsdp", None),
        P("dp", "fsdp", None),
        P("dp", "fsdp", None),
        P("fsdp", None),
        P(None, "fsdp"),
        P(None, "fsdp"),
        P(None, "fsdp"),
        P("fsdp", None),
        P(None, "fsdp"),
        P("fsdp", None),
        P("fsdp", None),
        P("dp", "fsdp", None),
        P("dp", None, None, "fsdp"),
        P("dp", "fsdp", None),
        P("dp", None, "fsdp"),
        P(("dp", "fsdp"), None),
        P(None, "fsdp"),
        P(("dp", "fsdp"), None),
    )
    return jax.shard_map(
        local,
        mesh=mesh,
        in_specs=placed,
        out_specs=(
            P(("dp", "fsdp"), None),
            P(("dp", "fsdp"), None),
            P("fsdp", None),
            P(None, "fsdp"),
            P(None, "fsdp"),
            P(None, "fsdp"),
            P("fsdp", None),
            P(None, "fsdp"),
            P("fsdp", None),
            P("fsdp", None),
            P("dp", "fsdp", None),
            P("dp", None, None, "fsdp"),
            P("dp", "fsdp", None),
            P("dp", None, "fsdp"),
        ),
        check_vma=False,
    )
```

time: 803 us -> 574 us (0.71)
  waiting for transfers between devices: 323 us -> 154 us
  Pallas kernels: 182 us -> 295 us
  matrix products: 102 us -> 1.08 us
  local copies, waits for them, and re-layouts: 90.9 us -> 39.5 us
  other arithmetic: 48.7 us -> 9.14 us
  starting transfers between devices: 34.7 us -> 53.5 us
    pallas_call x16 -> x23, Pallas kernels: 182 us -> 295 us  [the longest x4 119 us: expert_chunk(): pl.pallas_call(functools.partial(expert_kernel, first, micro, len(held),...]
    dot_general x73 -> x1, matrix products: 102 us -> 1.08 us  [local(): jnp.einsum('mse,ts->met', chosen_e.astype(bf16), before, preferred_elemen...]
    all_gather x5 -> x4, waiting for transfers between devices: 92.3 us -> 0.02 us  [the longest x3 0.02 us: local(): gathered = lax.all_gather(before_it, 'fsdp', axis=0)]
    ppermute x24 -> x38, waiting for transfers between devices: 213 us -> 136 us  [exchange(): return lax.ppermute(a, 'dp', [(i, i ^ k) for i in range(size)])]
    convert_element_type x7 -> x2, other arithmetic: 24.6 us -> 1.39 us  [the longest x1 0.77 us: local(): chosen = chosen.astype(f32).reshape(micro_count * seq_len, LANES)]
    unnamed x436 -> x141, local copies, waits for them, and re-layouts: 36 us -> 15.5 us
    ppermute x24 -> x38, starting transfers between devices: 34.1 us -> 52 us  [exchange(): return lax.ppermute(a, 'dp', [(i, i ^ k) for i in range(size)])]
    slice x26 -> x21, local copies, waits for them, and re-layouts: 25.5 us -> 10.5 us  [the longest x3 1.71 us: local(): branch_plugin_source[here]]
  transfers between devices with their start and end apart: 34 -> 48, of which waited for: 13 -> 16; matrix products, arithmetic and copies ran while one was open for 26% -> 6% of each run, Pallas kernels for 23% -> 52%
where the time goes in v2:
time: 574 us; the launch traced here: 568 us
  Pallas kernels  295 us (51%)
  waiting for transfers between devices  154 us (27%)
  starting transfers between devices  53.5 us (9%)
  local copies, waits for them, and re-layouts  39.5 us (7%)
  between operations  15.8 us (3%)
  other arithmetic  9.14 us (2%)
    ppermute x38, waiting for transfers between devices, exchange(): return lax.ppermute(a, 'dp', [(i, i ^ k) for i in range(size)])  136 us
    pallas_call x4, Pallas kernels, expert_chunk(): pl.pallas_call(functools.partial(expert_kernel, first, micro, len(held),...  119 us
    pallas_call x2, Pallas kernels, attn_backward(): pl.pallas_call(functools.partial(attn_backward_kernel, peers, last, len(p...  52.7 us
    ppermute x38, starting transfers between devices, exchange(): return lax.ppermute(a, 'dp', [(i, i ^ k) for i in range(size)])  52 us
    pallas_call x2, Pallas kernels, attn_forward(): pl.pallas_call(attn_forward_kernel, grid=(1,), in_specs=[pl.BlockSpec(mem...  37.2 us
    pallas_call x8, Pallas kernels, combine(): pl.pallas_call(functools.partial(combine_kernel, peer, len(rows), micro,...  35.6 us
    pallas_call x2, Pallas kernels, dispatch(): pl.pallas_call(functools.partial(dispatch_kernel, peers, capacity), grid=...  27 us
    reduce_scatter x1, waiting for transfers between devices, local(): lax.psum_scatter(attn_grads, 'fsdp', scatter_dimension=0, tiled=False)  18.4 us
  transfers between devices with their start and end apart: 48, of which 16 were waited for; matrix products, arithmetic and copies ran while one was open for 6% of the time, Pallas kernels for 52%

profile of v2, /device:TPU:0, one launch (start us, length us, event | category | flops | bytes accessed | tf_op | source)
XLA Modules:
  0.0 568.5 jit_solution(14826069657676190251)
XLA Ops:
  41.5 17.5 %collective-permute-done.1.refs_6_ = bf16[384,1024]{1,0:T(8,128)(2,1)} collective-permute-done((bf16[384,1024]{1,0:T(8,128)(2,1)}, bf16[384,1024]{1,0:T(8,128)(2,1)}, u32[]{:S(2)}, u32[]{:S(2)}) %collective-permute-start.1) | collective-permute-done | bytes 786464 | tf_op jit(solution)/shard_map/ppermute | solution.py:980
  69.4 25.4 %collective-permute-done.3.refs_1_ = bf16[4,1152,128]{2,1,0:T(8,128)(2,1)S(1)} collective-permute-done((bf16[4,1152,128]{2,1,0:T(8,128)(2,1)S(1)}, bf16[4,1152,128]{2,1,0:T(8,128)(2,1)S(1)}, u32[]{:S(2)}, u32[]{:S(2)}) %collective-permute-start.3) | collective-permute-done | bytes 1179680 | tf_op jit(solution)/shard_map/ppermute | solution.py:980
  94.8 24.2 %collective-permute-done.4.refs_2_ = bf16[4,1152,128]{2,1,0:T(8,128)(2,1)S(1)} collective-permute-done((bf16[4,1152,128]{2,1,0:T(8,128)(2,1)S(1)}, bf16[4,1152,128]{2,1,0:T(8,128)(2,1)S(1)}, u32[]{:S(2)}, u32[]{:S(2)}) %collective-permute-start.4) | collective-permute-done | bytes 1179680 | tf_op jit(solution)/shard_map/ppermute | solution.py:980
  128.9 9.5 %unpack.1 = (bf16[1024,2048]{1,0:T(8,128)(2,1)}, bf16[1024,1024]{1,0:T(8,128)(2,1)}, bf16[12,1024,128]{2,1,0:T(8,128)(2,1)}) custom-call(s32[2]{0:T(128)} %pad_add_fusion.me_ref, bf16[8,1152,128]{2,1,0:T(8,128)(2,1)} %bitcast.150, bf16[4,1152,128]{2,1,0:T(8,128)(2,1)} %copy-done.13, bf16[4,1152,128]{2,1,0:T(8,128)(2,1)} %copy-done.14, ...), custom_call_target="tpu_custom_call" | custom-call | tf_op jit(solution)/shard_map/unpack/pallas_call | solution.py:517
  141.5 18.8 %attention_forward.2 = (f32[384,1024]{1,0:T(8,128)}, bf16[384,1024]{1,0:T(8,128)(2,1)}, bf16[384,512]{1,0:T(8,128)(2,1)}, bf16[384,512]{1,0:T(8,128)(2,1)}, f32[...) custom-call(s32[2]{0:T(128)} %pad_add_fusion.me_ref, ...), custom_call_target="tpu_custom_call" | custom-call | flops 5234491392 | bytes 20971520 | tf_op jit(solution)/shard_map/attention_forward/pallas_call | solution.py:627
  166.7 18.4 %attention_forward.3 = (f32[384,1024]{1,0:T(8,128)}, bf16[384,1024]{1,0:T(8,128)(2,1)}, bf16[384,512]{1,0:T(8,128)(2,1)}, bf16[384,512]{1,0:T(8,128)(2,1)}, f32[...) custom-call(s32[2]{0:T(128)} %pad_add_fusion.me_ref, ...), custom_call_target="tpu_custom_call" | custom-call | flops 5234491392 | bytes 20971520 | tf_op jit(solution)/shard_map/attention_forward/pallas_call | solution.py:627
  185.2 15.0 %collective-permute-done.13.refs_2_ = bf16[400,1024]{1,0:T(8,128)(2,1)S(1)} collective-permute-done((bf16[400,1024]{1,0:T(8,128)(2,1)}, bf16[400,1024]{1,0:T(8,128)(2,1)S(1)}, u32[]{:S(2)}, u32[]{:S(2)}) %collective-permute-start.13) | collective-permute-done | bytes 819232 | tf_op jit(solution)/shard_map/ppermute | solution.py:980
  203.7 13.6 %dispatch.2 = (bf16[4,8,112,1024]{3,2,1,0:T(8,128)(2,1)}, bf16[4,8,112,1024]{3,2,1,0:T(8,128)(2,1)}, f32[4,8,112,128]{3,2,1,0:T(8,128)}, f32[4,8,384]{2,1,0:T(8,128)}) custom-call(bf16[400,1024]{1,0:T(8,128)(2,1)} %get-tuple-element.289.refs_0_.moe_ref, bf16[400,1024]{1,0:T(8,128)(2,1)} %copy-done.44, bf16[400,1024]{1,0:T(8,128)(2,1)} %copy-done.45, ...), custom_call_target="tpu_custom_call" | custom-call | flops 5637144576 | bytes 29360128 | tf_op jit(solution)/shard_map/dispatch/pallas_call | solution.py:153
  221.6 16.0 %collective-permute-done.16.refs_2_ = bf16[400,1024]{1,0:T(8,128)(2,1)S(1)} collective-permute-done((bf16[400,1024]{1,0:T(8,128)(2,1)}, bf16[400,1024]{1,0:T(8,128)(2,1)S(1)}, u32[]{:S(2)}, u32[]{:S(2)}) %collective-permute-start.16) | collective-permute-done | bytes 819232 | tf_op jit(solution)/shard_map/ppermute | solution.py:980
  238.5 13.5 %dispatch.3 = (bf16[4,8,112,1024]{3,2,1,0:T(8,128)(2,1)}, bf16[4,8,112,1024]{3,2,1,0:T(8,128)(2,1)}, f32[4,8,112,128]{3,2,1,0:T(8,128)}, f32[4,8,384]{2,1,0:T(8,128)}) custom-call(bf16[400,1024]{1,0:T(8,128)(2,1)} %get-tuple-element.293.refs_0_.moe_ref, bf16[400,1024]{1,0:T(8,128)(2,1)} %copy-done.47, bf16[400,1024]{1,0:T(8,128)(2,1)} %copy-done.48, ...), custom_call_target="tpu_custom_call" | custom-call | flops 5637144576 | bytes 29360128 | tf_op jit(solution)/shard_map/dispatch/pallas_call | solution.py:153
  252.6 53.1 %experts.4 = (bf16[2,4,112,1024]{3,2,1,0:T(8,128)(2,1)}, bf16[2,4,112,1024]{3,2,1,0:T(8,128)(2,1)}, bf16[2,4,112,1024]{3,2,1,0:T(8,128)(2,1)}, bf16[2,4,112,1024...) custom-call(f32[4,8,384]{2,1,0:T(8,128)} %get-tuple-element.298.refs, ...), custom_call_target="tpu_custom_call" | custom-call | flops 35840000000 | bytes 81264640 | tf_op jit(solution)/shard_map/experts/pallas_call | solution.py:324
  305.7 29.7 %experts.5 = (bf16[2,2,112,1024]{3,2,1,0:T(8,128)(2,1)}, bf16[2,2,112,1024]{3,2,1,0:T(8,128)(2,1)}, bf16[2,2,112,1024]{3,2,1,0:T(8,128)(2,1)}, bf16[2,2,112,1024...) custom-call(f32[4,8,384]{2,1,0:T(8,128)} %get-tuple-element.298.refs, ...), custom_call_target="tpu_custom_call" | custom-call | flops 17920000000 | bytes 40632320 | tf_op jit(solution)/shard_map/experts/pallas_call | solution.py:324
  344.7 10.3 %collective-permute-done.18.refs_4_ = bf16[384,1024]{1,0:T(8,128)(2,1)S(1)} collective-permute-done((bf16[384,1024]{1,0:T(8,128)(2,1)}, bf16[384,1024]{1,0:T(8,128)(2,1)S(1)}, u32[]{:S(2)}, u32[]{:S(2)}) %collective-permute-start.18) | collective-permute-done | bytes 786464 | tf_op jit(solution)/shard_map/ppermute | solution.py:980
  358.1 4.7 combine.12
  383.3 4.6 combine.14
  388.0 17.8 %experts.6 = (bf16[1,2,112,1024]{3,2,1,0:T(8,128)(2,1)}, bf16[1,2,112,1024]{3,2,1,0:T(8,128)(2,1)}, bf16[1,2,112,1024]{3,2,1,0:T(8,128)(2,1)}, bf16[1,2,112,1024...) custom-call(f32[4,8,384]{2,1,0:T(8,128)} %get-tuple-element.298.refs, ...), custom_call_target="tpu_custom_call", output_to_operand_aliasing={{8}: (7, {})} | custom-call | flops 8960000000 | bytes 33292288 | tf_op jit(solution)/shard_map/experts/pallas_call | solution.py:324
  411.0 17.9 %experts.7 = (bf16[1,2,112,1024]{3,2,1,0:T(8,128)(2,1)}, bf16[1,2,112,1024]{3,2,1,0:T(8,128)(2,1)}, bf16[1,2,112,1024]{3,2,1,0:T(8,128)(2,1)}, bf16[1,2,112,1024...) custom-call(f32[4,8,384]{2,1,0:T(8,128)} %get-tuple-element.339.refs, ...), custom_call_target="tpu_custom_call", output_to_operand_aliasing={{8}: (7, {})} | custom-call | flops 8960000000 | bytes 33292288 | tf_op jit(solution)/shard_map/experts/pallas_call | solution.py:324
  435.0 26.0 %attention_backward.2 = (bf16[768,1024]{1,0:T(8,128)(2,1)}, bf16[8,1040,128]{2,1,0:T(8,128)(2,1)}) custom-call(s32[2]{0:T(128)} %pad_add_fusion.me_ref, bf16[768,1024]{1,0:T(8,128)(2,1)} %x_ref.7, bf16[768,1024]{1,0:T(8,128)(2,1)} %cot_ref.3, s32[2,1,384]{2,1,0:T(1,128)} %broadcast_in_dim.36.row_ref, s32[2,384,1]{2,1,0:T(8,128)} %copy.220.col_ref, ...), custom_call_target="tpu_custom_call" | custom-call | flops 7851737088 | bytes 31457280 | tf_op jit(solution)/shard_map/attention_backward/pallas_call | solution.py:835
  463.2 26.6 %attention_backward.3 = (bf16[768,1024]{1,0:T(8,128)(2,1)}, bf16[8,1040,128]{2,1,0:T(8,128)(2,1)}) custom-call(s32[2]{0:T(128)} %pad_add_fusion.me_ref, bf16[768,1024]{1,0:T(8,128)(2,1)} %x_ref.7, bf16[768,1024]{1,0:T(8,128)(2,1)} %cot_ref.3, s32[2,1,384]{2,1,0:T(1,128)} %broadcast_in_dim.36.row_ref, ...), custom_call_target="tpu_custom_call", output_to_operand_aliasing={{0}: (35, {})} | custom-call | flops 7851737088 | bytes 31457280 | tf_op jit(solution)/shard_map/attention_backward/pallas_call | solution.py:835
  494.2 6.0 %collective-permute-start.35 = (bf16[1,2,112,1024]{3,2,1,0:T(8,128)(2,1)}, bf16[1,2,112,1024]{3,2,1,0:T(8,128)(2,1)}, u32[]{:S(2)}, u32[]{:S(2)}) collective-permute-start(bf16[1,2,112,1024]{3,2,1,0:T(8,128)(2,1)} %get-tuple-element.447), channel_id=1, source_target_pairs={{0,8},{8,0},{16,24},{24,16},{1,9},{9,1},{17,25},{25,17},{2,10},{10... | collective-permute-start | bytes 1376264 | tf_op jit(solution)/shard_map/ppermute | solution.py:980
  506.2 5.7 %collective-permute-done.35.refs_4_ = bf16[1,2,112,1024]{3,2,1,0:T(8,128)(2,1)} collective-permute-done((bf16[1,2,112,1024]{3,2,1,0:T(8,128)(2,1)}, bf16[1,2,112,1024]{3,2,1,0:T(8,128)(2,1)}, u32[]{:S(2)}, u32[]{:S(2)}) %collective-permute-start.35) | collective-permute-done | bytes 458784 | tf_op jit(solution)/shard_map/ppermute | solution.py:980
  519.0 18.4 %reduce-scatter.8.cloned.1.call-done = bf16[1,1040,128]{2,1,0:T(8,128)(2,1)} async-done(((bf16[8,1040,128]{2,1,0:T(8,128)(2,1)}), bf16[1,1040,128]{2,1,0:T(8,128)(2,1)}) %reduce-scatter.8.cloned.1.call-update) | async-done | bytes 266256 | tf_op jit(solution)/shard_map/reduce_scatter | solution.py:1249
  546.4 4.7 mixture.2.refs_7_
  551.1 4.8 mixture.3
  (319 shorter events, 150.4 us)
Async XLA Ops:
  7.2 51.8 %all-gather.9.cloned.1.call-start = ((), (), s32[]{:S(2)}) async-start(), calls=%async_computation.6 | async-start | bytes 2654208 | tf_op jit(solution)/shard_map/all_gather | solution.py:1093
  11.9 240.1 %all-gather.13.cloned.1.call-start = ((), (), s32[]{:S(2)}) async-start(), calls=%async_computation.8 | async-start | bytes 19464192 | tf_op jit(solution)/shard_map/all_gather | solution.py:1121
  18.6 287.1 %all-gather.15.cloned.1.call-start = ((), (), s32[]{:S(2)}) async-start(), calls=%async_computation.9 | async-start | bytes 9732096 | tf_op jit(solution)/shard_map/all_gather | solution.py:1121
  22.8 36.2 %collective-permute-start.1 = (bf16[384,1024]{1,0:T(8,128)(2,1)}, bf16[384,1024]{1,0:T(8,128)(2,1)}, u32[]{:S(2)}, u32[]{:S(2)}) collective-permute-start(bf16[384,1024]{1,0:T(8,128)(2,1)} %get-tuple-element.294.refs_4_), channel_id=1, source_target_pairs={{0,16},{8,24},{16,0},{24,8},{1,17},{9,25},{17,1},{25,9},{2,18},{10... | collective-permute-start | bytes 2359304 | tf_op jit(solution)/shard_map/ppermute | solution.py:980
  24.3 34.6 %collective-permute-start.2 = (bf16[384,1024]{1,0:T(8,128)(2,1)}, bf16[384,1024]{1,0:T(8,128)(2,1)}, u32[]{:S(2)}, u32[]{:S(2)}) collective-permute-start(bf16[384,1024]{1,0:T(8,128)(2,1)} %get-tuple-element.294.refs_4_), channel_id=1, source_target_pairs={{0,24},{8,16},{16,8},{24,0},{1,25},{9,17},{17,9},{25,1},{2,26},{10... | collective-permute-start | bytes 2359304 | tf_op jit(solution)/shard_map/ppermute | solution.py:980
  62.5 325.5 %all-gather.11.cloned.1.call-start = ((), (), s32[]{:S(2)}) async-start(), calls=%async_computation.7 | async-start | bytes 9732096 | tf_op jit(solution)/shard_map/all_gather | solution.py:1121
  65.2 395.9 %reduce-scatter.4.cloned.1.call-start = ((), (), s32[]{:S(2)}) async-start(), calls=%async_computation.3 | async-start | bytes 5308416 | tf_op jit(solution)/shard_map/reduce_scatter | solution.py:1180
  67.1 51.9 %collective-permute-start.4 = (bf16[4,1152,128]{2,1,0:T(8,128)(2,1)S(1)}, bf16[4,1152,128]{2,1,0:T(8,128)(2,1)S(1)}, u32[]{:S(2)}, u32[]{:S(2)}) collective-permute-start(bf16[4,1152,128]{2,1,0:T(8,128)(2,1)S(1)} %constant_dynamic-slice_fusion.4), channel_id=1, source_target_pairs={{0,16},{8,24},{16,0},{24,8},{1,17},{9,25},{17,1},{25,9},{2,18},{10... | collective-permute-start | bytes 3538952 | tf_op jit(solution)/shard_map/ppermute | solution.py:980
  67.9 51.1 %collective-permute-start.5 = (bf16[4,1152,128]{2,1,0:T(8,128)(2,1)S(1)}, bf16[4,1152,128]{2,1,0:T(8,128)(2,1)S(1)}, u32[]{:S(2)}, u32[]{:S(2)}) collective-permute-start(bf16[4,1152,128]{2,1,0:T(8,128)(2,1)S(1)} %constant_dynamic-slice_fusion.4), channel_id=1, source_target_pairs={{0,24},{8,16},{16,8},{24,0},{1,25},{9,17},{17,9},{25,1},{2,26},{10... | collective-permute-start | bytes 3538952 | tf_op jit(solution)/shard_map/ppermute | solution.py:980
  125.4 36.6 %collective-permute-start.10 = (bf16[384,1024]{1,0:T(8,128)(2,1)}, bf16[384,1024]{1,0:T(8,128)(2,1)}, u32[]{:S(2)}, u32[]{:S(2)}) collective-permute-start(bf16[384,1024]{1,0:T(8,128)(2,1)} %get-tuple-element.335.refs_4_), channel_id=1, source_target_pairs={{0,16},{8,24},{16,0},{24,8},{1,17},{9,25},{17,1},{25,9},{2,18},{10... | collective-permute-start | bytes 2359304 | tf_op jit(solution)/shard_map/ppermute | solution.py:980
  126.0 36.0 %collective-permute-start.11 = (bf16[384,1024]{1,0:T(8,128)(2,1)}, bf16[384,1024]{1,0:T(8,128)(2,1)}, u32[]{:S(2)}, u32[]{:S(2)}) collective-permute-start(bf16[384,1024]{1,0:T(8,128)(2,1)} %get-tuple-element.335.refs_4_), channel_id=1, source_target_pairs={{0,24},{8,16},{16,8},{24,0},{1,25},{9,17},{17,9},{25,1},{2,26},{10... | collective-permute-start | bytes 2359304 | tf_op jit(solution)/shard_map/ppermute | solution.py:980
  127.4 35.8 %collective-permute-start.9 = (bf16[384,1024]{1,0:T(8,128)(2,1)}, bf16[384,1024]{1,0:T(8,128)(2,1)}, u32[]{:S(2)}, u32[]{:S(2)}) collective-permute-start(bf16[384,1024]{1,0:T(8,128)(2,1)} %get-tuple-element.335.refs_4_), channel_id=1, source_target_pairs={{0,8},{8,0},{16,24},{24,16},{1,9},{9,1},{17,25},{25,17},{2,10},{10... | collective-permute-start | bytes 2359304 | tf_op jit(solution)/shard_map/ppermute | solution.py:980
  163.7 36.4 %collective-permute-start.13 = (bf16[400,1024]{1,0:T(8,128)(2,1)}, bf16[400,1024]{1,0:T(8,128)(2,1)S(1)}, u32[]{:S(2)}, u32[]{:S(2)}) collective-permute-start(bf16[400,1024]{1,0:T(8,128)(2,1)} %get-tuple-element.291), channel_id=1, source_target_pairs={{0,16},{8,24},{16,0},{24,8},{1,17},{9,25},{17,1},{25,9},{2,18},{10... | collective-permute-start | bytes 2457608 | tf_op jit(solution)/shard_map/ppermute | solution.py:980
  164.7 35.4 %collective-permute-start.14 = (bf16[400,1024]{1,0:T(8,128)(2,1)}, bf16[400,1024]{1,0:T(8,128)(2,1)S(1)}, u32[]{:S(2)}, u32[]{:S(2)}) collective-permute-start(bf16[400,1024]{1,0:T(8,128)(2,1)} %get-tuple-element.292), channel_id=1, source_target_pairs={{0,24},{8,16},{16,8},{24,0},{1,25},{9,17},{17,9},{25,1},{2,26},{10... | collective-permute-start | bytes 2457608 | tf_op jit(solution)/shard_map/ppermute | solution.py:980
  201.7 35.9 %collective-permute-start.16 = (bf16[400,1024]{1,0:T(8,128)(2,1)}, bf16[400,1024]{1,0:T(8,128)(2,1)S(1)}, u32[]{:S(2)}, u32[]{:S(2)}) collective-permute-start(bf16[400,1024]{1,0:T(8,128)(2,1)} %get-tuple-element.333), channel_id=1, source_target_pairs={{0,16},{8,24},{16,0},{24,8},{1,17},{9,25},{17,1},{25,9},{2,18},{10... | collective-permute-start | bytes 2457608 | tf_op jit(solution)/shard_map/ppermute | solution.py:980
  202.2 35.4 %collective-permute-start.17 = (bf16[400,1024]{1,0:T(8,128)(2,1)}, bf16[400,1024]{1,0:T(8,128)(2,1)}, u32[]{:S(2)}, u32[]{:S(2)}) collective-permute-start(bf16[400,1024]{1,0:T(8,128)(2,1)} %get-tuple-element.334), channel_id=1, source_target_pairs={{0,24},{8,16},{16,8},{24,0},{1,25},{9,17},{17,9},{25,1},{2,26},{10... | collective-permute-start | bytes 2457608 | tf_op jit(solution)/shard_map/ppermute | solution.py:980
  305.7 188.5 %reduce-scatter.6.cloned.1.call-start = ((), (), s32[]{:S(2)}) async-start(), calls=%async_computation.4 | async-start | bytes 5308416 | tf_op jit(solution)/shard_map/reduce_scatter | solution.py:1224
  362.8 44.6 %collective-permute-start.23 = (bf16[768,1024]{1,0:T(8,128)(2,1)}, bf16[768,1024]{1,0:T(8,128)(2,1)S(1)}, u32[]{:S(2)}, u32[]{:S(2)}) collective-permute-start(bf16[768,1024]{1,0:T(8,128)(2,1)} %combine.12), channel_id=1, source_target_pairs={{0,16},{8,24},{16,0},{24,8},{1,17},{9,25},{17,1},{25,9},{2,18},{10... | collective-permute-start | bytes 4718600 | tf_op jit(solution)/shard_map/ppermute | solution.py:980
  367.5 39.9 %collective-permute-start.22 = (bf16[768,1024]{1,0:T(8,128)(2,1)}, bf16[768,1024]{1,0:T(8,128)(2,1)S(1)}, u32[]{:S(2)}, u32[]{:S(2)}) collective-permute-start(bf16[768,1024]{1,0:T(8,128)(2,1)} %combine.11), channel_id=1, source_target_pairs={{0,8},{8,0},{16,24},{24,16},{1,9},{9,1},{17,25},{25,17},{2,10},{10... | collective-permute-start | bytes 4718600 | tf_op jit(solution)/shard_map/ppermute | solution.py:980
  429.7 107.7 %reduce-scatter.8.cloned.1.call-start = ((), (), s32[]{:S(2)}) async-start(), calls=%async_computation.5 | async-start | bytes 2396160 | tf_op jit(solution)/shard_map/reduce_scatter | solution.py:1249
  502.7 36.2 %collective-permute-start.37 = (bf16[1,2,112,1024]{3,2,1,0:T(8,128)(2,1)}, bf16[1,2,112,1024]{3,2,1,0:T(8,128)(2,1)}, u32[]{:S(2)}, u32[]{:S(2)}) collective-permute-start(bf16[1,2,112,1024]{3,2,1,0:T(8,128)(2,1)} %get-tuple-element.449), channel_id=1, source_target_pairs={{0,24},{8,16},{16,8},{24,0},{1,25},{9,17},{17,9},{25,1},{2,26},{10... | collective-permute-start | bytes 1376264 | tf_op jit(solution)/shard_map/ppermute | solution.py:980
  502.7 37.8 %collective-permute-start.32 = (bf16[1,2,112,1024]{3,2,1,0:T(8,128)(2,1)}, bf16[1,2,112,1024]{3,2,1,0:T(8,128)(2,1)}, u32[]{:S(2)}, u32[]{:S(2)}) collective-permute-start(bf16[1,2,112,1024]{3,2,1,0:T(8,128)(2,1)} %get-tuple-element.443), channel_id=1, source_target_pairs={{0,8},{8,0},{16,24},{24,16},{1,9},{9,1},{17,25},{25,17},{2,10},{10... | collective-permute-start | bytes 1376264 | tf_op jit(solution)/shard_map/ppermute | solution.py:980
  504.1 47.0 %collective-permute-start.33 = (bf16[1,2,112,1024]{3,2,1,0:T(8,128)(2,1)}, bf16[1,2,112,1024]{3,2,1,0:T(8,128)(2,1)}, u32[]{:S(2)}, u32[]{:S(2)}) collective-permute-start(bf16[1,2,112,1024]{3,2,1,0:T(8,128)(2,1)} %get-tuple-element.444), channel_id=1, source_target_pairs={{0,16},{8,24},{16,0},{24,8},{1,17},{9,25},{17,1},{25,9},{2,18},{10... | collective-permute-start | bytes 1376264 | tf_op jit(solution)/shard_map/ppermute | solution.py:980
  511.9 39.2 %collective-permute-start.34 = (bf16[1,2,112,1024]{3,2,1,0:T(8,128)(2,1)}, bf16[1,2,112,1024]{3,2,1,0:T(8,128)(2,1)}, u32[]{:S(2)}, u32[]{:S(2)}) collective-permute-start(bf16[1,2,112,1024]{3,2,1,0:T(8,128)(2,1)} %get-tuple-element.445), channel_id=1, source_target_pairs={{0,24},{8,16},{16,8},{24,0},{1,25},{9,17},{17,9},{25,1},{2,26},{10... | collective-permute-start | bytes 1376264 | tf_op jit(solution)/shard_map/ppermute | solution.py:980
  (84 other events, 1008.5 us)
Sparse Core Ops, SparseCore 0:
  12.0 34.3 all-gather.8
  48.0 154.5 all-gather.12
  204.2 82.4 all-gather.14
  288.1 82.7 all-gather.10
  373.1 53.4 reduce-scatter.3
  429.9 55.4 reduce-scatter.5
  494.3 43.0 reduce-scatter.7

commit v3 on v2

--- a/solution.py
+++ b/solution.py
@@ -2,6 +2,7 @@
 
 import jax
 import jax.numpy as jnp
+import numpy as np
 from jax import lax
 from jax.experimental import pallas as pl
 from jax.experimental.pallas import tpu as pltpu
@@ -41,9 +42,11 @@
 
 def rotation(length):
     half_size = HD // 2
-    frequency = rope_base ** (-(2.0 * jnp.arange(half_size, dtype=f32)) / HD)
-    angles = jnp.arange(length, dtype=f32)[:, None] * frequency[None, :]
-    return tuple(jnp.tile(f(angles), (1, LANES // half_size)) for f in (jnp.cos, jnp.sin))
+    frequency = rope_base ** (-2.0 * np.arange(half_size) / HD)
+    angles = np.arange(length)[:, None] * frequency[None, :]
+    return tuple(
+        jnp.asarray(np.tile(f(angles), (1, LANES // half_size)), f32) for f in (np.cos, np.sin)
+    )
 
 
 def columns_to_rows(a):
@@ -116,8 +119,8 @@
 
 
 def dispatch_kernel(peers, capacity, *refs):
-    x_refs, cots = refs[:peers], refs[peers : 2 * peers]
-    xs_ref, cs_ref, gs_ref, rank_ref = refs[2 * peers :]
+    x_refs, cots = refs[: peers + 1], refs[peers + 1 : 2 * peers + 1]
+    xs_ref, cs_ref, gs_ref, rank_ref, column_ref = refs[2 * peers + 1 :]
     count, _, width = xs_ref.shape[1:]
     length = cots[0].shape[0]
     shape = xs_ref.shape[1:]
@@ -125,8 +128,15 @@
 
         @pl.when(pl.program_id(0) == i)
         def _():
-            table = get_extra(x_refs[i], length, length)
+            if i < peers - 1:
+                table = get_extra(x_refs[i], EXTRA + length, length)
+                x = x_refs[i][EXTRA : EXTRA + length]
+            else:
+                table = get_extra(x_refs[i], 0, length)
+                x = jnp.concatenate([x_refs[i][EXTRA:], x_refs[i + 1][...]], axis=0)
             rank_ref[0] = table[:count]
+            spare = jnp.zeros((LANES - count, length), f32)
+            column_ref[0] = jnp.concatenate([table[:count], spare], axis=0).T
             gates = table[count : 2 * count] + table[2 * count : 3 * count] + table[3 * count :]
             hot = []
             for e in range(count):
@@ -135,12 +145,12 @@
                 gate = jnp.sum(jnp.where(hits, gates[e : e + 1], 0.0), axis=1, keepdims=True)
                 gs_ref[0, e] = jnp.broadcast_to(gate, (capacity, LANES))
             hot = jnp.concatenate(hot, axis=0)
-            xs_ref[0] = nn(hot, x_refs[i][:length]).astype(bf16).reshape(shape)
+            xs_ref[0] = nn(hot, x).astype(bf16).reshape(shape)
             cs_ref[0] = nn(hot, cots[i][...]).astype(bf16).reshape(shape)
 
 
 def dispatch(rows, cots, count, capacity):
-    peers = len(rows)
+    peers = len(cots)
     length, width = cots[0].shape
 
     def out_spec(lanes):
@@ -159,12 +169,14 @@
             out_spec(width),
             out_spec(LANES),
             pl.BlockSpec((1, count, length), lambda k: (k, 0, 0)),
+            pl.BlockSpec((1, length, LANES), lambda k: (k, 0, 0)),
         ],
         out_shape=[
             shaped(width, bf16),
             shaped(width, bf16),
             shaped(LANES, f32),
             jax.ShapeDtypeStruct((peers, count, length), f32),
+            jax.ShapeDtypeStruct((peers, length, LANES), f32),
         ],
         compiler_params=pltpu.CompilerParams(vmem_limit_bytes=VMEM),
         cost_estimate=pl.CostEstimate(
@@ -174,14 +186,14 @@
     )(*rows, *cots)
 
 
-def expert_kernel(first, micro, held, add, final, *refs):
+def expert_kernel(first, micro, held, add, final, filled, *refs):
     tables, x_refs, c_refs, g_refs = (refs[i * micro : (i + 1) * micro] for i in range(4))
     w_ref, mask_ref = refs[4 * micro : 4 * micro + 2]
     n, _, capacity, width = x_refs[0].shape
     at = 4 * micro + 2
     old_products = refs[at : at + held]
     old_grads = refs[at + held]
-    outs = refs[at + held + 1 :]
+    outs = refs[at + held + 1 + filled :]
     y_refs, m_refs = outs[:n], outs[n : 2 * n]
     grad_ref = outs[2 * n]
     prod_refs = outs[2 * n + 1 : 2 * n + 1 + micro]
@@ -297,7 +309,7 @@
 
 
 def expert_chunk(
-    slots, weights, masks, first, inner_width, grad_at, grad_count, grads, products, add, final
+    slots, weights, masks, first, inner_width, grad_at, grad_count, grads, products, add, final=None, filled=()
 ):
     micro = len(slots)
     tables = [t[3] for t in slots]
@@ -314,6 +326,9 @@
     out_shape = jax.ShapeDtypeStruct((micro, count, capacity, width), bf16)
     back_spec, back_shape = out_spec, out_shape
     if final:
+        total, step = final
+        out_shape = jax.ShapeDtypeStruct((total, count, capacity, width), bf16)
+        out_spec = pl.BlockSpec((1, 1, capacity, width), lambda e: (step, e, 0, 0))
         back_shape = jax.ShapeDtypeStruct((count * capacity + EXTRA, width), bf16)
         back_spec = pl.BlockSpec(back_shape.shape, lambda e: (0, 0))
     grad_spec = pl.BlockSpec((SHARDS, 1, grad_rows, LANES), lambda e: (0, grad_at + e, 0, 0))
@@ -321,8 +336,11 @@
     work = n * micro * capacity * count
     held = products or []
     kept = jnp.zeros((8, LANES), f32) if grads is None else grads
+    at = 2 + 4 * micro + len(held)
+    aliases = {} if grads is None else {at: 2 * n}
+    aliases.update({at + 1 + k: k for k in range(len(filled))})
     return pl.pallas_call(
-        functools.partial(expert_kernel, first, micro, len(held), add, final),
+        functools.partial(expert_kernel, first, micro, len(held), add, bool(final), len(filled)),
         grid=(count,),
         in_specs=[pl.BlockSpec(tables[0].shape, lambda e: (0, 0, 0))] * micro
         + [slot_spec(width)] * (2 * micro)
@@ -332,7 +350,8 @@
             pl.BlockSpec(masks.shape, lambda e: (0, 0, 0)),
         ]
         + [prod_spec] * len(held)
-        + [grad_spec if add else pl.BlockSpec(memory_space=pl.ANY)],
+        + [grad_spec if add else pl.BlockSpec(memory_space=pl.ANY)]
+        + [pl.BlockSpec(memory_space=pl.ANY)] * len(filled),
         out_specs=[out_spec] * n + [back_spec] * n + [grad_spec] + [prod_spec] * micro,
         out_shape=[out_shape] * n
         + [back_shape] * n
@@ -354,58 +373,70 @@
             bytes_accessed=8 * work * width + 6 * count * rows * LANES * SHARDS,
             transcendentals=work * inner_width,
         ),
-        input_output_aliases={} if grads is None else {2 + 4 * micro + len(held): 2 * n},
+        input_output_aliases=aliases,
         name="experts",
     )(
         *tables, *[t[0] for t in slots], *[t[1] for t in slots], *[t[2] for t in slots],
-        weights, masks, *held, kept,
-    )
-
-
-def combine_kernel(peer, chunks, micro, added, *refs):
-    tables, row_refs = refs[:micro], refs[micro : micro + chunks]
-    outs = refs[micro + chunks + (added is not None) :]
+        weights, masks, *held, kept, *filled,
+    )
+
+
+def combine_kernel(chunks, jobs, added, *refs):
+    columns, refs = refs[:jobs], refs[jobs:]
+    row_refs, refs = refs[: jobs * chunks], refs[jobs * chunks :]
+    outs = refs[added is not None :]
     capacity, width = row_refs[0].shape[2:]
-    length = tables[0].shape[2]
-    for m in range(micro):
-        total = None
-        e = 0
-        for ref in row_refs:
-            hot = []
-            here = ref.shape[1]
-            for i in range(here):
-                hits = hits_of(tables[m][peer, e : e + 1, :], capacity)
+    length = columns[0].shape[1]
+    slot = lax.broadcasted_iota(jnp.int32, (length, LANES), 1)
+    spare = jnp.zeros((LANES - capacity, width), bf16)
+    for job in range(jobs):
+        place = columns[job][0].astype(jnp.int32)
+        hot, rows = [], []
+        for ref in row_refs[job * chunks : (job + 1) * chunks]:
+            for i in range(ref.shape[1]):
+                e = len(hot)
+                hits = slot == place[:, e : e + 1]
                 hot.append(jnp.where(hits, 1.0, 0.0).astype(bf16))
-                e += 1
-            term = tn(jnp.concatenate(hot, axis=0), ref[m].reshape(here * capacity, width))
-            total = term if total is None else total + term
-        if added == m:
-            total = total + refs[micro + chunks][...].astype(f32)
+                rows += [ref[0, i], spare]
+        total = nn(jnp.concatenate(hot, axis=1), jnp.concatenate(rows, axis=0))
+        if added == job:
+            total = total + refs[0][...].astype(f32)
         if len(outs) > 1:
-            outs[m][...] = total.astype(bf16)
+            outs[job][...] = total.astype(bf16)
         else:
-            outs[0][m * length : (m + 1) * length, :] = total.astype(bf16)
-
-
-def combine(slots, rows, peer, apart=False, added=None, add=None):
-    tables = [t[3] for t in slots]
-    micro, length = len(tables), tables[0].shape[2]
-    capacity, width = rows[0].shape[2:]
-    work = micro * sum(a.shape[1] for a in rows) * capacity
-    whole = pl.BlockSpec(memory_space=pltpu.VMEM)
-    shapes = [(length, width)] * micro if apart else [(micro * length, width)]
-    operands = [*tables, *rows] + ([] if add is None else [add])
+            outs[0][job * length : (job + 1) * length] = total.astype(bf16)
+
+
+def combine(slots, jobs, apart=False, add=None):
+    columns = [slots[m][4] for _, _, m in jobs]
+    length = columns[0].shape[1]
+    chunks = len(jobs[0][1])
+    capacity, width = jobs[0][1][0].shape[2:]
+    work = len(jobs) * sum(a.shape[1] for a in jobs[0][1]) * capacity
+
+    def at(place, a):
+        return pl.BlockSpec((1,) + a.shape[1:], lambda i: (place,) + (0,) * (a.ndim - 1))
+
+    added, spec, operand = None, [], []
+    if add is not None:
+        added, block, place = add
+        operand = [block]
+        spec = [pl.BlockSpec((length, width), lambda i: (place, 0))]
+    shapes = [(length, width)] * len(jobs) if apart else [(len(jobs) * length, width)]
     out = pl.pallas_call(
-        functools.partial(combine_kernel, peer, len(rows), micro, added),
-        in_specs=[whole] * len(operands),
-        out_specs=[whole] * len(shapes),
+        functools.partial(combine_kernel, chunks, len(jobs), added),
+        grid=(1,),
+        in_specs=[at(job[0], a) for job, a in zip(jobs, columns)]
+        + [at(m, a) for _, rows, m in jobs for a in rows]
+        + spec,
+        out_specs=[pl.BlockSpec(shape, lambda i: (0, 0)) for shape in shapes],
         out_shape=[jax.ShapeDtypeStruct(shape, bf16) for shape in shapes],
         compiler_params=pltpu.CompilerParams(vmem_limit_bytes=VMEM),
         cost_estimate=pl.CostEstimate(
             flops=2 * work * length * width, bytes_accessed=3 * work * width, transcendentals=0
         ),
         name="combine",
-    )(*operands)
+    )(*columns, *[a for _, rows, _ in jobs for a in rows], *operand)
     return out if apart else out[0]
 
 
@@ -414,6 +445,7 @@
 SPAN = GROUP * HD
 REPEAT = H // KVH
 NGROUPS = KVH // GROUP
+GRAD_ROWS = 9 * REDUCED_DIM
 
 
 def query_order():
@@ -444,9 +476,9 @@
     return jnp.concatenate([a[o * size : (o + 1) * size] for o in order], axis=0)
 
 
-def put_rows(a, order, size):
+def columns_back(a, order, size):
     inverse = sorted(range(len(order)), key=lambda i: order[i])
-    return take_rows(a, inverse, size)
+    return jnp.concatenate([a[:, o * size : (o + 1) * size] for o in inverse], axis=1)
 
 
 def lay_out_columns(a):
@@ -479,43 +511,47 @@
     return jnp.where(lanes_like(a) // HD == n, a, jnp.zeros_like(a))
 
 
-def unpack_kernel(peers, me_ref, *refs):
-    own, near, far = refs[0], refs[1:peers], refs[peers : 2 * peers - 1]
-    qkv_ref, exit_ref, other_ref = refs[2 * peers - 1 :]
+def unpack_kernel(peers, places, me_ref, *refs):
+    packed = refs[: len(places)]
+    qkv_ref, exit_ref, other_ref = refs[len(places) :]
     width = qkv_ref.shape[0]
-    shards = own.shape[0]
-    ru, half = width // shards, width // 2
     a, b = qkv_ref.shape[1] // LANES // peers, exit_ref.shape[1] // LANES // peers
     c = other_ref.shape[0] // peers
-    order = [n * REPEAT + r for r in range(REPEAT) for n in range(GROUP)]
-
-    def place(part, h, q):
-        def block(j):
-            return part[:, j * ru : (j + 1) * ru, :].reshape(half, LANES)
-
-        rows = pl.ds(pl.multiple_of(h * half, half), half)
-        for j in range(a):
-            columns = pl.ds(pl.multiple_of((q * a + j) * LANES, LANES), LANES)
-            qkv_ref[rows, columns] = block(j)
-        for j in range(b):
-            columns = pl.ds(pl.multiple_of((q * b + j) * LANES, LANES), LANES)
-            exit_ref[rows, columns] = take_rows(block(a + j), order, HD)
-        for j in range(c):
-            other_ref[q * c + j, rows, :] = block(a + b + j)
-
-    me, core = me_ref[0], me_ref[1]
-    for h in range(2):
-        place(own.at[h * shards // 2 : (h + 1) * shards // 2], h, me)
-    for k in range(1, peers):
-        place(near[k - 1], core, me ^ k)
-        place(far[k - 1], 1 - core, me ^ k)
-
-
-def unpack(me, own, near, far, width, qkv_width, others):
+    ru = packed[0].shape[1] // (a + b + c)
+    step = min(ru, HD)
+    me, core, chip = me_ref[0], me_ref[1], me_ref[2]
+    for (k, other_core, first), part in zip(places, packed):
+        q = me ^ k
+        for i in range(part.shape[0]):
+            shard = (chip ^ (first + i)) * 2 + (core ^ other_core)
+
+            def block(j):
+                return part[i, j * ru : (j + 1) * ru, :]
+
+            def columns(j):
+                return pl.ds(pl.multiple_of(j * LANES, LANES), LANES)
+
+            rows = pl.ds(pl.multiple_of(shard * ru, ru), ru)
+            for j in range(a):
+                qkv_ref[rows, columns(q * a + j)] = block(j)
+            for sub in range(ru // step):
+                row = shard * ru + sub * step
+                head, within = row // HD, row % HD
+                g, n, r = head // (GROUP * REPEAT), head // REPEAT % GROUP, head % REPEAT
+                row = ((g * REPEAT + r) * GROUP + n) * HD + within
+                rows_out = pl.ds(pl.multiple_of(row, step), step)
+                for j in range(b):
+                    exit_ref[rows_out, columns(q * b + j)] = block(a + j)[
+                        sub * step : (sub + 1) * step
+                    ]
+            for j in range(c):
+                other_ref[q * c + j, rows, :] = block(a + b + j)
+
+
+def unpack(me, packed, places, peers, width, qkv_width, others):
     whole = pl.BlockSpec(memory_space=pltpu.VMEM)
-    packed = [own, *near, *far]
     return pl.pallas_call(
-        functools.partial(unpack_kernel, len(near) + 1),
+        functools.partial(unpack_kernel, peers, places),
         in_specs=[pl.BlockSpec(memory_space=pltpu.SMEM)] + [whole] * len(packed),
         out_specs=[whole] * 3,
         out_shape=[
@@ -532,8 +568,14 @@
     return lax.rsqrt(jnp.mean(values * values, axis=-1, keepdims=True) + eps_norm)
 
 
+def shut_of(labels):
+    labels = labels.astype(f32)
+    of_query = jnp.broadcast_to(labels, (LANES, labels.shape[1])).T[:, :1]
+    return jnp.where(labels <= of_query, 0.0, -1e30)
+
+
 def attn_forward_kernel(
-    me_ref, x_ref, chosen_ref, rank_ref, row_ref, col_ref, mask_ref, cos_ref, sin_ref, qkv_ref,
+    me_ref, x_ref, chosen_ref, rank_ref, row_ref, mask_ref, cos_ref, sin_ref, qkv_ref,
     exit_ref, oth_ref, kout_ref, vout_ref, rout_ref, gain_ref,
     res_ref, q_ref, k_ref, v_ref, lse_ref, att_ref, lora_ref, olora_ref, rlora_ref, gate_ref,
     *sent_refs,
@@ -554,7 +596,7 @@
     k = nn(normed, qkv_ref[:, qw : qw + kw]) + nt(lora[1], k_out)
     k_ref[...] = rope(k, cos, sin, 1.0).astype(bf16)
     v_ref[...] = (nn(normed, qkv_ref[:, qw + kw :]) + nt(lora[2], vout_ref[...])).astype(bf16)
-    shut = jnp.where(row_ref[0] <= col_ref[0], 0.0, -1e30)
+    shut = shut_of(row_ref[0])
     lane = lax.broadcasted_iota(jnp.int32, (length, LANES), 1)
     logs = jnp.zeros((length, LANES), f32)
     for g in range(NGROUPS):
@@ -585,7 +627,7 @@
     res_ref[...] = residual
     moe = (residual * scale_rows(residual) * gain_ref[1:2, :]).astype(bf16)
     for ref in sent_refs:
-        ref[:length] = moe
+        ref[EXTRA : EXTRA + length] = moe
     route_lora = (nn(moe, oth_ref[7]) * mask).astype(bf16)
     rlora_ref[...] = route_lora
     logits = nn(moe, oth_ref[8]) + nn(route_lora, rout_ref[...])
@@ -595,16 +637,18 @@
     )
     gates = weight / jnp.sum(weight, axis=1, keepdims=True)
     gate_ref[0] = gates.T[: gate_ref.shape[1]]
-    own = gate_ref.shape[1] // len(sent_refs)
+    own = gate_ref.shape[1] // (len(sent_refs) + 1)
+
+    def numbers(k):
+        group = pl.ds(pl.multiple_of((me_ref[0] ^ k) * own, own), own)
+        return jnp.concatenate([rank_ref[0, group, :], *pieces_of(gate_ref[0, group, :])], axis=0)
+
     for k, ref in enumerate(sent_refs):
-        group = pl.ds(pl.multiple_of((me_ref[0] ^ k) * own, own), own)
-        value = jnp.concatenate(
-            [rank_ref[0, group, :], *pieces_of(gate_ref[0, group, :])], axis=0
-        )
-        put_extra(ref, length, length, value)
-
-
-def attn_forward(step, me, hidden, chosen, rank, rows, cols, mask, cos, sin, weights, peers):
+        put_extra(ref, 0, length, numbers(len(sent_refs)))
+        put_extra(ref, EXTRA + length, length, numbers(k))
+
+
+def attn_forward(step, me, hidden, chosen, rank, rows, mask, cos, sin, weights, peers):
     _, experts, length = rank.shape
     width = hidden.shape[1]
 
@@ -622,13 +666,13 @@
         ((length, width), f32), ((length, qw), bf16), ((length, kw), bf16), ((length, kw), bf16),
          ((length, LANES), f32), ((length, qw), bf16), ((length, 3 * LANES), bf16),
         ((length, LANES), bf16), ((length, LANES), bf16), ((1, experts, length), f32),
-    ] + [((length + EXTRA, width), bf16)] * peers
+    ] + [((length + 2 * EXTRA, width), bf16)] * (peers - 1)
     shapes = [jax.ShapeDtypeStruct(*shape) for shape in shapes]
     return pl.pallas_call(
         attn_forward_kernel,
         grid=(1,),
         in_specs=[pl.BlockSpec(memory_space=pltpu.SMEM), by_row(hidden), by_row(chosen)]
-        + [by_step(a) for a in (rank, rows, cols, mask)]
+        + [by_step(a) for a in (rank, rows, mask)]
         + [whole(a) for a in (cos, sin, *weights)],
         out_specs=[whole(a) for a in shapes],
         out_shape=shapes,
@@ -639,7 +683,7 @@
             transcendentals=H * length * length,
         ),
         name="attention_forward",
-    )(me, hidden, chosen, rank, rows, cols, mask, cos, sin, *weights)
+    )(me, hidden, chosen, rank, rows, mask, cos, sin, *weights)
 
 
 def last_hits(rank_ref, count, capacity):
@@ -647,7 +691,7 @@
 
 
 def attn_backward_kernel(
-    peers, last, parts, older, me_ref, x_ref, cot_ref, row_ref, col_ref, mask_ref, cos_ref, sin_ref,
+    step, peers, last, parts, older, me_ref, x_ref, cot_ref, row_ref, mask_ref, cos_ref, sin_ref,
     qkv_ref, exit_ref, oth_ref, kout_ref, vout_ref, rout_ref, gain_ref,
     res_ref, q_ref, k_ref, v_ref, lse_ref, att_ref, lora_ref, olora_ref, rlora_ref, gate_ref, moe_ref,
     rank_ref, *refs,
@@ -655,7 +699,7 @@
     part_refs, tail_refs = refs[:parts], refs[parts : parts + peers]
     at = parts + peers
     old_grads = refs[at : at + older]
-    out_ref, grad_ref, product_ref, dq_ref, dk_ref, dv_ref = refs[at + 2 * older :]
+    out_ref, grad_ref, product_ref, dq_ref, dk_ref, dv_ref, hold_ref = refs[at + 2 * older :]
     length, width = x_ref.shape
     experts = gate_ref.shape[1]
     own = experts // peers
@@ -694,7 +738,7 @@
     out_lora_grad = (nn(att_grad, merge_out) * mask).astype(bf16)
     head_grad = (nt(att_grad, exit_ref[...]) + nt(out_lora_grad, merge_in)).astype(bf16)
 
-    shut = jnp.where(row_ref[0] <= col_ref[0], 0.0, -1e30)
+    shut = shut_of(row_ref[0])
     logs = lse_ref[...]
     for g in range(NGROUPS):
         kg = k_ref[:, g * SPAN : (g + 1) * SPAN]
@@ -764,62 +808,56 @@
         res_grad + scale * scaled - hidden * (scale * scale * scale * inner)
     ).astype(bf16)
 
+    ru = width // SHARDS
+    top = step * GRAD_ROWS
+    for old in old_grads:
+        grad_ref[:, :top] = old[...]
+    adapter = me_ref[3 + step]
+
+    def own_rows(a, b):
+        term = tn(a, b)
+        hold_ref[:, : term.shape[1]] = term
+        rows = pl.ds(pl.multiple_of(adapter * REDUCED_DIM, REDUCED_DIM), REDUCED_DIM)
+        return hold_ref[rows, : term.shape[1]]
+
     lora = [lora_ref[:, i * LANES : (i + 1) * LANES] for i in range(3)]
-    terms = (
-        tn(jnp.concatenate(lora_grads, axis=1), normed),
-        tn(lora[0], dq),
-        tn(lora[1], dk),
-        tn(lora[2], dv),
-        tn(out_lora_grad, att_ref[...]),
-        tn(olora_ref[...], att_grad),
-        tn(route_lora_grad, moe_ref[...]),
-        tn(rlora_ref[...], logit_grad),
-    )
-    ru = width // SHARDS
-
-    def put(place, value):
-        if older:
-            value = value + old_grads[0][place].astype(f32)
-        grad_ref[place] = value.astype(bf16)
-
-    def put_columns(at, value):
+    pieces = [own_rows(g, normed) for g in lora_grads]
+    pieces.append(columns_back(own_rows(lora[0], dq), query_halves(), HALF))
+    key_piece = columns_back(own_rows(lora[1], dk), key_halves(), HALF)
+    value_piece = own_rows(lora[2], dv)
+    pieces.append(
+        jnp.concatenate(
+            [
+                part[:, h * HD : (h + 1) * HD]
+                for h in range(KVH)
+                for part in (key_piece, value_piece)
+            ],
+            axis=1,
+        )
+    )
+    pieces.append(columns_back(own_rows(out_lora_grad, att_ref[...]), query_order(), HD))
+    pieces.append(own_rows(olora_ref[...], att_grad))
+    pieces.append(own_rows(route_lora_grad, moe_ref[EXTRA : EXTRA + length]))
+    for i, piece in enumerate(pieces):
+        rows = slice(top + i * REDUCED_DIM, top + (i + 1) * REDUCED_DIM)
         for s in range(SHARDS):
-            put((s, slice(at, at + value.shape[0])), value[:, s * ru : (s + 1) * ru])
-
-    def put_rows_at(at, value):
-        size = value.shape[0] // SHARDS
-        put((slice(None), slice(at, at + size)), value.reshape(SHARDS, size, LANES))
-
-    at = 0
-    sizes = attn_grad_rows(width)
-    turned = {
-        1: lambda a: put_rows(a.T, query_halves(), HALF),
-        2: lambda a: put_rows(a.T, key_halves(), HALF),
-        3: lambda a: a.T,
-        4: lambda a: put_rows(a.T, query_order(), HD),
-        7: lambda a: a,
-    }
-    for i, (size, term) in enumerate(zip(sizes, terms)):
-        if i in turned:
-            put_rows_at(at, turned[i](term))
-        else:
-            put_columns(at, term)
-        at += size
-
-
-def attn_grad_rows(width):
-    ru, qs, ks = width // SHARDS, H * HD // SHARDS, KVH * HD // SHARDS
-    return (3 * LANES, qs, ks, ks, qs, LANES, LANES, LANES // SHARDS)
+            grad_ref[s, rows] = piece[:, s * ru : (s + 1) * ru].astype(bf16)
+    piece = own_rows(rlora_ref[...], logit_grad)
+    lane = lax.broadcasted_iota(jnp.int32, piece.shape, 1)
+    number = jnp.broadcast_to(adapter, piece.shape).astype(f32)
+    piece = jnp.where(lane < LANES // 2, piece, number).astype(bf16)
+    for s in range(SHARDS):
+        grad_ref[s, top + GRAD_ROWS - REDUCED_DIM : top + GRAD_ROWS] = piece
 
 
 def attn_backward(
-    step, last, me, hidden, cotangent, rows, cols, mask, cos, sin, weights, saved, moe, rank, parts, tails, older
+    step, last, me, hidden, cotangent, rows, mask, cos, sin, weights, saved, moe, rank, parts, tails, older
 ):
     length = rows.shape[2]
     width = hidden.shape[1]
     peers = len(tails)
     experts = saved[-1].shape[1]
-    grads = jax.ShapeDtypeStruct((SHARDS, sum(attn_grad_rows(width)), LANES), bf16)
+    grads = jax.ShapeDtypeStruct((SHARDS, (step + 1) * GRAD_ROWS, LANES), bf16)
 
     def by_row(a):
         return pl.BlockSpec((length, a.shape[1]), lambda i: (step, 0))
@@ -831,14 +869,14 @@
         return pl.BlockSpec(a.shape, lambda i: (0,) * a.ndim)
 
     qw, kw = H * HD, KVH * HD
-    ahead = 8 + len(weights) + len(saved) + 2 + len(parts) + peers
+    ahead = 7 + len(weights) + len(saved) + 2 + len(parts) + peers
     return pl.pallas_call(
-        functools.partial(attn_backward_kernel, peers, last, len(parts), len(older) // 2),
+        functools.partial(attn_backward_kernel, step, peers, last, len(parts), len(older) // 2),
         grid=(1,),
         in_specs=[pl.BlockSpec(memory_space=pltpu.SMEM), by_row(hidden), by_row(cotangent)]
-        + [by_step(a) for a in (rows, cols, mask)]
+        + [by_step(a) for a in (rows, mask)]
         + [whole(a) for a in (cos, sin, *weights, *saved)]
-        + [pl.BlockSpec((length, width), lambda i: (0, 0)), by_step(rank)]
+        + [whole(moe), by_step(rank)]
         + [by_row(a) for a in parts]
         + [whole(a) for a in tails]
         + ([whole(older[0]), pl.BlockSpec(memory_space=pl.ANY)] if older else []),
@@ -849,6 +887,7 @@
             pltpu.VMEM((length, qw), bf16),
             pltpu.VMEM((length, kw), bf16),
             pltpu.VMEM((length, kw), bf16),
+            pltpu.VMEM((LANES, max(width, qw)), f32),
         ],
         compiler_params=pltpu.CompilerParams(vmem_limit_bytes=VMEM),
         cost_estimate=pl.CostEstimate(
@@ -859,28 +898,24 @@
         input_output_aliases={ahead + 1: 0} if older else {},
         name="attention_backward",
     )(
-        me, hidden, cotangent, rows, cols, mask, cos, sin, *weights, *saved, moe, rank, *parts, *tails, *older
-    )
-
-
-def mixture_kernel(peers, count, last, res_ref, rank_ref, *refs):
-    parts, tails, out_ref = refs[:count], refs[count : count + peers], refs[-1]
-    capacity, width = tails[0].shape[2:]
-    hits = last_hits(rank_ref, peers * last, capacity)
+        me, hidden, cotangent, rows, mask, cos, sin, *weights, *saved, moe, rank, *parts, *tails, *older
+    )
+
+
+def mixture_kernel(res_ref, rank_ref, own_ref, far_ref, *refs):
+    parts, out_ref = refs[:3], refs[-1]
+    last, capacity, width = far_ref.shape[1:]
+    hits = last_hits(rank_ref, 2 * last, capacity)
     hot = jnp.concatenate([jnp.where(h, 1.0, 0.0).astype(bf16) for h in hits], axis=0)
-    rows = jnp.concatenate([ref[0].reshape(last * capacity, width) for ref in tails], axis=0)
-    total = tn(hot, rows)
+    rows = [ref[0].reshape(last * capacity, width) for ref in (own_ref, far_ref)]
+    total = tn(hot, jnp.concatenate(rows, axis=0))
     for ref in parts:
         total = total + ref[...].astype(f32)
     out_ref[...] = (res_ref[...] + total).astype(bf16)
 
 
-def add_mixture(step, residual, rank, parts, tails, older):
-    length = rank.shape[2]
-    width = residual.shape[1]
-
-    def by_row(a):
-        return pl.BlockSpec((length, a.shape[1]), lambda i: (step, 0))
+def add_mixture(step, total, residual, rank, own, far, parts, older):
+    length, width = residual.shape
 
     def by_step(a):
         return pl.BlockSpec((1,) + a.shape[1:], lambda i: (step,) + (0,) * (a.ndim - 1))
@@ -889,21 +924,20 @@
         return pl.BlockSpec(a.shape, lambda i: (0,) * a.ndim)
 
     return pl.pallas_call(
-        functools.partial(mixture_kernel, len(tails), len(parts), tails[0].shape[1]),
+        mixture_kernel,
         grid=(1,),
-        in_specs=[whole(residual), by_step(rank)]
-        + [by_row(a) for a in parts]
-        + [whole(a) for a in tails]
+        in_specs=[whole(residual), by_step(rank), by_step(own), by_step(far)]
+        + [pl.BlockSpec((length, width), lambda i: (step, 0))] * len(parts)
         + [pl.BlockSpec(memory_space=pl.ANY)] * len(older),
-        out_specs=by_row(parts[0]),
-        out_shape=jax.ShapeDtypeStruct(parts[0].shape, bf16),
+        out_specs=pl.BlockSpec((length, width), lambda i: (step, 0)),
+        out_shape=jax.ShapeDtypeStruct((total * length, width), bf16),
         compiler_params=pltpu.CompilerParams(vmem_limit_bytes=VMEM),
         cost_estimate=pl.CostEstimate(
-            flops=2 * length * 1000 * width, bytes_accessed=20 * length * width, transcendentals=0
+            flops=2 * length * 256 * width, bytes_accessed=16 * length * width, transcendentals=0
         ),
-        input_output_aliases={2 + len(parts) + len(tails): 0} if older else {},
+        input_output_aliases={4 + len(parts): 0} if older else {},
         name="mixture",
-    )(residual, rank, *parts, *tails, *older)
+    )(residual, rank, own, far, *parts, *older)
 
 
 def finish_experts_kernel(chunks, *refs):
@@ -942,35 +976,75 @@
     )(*parts)
 
 
-def finish_attention_kernel(sizes, peers, *refs):
-    parts, outs = refs[:peers], refs[peers:]
+def gather_grads_kernel(g_ref, out_ref, sums_ref):
+    sources, rows, _ = g_ref.shape
+    sums_ref[...] = jnp.zeros_like(sums_ref)
+    for source in range(sources):
+        for at in range(0, rows, GRAD_ROWS):
+            piece = g_ref[source, at : at + GRAD_ROWS].astype(f32)
+            number = piece[GRAD_ROWS - 1 :, LANES - 1 :]
+            for a in range(PLUGIN_CHOICES):
+                sums_ref[a] += jnp.where(number == a, piece, 0.0)
+    for a in range(PLUGIN_CHOICES):
+        for at in range(0, GRAD_ROWS, REDUCED_DIM):
+            rows = slice((at // REDUCED_DIM * PLUGIN_CHOICES + a) * REDUCED_DIM, None)
+            rows = slice(rows.start, rows.start + REDUCED_DIM)
+            out_ref[rows] = sums_ref[a, at : at + REDUCED_DIM].astype(bf16)
+
+
+def gather_grads(received):
+    whole = pl.BlockSpec(memory_space=pltpu.VMEM)
+    return pl.pallas_call(
+        gather_grads_kernel,
+        in_specs=[whole],
+        out_specs=whole,
+        out_shape=jax.ShapeDtypeStruct((GRAD_ROWS * PLUGIN_CHOICES, LANES), bf16),
+        scratch_shapes=[pltpu.VMEM((PLUGIN_CHOICES, GRAD_ROWS, LANES), f32)],
+        compiler_params=pltpu.CompilerParams(vmem_limit_bytes=VMEM),
+        name="gather_grads",
+    )(received)
+
+
+def finish_attention_kernel(peers, shard_ref, *refs):
+    parts, outs = refs[:peers], refs[peers:-1]
+    hold = refs[-1]
     total = parts[0][...].astype(f32)
     for ref in parts[1:]:
         total = total + ref[...].astype(f32)
-    at = 0
-    for i, (size, ref) in enumerate(zip(sizes, outs)):
-        piece = total[at : at + size]
-        at += size
-        if i in (0, 1, 2, 3, 6):
-            ref[...] = piece.T
-        else:
-            ref[...] = piece[:, : ref.shape[1]]
-
-
-def finish_attention(parts, sizes, experts):
+    piece = [total[i * LANES : (i + 1) * LANES] for i in range(9)]
+    for i in range(3):
+        outs[0][:, i * LANES : (i + 1) * LANES] = piece[i].T
+    outs[1][...] = piece[3]
+    turned = piece[4].T
+    outs[2][...] = turned[: outs[2].shape[0]]
+    outs[3][...] = turned[outs[2].shape[0] :]
+    outs[4][...] = piece[5].T
+    outs[5][...] = piece[6]
+    outs[6][...] = piece[7].T
+    hold[...] = piece[8]
+    size = outs[7].shape[0]
+    rows = pl.ds(pl.multiple_of(shard_ref[0] * size, size), size)
+    outs[7][...] = hold[rows, : outs[7].shape[1]]
+
+
+def finish_attention(shard, parts, experts):
+    adapters, size = LANES, LANES // SHARDS
+    half = KVH * HD // SHARDS
     shapes = [
-        (LANES, sizes[0]), (LANES, sizes[1]), (LANES, sizes[2]), (LANES, sizes[3]),
-        (sizes[4], LANES), (sizes[5], LANES), (LANES, sizes[6]), (sizes[7], experts),
+        (LANES, 3 * adapters), (adapters, LANES), (half, adapters), (half, adapters),
+        (LANES, adapters), (adapters, LANES), (LANES, adapters), (size, experts),
     ]
     whole = pl.BlockSpec(memory_space=pltpu.VMEM)
-    return pl.pallas_call(
-        functools.partial(finish_attention_kernel, sizes, len(parts)),
-        in_specs=[whole] * len(parts),
+    out = pl.pallas_call(
+        functools.partial(finish_attention_kernel, len(parts)),
+        in_specs=[pl.BlockSpec(memory_space=pltpu.SMEM)] + [whole] * len(parts),
         out_specs=[whole] * len(shapes),
         out_shape=[jax.ShapeDtypeStruct(s, f32) for s in shapes],
+        scratch_shapes=[pltpu.VMEM((LANES, LANES), f32)],
         compiler_params=pltpu.CompilerParams(vmem_limit_bytes=VMEM),
         name="finish_attention",
-    )(*parts)
+    )(shard, *parts)
+    return [a.T if i in (2, 3) else a for i, a in enumerate(out)]
 
 
 def exchange(a, k):
@@ -1023,7 +1097,10 @@
     peers = range(dp_count)
     last = CHUNKS[-1]
     core = lax.axis_index("fsdp") % 2
-    me = jnp.stack([dp_rank, core]).astype(jnp.int32)
+    chip = lax.axis_index("fsdp") // 2 if shard_count == SHARDS else jnp.zeros_like(core)
+    me = jnp.concatenate([jnp.stack([dp_rank, core, chip]), plugin_choice_per_text[dp_rank]])
+    me = me.astype(jnp.int32)
+    shard = lax.axis_index("fsdp").astype(jnp.int32).reshape(1)
     cot_rows = [exit_cotangent[m * seq_len : (m + 1) * seq_len] for m in range(micro_count)]
     cot_from = [[exchange(cot_rows[0], k)] for k in peers]
 
@@ -1046,7 +1123,25 @@
     )
     own_mask = masks[:, :1]
     section_rows = section_labels[:, None, :]
-    section_cols = section_labels[:, :, None]
+
+    chunk_weights = []
+
+    def gather_chunk(first, size, before_it, cot_from):
+        here = slice(first, first + size)
+        shards = (
+            branch_widen_coefficients[here],
+            branch_contract_coefficients[here],
+            branch_plugin_source[here],
+            branch_plugin_target[here],
+            contract_plugin_source[here],
+            contract_plugin_target[here],
+        )
+        if first:
+            shards, before_it, cot_from[1] = lax.optimization_barrier((shards, before_it, cot_from[1]))
+        packed = pack_experts(*shards)
+        gathered = lax.all_gather(packed, "fsdp", axis=0)
+        chunk_weights.append(regroup(gathered, model_width, inner_width))
+        return packed
 
     ru = model_width // shard_count
     kv_cols = lookup_plugin_target.shape[1]
@@ -1082,44 +1177,41 @@
         size = a.shape[axis] // dp_count
         return lax.dynamic_slice_in_dim(a, dp_rank * size, size, axis)
 
+    before_it = gather_chunk(0, CHUNKS[0], None, cot_from)
+    parts = (triple_coefficients, attend_exit_coefficients, others)
+    parts, before_it = lax.optimization_barrier((parts, before_it))
     part = jnp.concatenate(
         [
-            columns_to_rows(own_part(lay_out_columns(triple_coefficients), 1)),
-            columns_to_rows(own_part(attend_exit_coefficients, 1)),
-            own_part(others, 0),
+            columns_to_rows(own_part(lay_out_columns(parts[0]), 1)),
+            columns_to_rows(own_part(parts[1], 1)),
+            own_part(parts[2], 0),
         ],
         axis=0,
     )
-    part_all = lax.all_gather(part, "fsdp", axis=0)
-    (part_all, cot_from, rank, chosen, masks, own_mask, section_cols, cos_table, sin_table) = (
-        lax.optimization_barrier(
-            (part_all, cot_from, rank, chosen, masks, own_mask, section_cols, cos_table, sin_table)
-        )
-    )
-    mine = lax.dynamic_slice_in_dim(part_all, core * (shard_count // 2), shard_count // 2, 0)
-    near = [exchange(mine, k) for k in peers[1:]]
+    if shard_count == SHARDS:
+        chips = [part]
+        for d in range(1, shard_count // 2):
+            pairs = [(i, i ^ (2 * d)) for i in range(shard_count)]
+            chips.append(lax.ppermute(part, "fsdp", pairs))
+        mine = jnp.stack(chips)
+    else:
+        part_all = lax.all_gather(part, "fsdp", axis=0)
+        mine = part_all.reshape(shard_count // 2, 2, *part.shape)
+        mine = lax.dynamic_index_in_dim(mine, core, 1, keepdims=False)
+    rank_far = jnp.concatenate([rank_last[:, :last], rank_last[:, 3 * last :]], axis=1)
+    (mine, cot_from, rank, rank_last, rank_far, chosen, masks, own_mask, me) = lax.optimization_barrier(
+        (mine, cot_from, rank, rank_last, rank_far, chosen, masks, own_mask, me)
+    )
+    half = mine.shape[0] // 2
+    beside = [exchange(mine, 1), exchange(mine, 2)]
+    near = [mine, *beside, exchange(beside[1][:half], 1), exchange(beside[0][half:], 2)]
     pairs = [(i, i ^ 1) for i in range(shard_count)]
     far = [lax.ppermute(a, "fsdp", pairs) for a in near]
-
-    chunk_weights = []
-    first = 0
-    before_it = part
-    for size in CHUNKS:
-        here = slice(first, first + size)
-        shards = (
-            branch_widen_coefficients[here],
-            branch_contract_coefficients[here],
-            branch_plugin_source[here],
-            branch_plugin_target[here],
-            contract_plugin_source[here],
-            contract_plugin_target[here],
-        )
-        if first:
-            shards, cot_from = lax.optimization_barrier((shards, cot_from))
-        shards, before_it = lax.optimization_barrier((shards, before_it))
-        before_it = pack_experts(*shards)
-        gathered = lax.all_gather(before_it, "fsdp", axis=0)
-        chunk_weights.append(regroup(gathered, model_width, inner_width))
+    places = [(k, c, first) for c in range(2) for k, first in ((0, 0), (1, 0), (2, 0), (3, 0), (3, half))]
+
+    first = CHUNKS[0]
+    for size in CHUNKS[1:]:
+        before_it = gather_chunk(first, size, before_it, cot_from)
         first += size
 
     later, near = lax.optimization_barrier((cot_rows[1:], near))
@@ -1127,7 +1219,7 @@
         cot_from[k] += [exchange(a, k) for a in later]
 
     qkv, exit_full, other_full = unpack(
-        me, part_all, near, far, model_width, triple_coefficients.shape[1], other_slots
+        me, near + far, places, dp_count, model_width, triple_coefficients.shape[1], other_slots
     )
     kv_out = other_full[4].reshape(shard_count, 2, kv_cols, LANES)
     k_out = kv_out[:, 0].reshape(-1, LANES)
@@ -1146,18 +1238,25 @@
         if m > 0:
             me_then, sent[-1] = lax.optimization_barrier((me_then, sent[-1]))
         out = attn_forward(
-            m, me_then, layer_entering_state, chosen, rank, section_rows, section_cols, own_mask,
+            m, me_then, layer_entering_state, chosen, rank, section_rows, own_mask,
             cos_table, sin_table, weights, dp_count,
         )
-        saved.append(out[:-dp_count])
-        sent.append(list(out[-dp_count:]))
+        saved.append(out[: 1 - dp_count])
+        sent.append(list(out[1 - dp_count :]))
     first_rows, cot_from = lax.optimization_barrier((sent[0], cot_from))
     sent[0] = first_rows
     rows_from = None
+    half = EXTRA + seq_len // 2
     for m in micro:
         if m > 0:
             sent[m], rows_from = lax.optimization_barrier((sent[m], rows_from))
-        rows_from = [exchange(sent[m][k], k) for k in peers]
+        beside = [exchange(sent[m][1], 1), exchange(sent[m][2], 2)]
+        if m + 1 < micro_count:
+            beside, sent[m + 1] = lax.optimization_barrier((beside, sent[m + 1]))
+        else:
+            beside, slots[-1] = lax.optimization_barrier((beside, slots[-1]))
+        rows_from = [sent[m][0], *beside]
+        rows_from += [exchange(beside[1][:half], 1), exchange(beside[0][half : EXTRA + seq_len], 2)]
         cots = [cot_from[k][m] for k in peers]
         slots.append(dispatch(rows_from, cots, local_experts, capacity))
 
@@ -1169,7 +1268,7 @@
         count = head if first < head else local_experts - head
         outs.append(
             expert_chunk(
-                slots, chunk, masks, first, inner_width, at, count, grads, products, False, False
+                slots, chunk, masks, first, inner_width, at, count, grads, products, False
             )
         )
         grads, products = outs[-1][2 * n], list(outs[-1][2 * n + 1 :])
@@ -1184,32 +1283,32 @@
     def rows_of(place):
         return [o[place] for o in outs]
 
-    far_backs = combine(slots, rows_of(n + 3), 3, apart=True)
-    passed = [exchange(far_backs[0], 1), exchange(far_backs[1], 2)]
-    far_mixes = combine(slots, rows_of(3), 3, apart=True)
+    back_rows = [rows_of(n + k) for k in range(4)]
+    far_backs = combine(slots, [(3, back_rows[3], m) for m in micro], apart=True)
+    passed = [exchange(a, 1 + m) for m, a in enumerate(far_backs)]
+    far_mixes = combine(slots, [(3, rows_of(3), m) for m in micro], apart=True)
     far_mixes, passed = lax.optimization_barrier((far_mixes, passed))
-    backs = {
-        1: combine(slots, rows_of(n + 1), 1, added=1, add=passed[1]),
-        2: combine(slots, rows_of(n + 2), 2, added=0, add=passed[0]),
-    }
-    passed_mixes = [exchange(far_mixes[0], 1), exchange(far_mixes[1], 2)]
-    backs[0] = combine(slots, rows_of(n), 0)
-    back_home = [backs[0], exchange(backs[1], 1), exchange(backs[2], 2)]
-    mixes = {
-        0: combine(slots, rows_of(0), 0),
-        1: combine(slots, rows_of(1), 1, added=1, add=passed_mixes[1]),
-        2: combine(slots, rows_of(2), 2, added=0, add=passed_mixes[0]),
-    }
-    chunk, _ = lax.optimization_barrier((chunk_weights[-1], (backs, mixes)))
-    tails = []
+    backs = [
+        combine(slots, [(k, back_rows[k], m) for m in micro], add=(2 - k, passed[2 - k], 0))
+        for k in (1, 2)
+    ]
+    passed_mixes = [exchange(a, 1 + m) for m, a in enumerate(far_mixes)]
+    back_home = [exchange(a, k) for k, a in zip((1, 2), backs)]
+    own_back = combine(slots, [(0, back_rows[0], m) for m in micro])
+    own_mix = combine(slots, [(0, rows_of(0), m) for m in micro])
+    chunk, _, passed_mixes = lax.optimization_barrier(
+        (chunk_weights[-1], (backs, own_back, own_mix), passed_mixes)
+    )
+    tails, filled = [], []
+
     for m in micro:
         if m == micro_count - 1:
             chunk, back_home = lax.optimization_barrier((chunk, back_home))
         out = expert_chunk(
             [slots[m]], chunk, masks[m : m + 1], first, inner_width, first - head,
-            local_experts - head, grads, [products[m]], m > 0, True,
+            local_experts - head, grads, [products[m]], m > 0, (micro_count, m), filled,
         )
-        grads = out[2 * n]
+        filled, grads = list(out[:n]), out[2 * n]
         tails.append(out)
     back_last = []
     for m in micro:
@@ -1224,33 +1323,49 @@
         tail_sum = lax.psum_scatter(grads, "fsdp", scatter_dimension=0, tiled=False)
     else:
         tail_sum = grads
+    outs.append(filled)
+    mix_rows = [rows_of(k) for k in range(3)]
     older = []
     for m in micro:
         if m == micro_count - 1:
-            mixes, mix_tails, back_last[m], head_sum, older = lax.optimization_barrier(
-                (mixes, [list(t[:n]) for t in tails], back_last[m], head_sum, older)
+            back_last[m], head_sum, older, mix_rows = lax.optimization_barrier(
+                (back_last[m], head_sum, older, mix_rows)
             )
+            mixes = [
+                combine(slots, [(k, mix_rows[k], i) for i in micro], add=(2 - k, passed_mixes[2 - k], 0))
+                for k in (1, 2)
+            ]
+            mix_home = [exchange(a, k) for k, a in zip((1, 2), mixes)]
+            back_last[m], mixes, far_last = lax.optimization_barrier(
+                (back_last[m], mixes, filled[3])
+            )
+            far_last = exchange(far_last, 3)
         grad_input, attn_grads = attn_backward(
-            m, last, me, layer_entering_state, exit_cotangent, section_rows, section_cols, own_mask,
-            cos_table, sin_table, weights, saved[m], sent[m][0], rank_last, back_home, back_last[m],
+            m, last, me, layer_entering_state, exit_cotangent, section_rows, own_mask,
+            cos_table, sin_table, weights, saved[m], sent[m][0], rank_last, [own_back, *back_home], back_last[m],
             older,
         )
         older = [attn_grads, grad_input]
-    mix_home = [mixes[0], exchange(mixes[1], 1), exchange(mixes[2], 2)]
-    mix_last = [[exchange(t[k], k) for k in peers] for t in mix_tails]
-    attn_grads, mix_home, tail_sum = lax.optimization_barrier((attn_grads, mix_home, tail_sum))
+    attn_grads, mix_home = lax.optimization_barrier((attn_grads, mix_home))
+
+    if shard_count == SHARDS:
+        received = lax.all_to_all(attn_grads, "fsdp", split_axis=0, concat_axis=0, tiled=True)
+        expert_out = finish_experts([head_sum, tail_sum], model_width, inner_width)
+        received, expert_out = lax.optimization_barrier((received, expert_out))
+        own_sum = gather_grads(received)
+        attn_out = finish_attention(shard, [exchange(own_sum, k) for k in peers], expert_count)
+    else:
+        expert_out = scatter_experts([head_sum, tail_sum], inner_width)
+        holds = [(column_holder == me[3 + m]).astype(f32)[:, None] for m in micro]
+        attn_out = scatter_attention(attn_grads, holds, expert_count)
     block_out = []
     for m in micro:
-        block_out = [add_mixture(m, saved[m][0], rank_last, mix_home, mix_last[m], block_out)]
-
-    sizes = attn_grad_rows(model_width)
-    if shard_count == SHARDS:
-        expert_out = finish_experts([head_sum, tail_sum], model_width, inner_width)
-        own_sum = lax.psum_scatter(attn_grads, "fsdp", scatter_dimension=0, tiled=False)
-        attn_out = finish_attention([exchange(own_sum, k) for k in peers], sizes, expert_count)
-    else:
-        expert_out = scatter_experts([head_sum, tail_sum], inner_width)
-        attn_out = scatter_attention(attn_grads, sizes, expert_count)
+        block_out = [
+            add_mixture(
+                m, micro_count, saved[m][0], rank_far, filled[0], far_last, [own_mix, *mix_home],
+                block_out,
+            )
+        ]
     return (*block_out, grad_input, *attn_out, *expert_out)
 
 
@@ -1277,27 +1392,23 @@
     )
 
 
-def scatter_attention(packed, sizes, experts):
-    pieces, at = [], 0
-    for size in sizes:
-        pieces.append(packed[:, at : at + size].astype(f32))
-        at += size
-
-    def by_rows(a):
-        return a.reshape(-1, LANES)
-
-    def by_columns(a):
-        return jnp.swapaxes(a, 0, 1).reshape(a.shape[1], -1)
-
+def scatter_attention(packed, holds, experts):
+    dense = [0.0] * 9
+    for m, hold in enumerate(holds):
+        for i in range(9):
+            at = m * GRAD_ROWS + i * REDUCED_DIM
+            piece = jnp.swapaxes(packed[:, at : at + REDUCED_DIM], 0, 1).astype(f32)
+            dense[i] = dense[i] + jnp.tile(piece, (PLUGIN_CHOICES, 1, 1)) * hold[:, :, None]
+    flat = [a.reshape(a.shape[0], -1) for a in dense]
     full = (
-        (by_columns(pieces[0]).T, 0),
-        (by_rows(pieces[1]).T, 1),
-        (by_rows(pieces[2]).T, 1),
-        (by_rows(pieces[3]).T, 1),
-        (by_rows(pieces[4]), 0),
-        (by_columns(pieces[5]), 1),
-        (by_columns(pieces[6]).T, 0),
-        (by_rows(pieces[7])[:, :experts], 0),
+        (jnp.concatenate([a.T for a in flat[:3]], axis=1), 0),
+        (flat[3], 1),
+        (dense[4][..., :HD].reshape(LANES, -1), 1),
+        (dense[4][..., HD:].reshape(LANES, -1), 1),
+        (flat[5].T, 0),
+        (flat[6], 1),
+        (flat[7].T, 0),
+        (dense[8][:, 0, :experts], 0),
     )
     return [
         lax.psum(lax.psum_scatter(a, "fsdp", scatter_dimension=d, tiled=True), "dp")

time: 574 us -> 537 us (0.936)
  waiting for transfers between devices: 154 us -> 121 us
  local copies, waits for them, and re-layouts: 39.5 us -> 29.6 us
    ppermute x38 -> x36, waiting for transfers between devices: 136 us -> 87.4 us  [exchange(): return lax.ppermute(a, 'dp', [(i, i ^ k) for i in range(size)])]
    reduce_scatter x1 -> x0, waiting for transfers between devices: 18.4 us -> none  [local(): lax.psum_scatter(attn_grads, 'fsdp', scatter_dimension=0, tiled=False)]
    ppermute x0 -> x3, waiting for transfers between devices: none -> 13.9 us  [local(): chips.append(lax.ppermute(part, 'fsdp', pairs))]
    all_to_all x0 -> x1, waiting for transfers between devices: none -> 11.5 us  [local(): lax.all_to_all(attn_grads, 'fsdp', split_axis=0, concat_axis=0, tiled=True)]
    all_gather x4 -> x3, waiting for transfers between devices: 0.02 us -> 8.11 us  [gather_chunk(): gathered = lax.all_gather(packed, 'fsdp', axis=0)]
    ppermute x38 -> x36, starting transfers between devices: 52 us -> 44 us  [exchange(): return lax.ppermute(a, 'dp', [(i, i ^ k) for i in range(size)])]
    ppermute x0 -> x3, starting transfers between devices: none -> 7.56 us  [local(): chips.append(lax.ppermute(part, 'fsdp', pairs))]
    pallas_call x14 -> x15, Pallas kernels: 109 us -> 112 us  [the longest x2 50.8 us: attn_backward(): pl.pallas_call(functools.partial(attn_backward_kernel, step, peers, last,...]
  transfers between devices with their start and end apart: 48 -> 50, of which waited for: 16 -> 21; matrix products, arithmetic and copies ran while one was open for 6% -> 5% of each run, Pallas kernels for 52% -> 56%
where the time goes in v3:
time: 537 us; the launch traced here: 532 us
  Pallas kernels  298 us (55%)
  waiting for transfers between devices  121 us (23%)
  starting transfers between devices  56.9 us (11%)
  local copies, waits for them, and re-layouts  29.6 us (6%)
  between operations  15.3 us (3%)
  other arithmetic  10.8 us (2%)
    pallas_call x4, Pallas kernels, expert_chunk(): pl.pallas_call(functools.partial(expert_kernel, first, micro, len(held),...  119 us
    ppermute x36, waiting for transfers between devices, exchange(): return lax.ppermute(a, 'dp', [(i, i ^ k) for i in range(size)])  87.4 us
    pallas_call x2, Pallas kernels, attn_backward(): pl.pallas_call(functools.partial(attn_backward_kernel, step, peers, last,...  50.8 us
    ppermute x36, starting transfers between devices, exchange(): return lax.ppermute(a, 'dp', [(i, i ^ k) for i in range(size)])  44 us
    pallas_call x8, Pallas kernels, combine(): pl.pallas_call(functools.partial(combine_kernel, chunks, len(jobs), added...  39 us
    pallas_call x2, Pallas kernels, attn_forward(): pl.pallas_call(attn_forward_kernel, grid=(1,), in_specs=[pl.BlockSpec(mem...  36 us
    pallas_call x2, Pallas kernels, dispatch(): pl.pallas_call(functools.partial(dispatch_kernel, peers, capacity), grid=...  27.2 us
    unnamed x176, local copies, waits for them, and re-layouts  14.3 us
  transfers between devices with their start and end apart: 50, of which 21 were waited for; matrix products, arithmetic and copies ran while one was open for 5% of the time, Pallas kernels for 56%

profile of v3, /device:TPU:0, one launch (start us, length us, event | category | flops | bytes accessed | tf_op | source)
XLA Modules:
  0.0 531.7 jit_solution(7893627341087072338)
XLA Ops:
  42.3 13.9 %collective-permute-done.2 = bf16[1152,128]{1,0:T(8,128)(2,1)} collective-permute-done((bf16[1152,128]{1,0:T(8,128)(2,1)}, bf16[1152,128]{1,0:T(8,128)(2,1)}, u32[]{:S(2)}, u32[]{:S(2)}) %collective-permute-start.2) | collective-permute-done | bytes 294944 | tf_op jit(solution)/shard_map/ppermute | solution.py:1195
  66.6 23.9 %collective-permute-done.7.refs_2_ = bf16[4,1152,128]{2,1,0:T(8,128)(2,1)S(1)} collective-permute-done((bf16[4,1152,128]{2,1,0:T(8,128)(2,1)S(1)}, bf16[4,1152,128]{2,1,0:T(8,128)(2,1)S(1)}, u32[]{:S(2)}, u32[]{:S(2)}) %collective-permute-start.7) | collective-permute-done | bytes 1179680 | tf_op jit(solution)/shard_map/ppermute | solution.py:1054
  94.3 9.0 %collective-permute-done.8.refs_3_ = bf16[2,1152,128]{2,1,0:T(8,128)(2,1)S(1)} collective-permute-done((bf16[2,1152,128]{2,1,0:T(8,128)(2,1)S(1)}, bf16[2,1152,128]{2,1,0:T(8,128)(2,1)S(1)}, u32[]{:S(2)}, u32[]{:S(2)}) %collective-permute-start.8) | collective-permute-done | bytes 589856 | tf_op jit(solution)/shard_map/ppermute | solution.py:1054
  109.9 9.6 %unpack.1 = (bf16[1024,2048]{1,0:T(8,128)(2,1)}, bf16[1024,1024]{1,0:T(8,128)(2,1)}, bf16[12,1024,128]{2,1,0:T(8,128)(2,1)}) custom-call(s32[5]{0:T(128)} %pad_add_fusion.me_ref, bf16[4,1152,128]{2,1,0:T(8,128)(2,1)} %copy-done.3, bf16[4,1152,128]{2,1,0:T(8,128)(2,1)} %copy-done.5, bf16[4,1152,128]{2,1,0:T(8,128)(2,1)} %copy-done.4, ...), custom_call_target="tpu_custom_call" | custom-call | tf_op jit(solution)/shard_map/unpack/pallas_call | solution.py:553
  122.6 18.2 %attention_forward.2 = (f32[384,1024]{1,0:T(8,128)}, bf16[384,1024]{1,0:T(8,128)(2,1)}, bf16[384,512]{1,0:T(8,128)(2,1)}, bf16[384,512]{1,0:T(8,128)(2,1)}, f32[...) custom-call(s32[5]{0:T(128)} %pad_add_fusion.me_ref, ...), custom_call_target="tpu_custom_call" | custom-call | flops 5234491392 | bytes 20971520 | tf_op jit(solution)/shard_map/attention_forward/pallas_call | solution.py:671
  145.9 17.8 %attention_forward.3 = (f32[384,1024]{1,0:T(8,128)}, bf16[384,1024]{1,0:T(8,128)(2,1)}, bf16[384,512]{1,0:T(8,128)(2,1)}, bf16[384,512]{1,0:T(8,128)(2,1)}, f32[...) custom-call(s32[5]{0:T(128)} %pad_add_fusion.me_ref, ...), custom_call_target="tpu_custom_call" | custom-call | flops 5234491392 | bytes 20971520 | tf_op jit(solution)/shard_map/attention_forward/pallas_call | solution.py:671
  166.6 7.3 %collective-permute-done.21.refs_4_ = bf16[192,1024]{1,0:T(8,128)(2,1)S(1)} collective-permute-done((bf16[192,1024]{1,0:T(8,128)(2,1)S(1)}, bf16[192,1024]{1,0:T(8,128)(2,1)S(1)}, u32[]{:S(2)}, u32[]{:S(2)}) %collective-permute-start.21) | collective-permute-done | bytes 393248 | tf_op jit(solution)/shard_map/ppermute | solution.py:1054
  176.4 13.7 %dispatch.2 = (bf16[4,8,112,1024]{3,2,1,0:T(8,128)(2,1)}, bf16[4,8,112,1024]{3,2,1,0:T(8,128)(2,1)}, f32[4,8,112,128]{3,2,1,0:T(8,128)}, f32[4,8,384]{2,1,0:T(8,128)}, f32[4,384,128]{2,1,0:T(8,128)}) custom-call(bf16[416,1024]{1,0:T(8,128)(2,1)} %get-tuple-element.279.refs_0_.moe_ref, bf16[416,1024]{1,0:T(8,128)(2,1)} %copy-done.37, ...), custom_call_target="tpu_custom_call" | custom-call | flops 5637144576 | bytes 29360128 | tf_op jit(solution)/shard_map/dispatch/pallas_call | solution.py:163
  196.6 6.8 %collective-permute-done.25.refs_4_ = bf16[192,1024]{1,0:T(8,128)(2,1)S(1)} collective-permute-done((bf16[192,1024]{1,0:T(8,128)(2,1)S(1)}, bf16[192,1024]{1,0:T(8,128)(2,1)S(1)}, u32[]{:S(2)}, u32[]{:S(2)}) %collective-permute-start.25) | collective-permute-done | bytes 393248 | tf_op jit(solution)/shard_map/ppermute | solution.py:1054
  205.0 13.6 %dispatch.3 = (bf16[4,8,112,1024]{3,2,1,0:T(8,128)(2,1)}, bf16[4,8,112,1024]{3,2,1,0:T(8,128)(2,1)}, f32[4,8,112,128]{3,2,1,0:T(8,128)}, f32[4,8,384]{2,1,0:T(8,128)}, f32[4,384,128]{2,1,0:T(8,128)}) custom-call(bf16[416,1024]{1,0:T(8,128)(2,1)} %get-tuple-element.282.refs_0_.moe_ref, bf16[416,1024]{1,0:T(8,128)(2,1)} %copy-done.38, ...), custom_call_target="tpu_custom_call" | custom-call | flops 5637144576 | bytes 29360128 | tf_op jit(solution)/shard_map/dispatch/pallas_call | solution.py:163
  219.1 52.9 %experts.4 = (bf16[2,4,112,1024]{3,2,1,0:T(8,128)(2,1)}, bf16[2,4,112,1024]{3,2,1,0:T(8,128)(2,1)}, bf16[2,4,112,1024]{3,2,1,0:T(8,128)(2,1)}, bf16[2,4,112,1024...) custom-call(f32[4,8,384]{2,1,0:T(8,128)} %get-tuple-element.312.refs, ...), custom_call_target="tpu_custom_call" | custom-call | flops 35840000000 | bytes 81264640 | tf_op jit(solution)/shard_map/experts/pallas_call | solution.py:342
  274.8 29.8 %experts.5 = (bf16[2,2,112,1024]{3,2,1,0:T(8,128)(2,1)}, bf16[2,2,112,1024]{3,2,1,0:T(8,128)(2,1)}, bf16[2,2,112,1024]{3,2,1,0:T(8,128)(2,1)}, bf16[2,2,112,1024...) custom-call(f32[4,8,384]{2,1,0:T(8,128)} %get-tuple-element.312.refs, ...), custom_call_target="tpu_custom_call" | custom-call | flops 17920000000 | bytes 40632320 | tf_op jit(solution)/shard_map/experts/pallas_call | solution.py:342
  316.3 12.6 %collective-permute-done.26.refs_6_ = bf16[384,1024]{1,0:T(8,128)(2,1)S(1)} collective-permute-done((bf16[384,1024]{1,0:T(8,128)(2,1)}, bf16[384,1024]{1,0:T(8,128)(2,1)S(1)}, u32[]{:S(2)}, u32[]{:S(2)}) %collective-permute-start.26) | collective-permute-done | bytes 786464 | tf_op jit(solution)/shard_map/ppermute | solution.py:1054
  337.5 4.8 combine.10
  353.7 5.5 %all-gather.7.cloned.1.call-done = bf16[16,2112,128]{2,1,0:T(8,128)(2,1)} async-done(((bf16[2,2112,128]{2,1,0:T(8,128)(2,1)}), bf16[16,2112,128]{2,1,0:T(8,128)(2,1)}) %all-gather.7.cloned.1.call-update) | async-done | bytes 8650768 | tf_op jit(solution)/shard_map/all_gather | solution.py:1142
  359.2 17.8 %experts.6 = (bf16[2,2,112,1024]{3,2,1,0:T(8,128)(2,1)}, bf16[2,2,112,1024]{3,2,1,0:T(8,128)(2,1)}, bf16[2,2,112,1024]{3,2,1,0:T(8,128)(2,1)}, bf16[2,2,112,1024...) custom-call(f32[4,8,384]{2,1,0:T(8,128)} %get-tuple-element.312.refs, ...), custom_call_target="tpu_custom_call", output_to_operand_aliasing={{8}: (7, {})} | custom-call | flops 8960000000 | bytes 33292288 | tf_op jit(solution)/shard_map/experts/pallas_call | solution.py:342
  377.1 6.2 %collective-permute-done.31.refs_2_ = bf16[768,1024]{1,0:T(8,128)(2,1)} collective-permute-done((bf16[768,1024]{1,0:T(8,128)(2,1)}, bf16[768,1024]{1,0:T(8,128)(2,1)}, u32[]{:S(2)}, u32[]{:S(2)}) %collective-permute-start.31) | collective-permute-done | bytes 1572896 | tf_op jit(solution)/shard_map/ppermute | solution.py:1054
  386.7 18.3 %experts.7 = (bf16[2,2,112,1024]{3,2,1,0:T(8,128)(2,1)}, bf16[2,2,112,1024]{3,2,1,0:T(8,128)(2,1)}, bf16[2,2,112,1024]{3,2,1,0:T(8,128)(2,1)}, bf16[2,2,112,1024...) custom-call(f32[4,8,384]{2,1,0:T(8,128)} %get-tuple-element.300.refs, ...), custom_call_target="tpu_custom_call", output_to_operand_aliasing={{8}: (7, {}), {0}: (8, {}), {1}: (9, {}), {2}: (10, {}), {3... | custom-call | flops 8960000000 | bytes 33292288 | tf_op jit(solution)/shard_map/experts/pallas_call | solution.py:342
  411.0 25.3 %attention_backward.2 = (bf16[768,1024]{1,0:T(8,128)(2,1)}, bf16[8,144,128]{2,1,0:T(8,128)(2,1)}) custom-call(s32[5]{0:T(128)} %pad_add_fusion.me_ref, bf16[768,1024]{1,0:T(8,128)(2,1)} %x_ref.7, bf16[768,1024]{1,0:T(8,128)(2,1)} %cot_ref.3, s32[2,1,384]{2,1,0:T(1,128)} %broadcast_in_dim.30.row_ref, f32[2,1,128]{2,1,0:T(1,128)} %copy-done.56, ...), custom_call_target="tpu_custom_call" | custom-call | flops 7851737088 | bytes 31457280 | tf_op jit(solution)/shard_map/attention_backward/pallas_call | solution.py:873
  436.3 5.7 %combine.15 = bf16[768,1024]{1,0:T(8,128)(2,1)} custom-call(f32[4,384,128]{2,1,0:T(8,128)} %get-tuple-element.310.refs_0_, f32[4,384,128]{2,1,0:T(8,128)} %get-tuple-element.311.refs_1_, bf16[2,4,112,1024]{3,2,1,0:T(8,128)(2,1)} %get-tuple-element.407.refs_2_.refs_5_, bf16[2,2,112,1024]{3,2,1,0:T(8,128)(2,1)} %get-tuple-element.408.refs_3_.refs_6_, ...), custom_call_target="tpu_custom_call" | custom-call | flops 1409286144 | bytes 5505024 | tf_op jit(solution)/shard_map/combine/pallas_call | solution.py:426
  443.7 5.6 %combine.14 = bf16[768,1024]{1,0:T(8,128)(2,1)} custom-call(f32[4,384,128]{2,1,0:T(8,128)} %get-tuple-element.310.refs_0_, f32[4,384,128]{2,1,0:T(8,128)} %get-tuple-element.311.refs_1_, bf16[2,4,112,1024]{3,2,1,0:T(8,128)(2,1)} %get-tuple-element.403.refs_2_.refs_5_, bf16[2,2,112,1024]{3,2,1,0:T(8,128)(2,1)} %get-tuple-element.404.refs_3_.refs_6_, ...), custom_call_target="tpu_custom_call" | custom-call | flops 1409286144 | bytes 5505024 | tf_op jit(solution)/shard_map/combine/pallas_call | solution.py:426
  450.1 25.5 %attention_backward.3 = (bf16[768,1024]{1,0:T(8,128)(2,1)}, bf16[8,288,128]{2,1,0:T(8,128)(2,1)}) custom-call(s32[5]{0:T(128)} %pad_add_fusion.me_ref, bf16[768,1024]{1,0:T(8,128)(2,1)} %x_ref.7, bf16[768,1024]{1,0:T(8,128)(2,1)} %cot_ref.3, s32[2,1,384]{2,1,0:T(1,128)} %broadcast_in_dim.30.row_ref, ...), custom_call_target="tpu_custom_call", output_to_operand_aliasing={{0}: (34, {})} | custom-call | flops 7851737088 | bytes 31457280 | tf_op jit(solution)/shard_map/attention_backward/pallas_call | solution.py:873
  475.7 5.4 %collective-permute-done.39.refs_1_ = bf16[768,1024]{1,0:T(8,128)(2,1)S(1)} collective-permute-done((bf16[768,1024]{1,0:T(8,128)(2,1)}, bf16[768,1024]{1,0:T(8,128)(2,1)S(1)}, u32[]{:S(2)}, u32[]{:S(2)}) %collective-permute-start.39) | collective-permute-done | bytes 1572896 | tf_op jit(solution)/shard_map/ppermute | solution.py:1054
  490.8 11.5 %all-to-all-done.g_ref = bf16[8,288,128]{2,1,0:T(8,128)(2,1)} async-done(((bf16[8,288,128]{2,1,0:T(8,128)(2,1)}), bf16[8,288,128]{2,1,0:T(8,128)(2,1)}, u32[]{:S(2)}, u32[]{:S(2)}) %all-to-all-start) | async-done | bytes 589856 | tf_op jit(solution)/shard_map/all_to_all | solution.py:1352
  (350 shorter events, 155.6 us)
Async XLA Ops:
  7.2 211.4 %all-gather.9.cloned.1.call-start = ((), (), s32[]{:S(2)}) async-start(), calls=%async_computation.6 | async-start | bytes 19464192 | tf_op jit(solution)/shard_map/all_gather | solution.py:1142
  12.5 262.2 %all-gather.11.cloned.1.call-start = ((), (), s32[]{:S(2)}) async-start(), calls=%async_computation.7 | async-start | bytes 9732096 | tf_op jit(solution)/shard_map/all_gather | solution.py:1142
  22.8 34.6 %collective-permute-start.3 = (bf16[384,1024]{1,0:T(8,128)(2,1)}, bf16[384,1024]{1,0:T(8,128)(2,1)}, u32[]{:S(2)}, u32[]{:S(2)}) collective-permute-start(bf16[384,1024]{1,0:T(8,128)(2,1)} %get-tuple-element.285.refs_5_), channel_id=1, source_target_pairs={{0,8},{8,0},{16,24},{24,16},{1,9},{9,1},{17,25},{25,17},{2,10},{10... | collective-permute-start | bytes 2359304 | tf_op jit(solution)/shard_map/ppermute | solution.py:1054
  24.3 35.6 %collective-permute-start.4 = (bf16[384,1024]{1,0:T(8,128)(2,1)}, bf16[384,1024]{1,0:T(8,128)(2,1)}, u32[]{:S(2)}, u32[]{:S(2)}) collective-permute-start(bf16[384,1024]{1,0:T(8,128)(2,1)} %get-tuple-element.285.refs_5_), channel_id=1, source_target_pairs={{0,16},{8,24},{16,0},{24,8},{1,17},{9,25},{17,1},{25,9},{2,18},{10... | collective-permute-start | bytes 2359304 | tf_op jit(solution)/shard_map/ppermute | solution.py:1054
  25.8 34.1 %collective-permute-start.5 = (bf16[384,1024]{1,0:T(8,128)(2,1)}, bf16[384,1024]{1,0:T(8,128)(2,1)}, u32[]{:S(2)}, u32[]{:S(2)}) collective-permute-start(bf16[384,1024]{1,0:T(8,128)(2,1)} %get-tuple-element.285.refs_5_), channel_id=1, source_target_pairs={{0,24},{8,16},{16,8},{24,0},{1,25},{9,17},{17,9},{25,1},{2,26},{10... | collective-permute-start | bytes 2359304 | tf_op jit(solution)/shard_map/ppermute | solution.py:1054
  62.0 297.2 %all-gather.7.cloned.1.call-start = ((), (), s32[]{:S(2)}) async-start(), calls=%async_computation.5 | async-start | bytes 9732096 | tf_op jit(solution)/shard_map/all_gather | solution.py:1142
  64.2 372.1 %reduce-scatter.3.cloned.1.call-start = ((), (), s32[]{:S(2)}) async-start(), calls=%async_computation.3 | async-start | bytes 5308416 | tf_op jit(solution)/shard_map/reduce_scatter | solution.py:1279
  64.4 26.1 %collective-permute-start.7 = (bf16[4,1152,128]{2,1,0:T(8,128)(2,1)S(1)}, bf16[4,1152,128]{2,1,0:T(8,128)(2,1)S(1)}, u32[]{:S(2)}, u32[]{:S(2)}) collective-permute-start(bf16[4,1152,128]{2,1,0:T(8,128)(2,1)S(1)} %pad_maximum_fusion.refs_0_), channel_id=1, source_target_pairs={{0,16},{8,24},{16,0},{24,8},{1,17},{9,25},{17,1},{25,9},{2,18},{10... | collective-permute-start | bytes 3538952 | tf_op jit(solution)/shard_map/ppermute | solution.py:1054
  66.0 26.0 %collective-permute-start.6 = (bf16[4,1152,128]{2,1,0:T(8,128)(2,1)S(1)}, bf16[4,1152,128]{2,1,0:T(8,128)(2,1)S(1)}, u32[]{:S(2)}, u32[]{:S(2)}) collective-permute-start(bf16[4,1152,128]{2,1,0:T(8,128)(2,1)S(1)} %pad_maximum_fusion.refs_0_), channel_id=1, source_target_pairs={{0,8},{8,0},{16,24},{24,16},{1,9},{9,1},{17,25},{25,17},{2,10},{10... | collective-permute-start | bytes 3538952 | tf_op jit(solution)/shard_map/ppermute | solution.py:1054
  66.6 38.8 %collective-permute-start.10 = (bf16[4,1152,128]{2,1,0:T(8,128)(2,1)S(1)}, bf16[4,1152,128]{2,1,0:T(8,128)(2,1)S(1)}, u32[]{:S(2)}, u32[]{:S(2)}) collective-permute-start(bf16[4,1152,128]{2,1,0:T(8,128)(2,1)S(1)} %pad_maximum_fusion.refs_0_), channel_id=1, source_target_pairs={{0,1},{1,0},{2,3},{3,2},{4,5},{5,4},{6,7},{7,6},{8,9},{9,8},{10,11... | collective-permute-start | bytes 3538952 | tf_op jit(solution)/shard_map/ppermute | solution.py:1209
  105.3 35.5 %collective-permute-start.15 = (bf16[384,1024]{1,0:T(8,128)(2,1)}, bf16[384,1024]{1,0:T(8,128)(2,1)S(1)}, u32[]{:S(2)}, u32[]{:S(2)}) collective-permute-start(bf16[384,1024]{1,0:T(8,128)(2,1)} %get-tuple-element.296.refs_5_), channel_id=1, source_target_pairs={{0,8},{8,0},{16,24},{24,16},{1,9},{9,1},{17,25},{25,17},{2,10},{10... | collective-permute-start | bytes 2359304 | tf_op jit(solution)/shard_map/ppermute | solution.py:1054
  106.0 36.4 %collective-permute-start.16 = (bf16[384,1024]{1,0:T(8,128)(2,1)}, bf16[384,1024]{1,0:T(8,128)(2,1)S(1)}, u32[]{:S(2)}, u32[]{:S(2)}) collective-permute-start(bf16[384,1024]{1,0:T(8,128)(2,1)} %get-tuple-element.296.refs_5_), channel_id=1, source_target_pairs={{0,16},{8,24},{16,0},{24,8},{1,17},{9,25},{17,1},{25,9},{2,18},{10... | collective-permute-start | bytes 2359304 | tf_op jit(solution)/shard_map/ppermute | solution.py:1054
  107.5 35.0 %collective-permute-start.17 = (bf16[384,1024]{1,0:T(8,128)(2,1)}, bf16[384,1024]{1,0:T(8,128)(2,1)}, u32[]{:S(2)}, u32[]{:S(2)}) collective-permute-start(bf16[384,1024]{1,0:T(8,128)(2,1)} %get-tuple-element.296.refs_5_), channel_id=1, source_target_pairs={{0,24},{8,16},{16,8},{24,0},{1,25},{9,17},{17,9},{25,1},{2,26},{10... | collective-permute-start | bytes 2359304 | tf_op jit(solution)/shard_map/ppermute | solution.py:1054
  272.1 215.5 %reduce-scatter.5.cloned.1.call-start = ((), (), s32[]{:S(2)}) async-start(), calls=%async_computation.4 | async-start | bytes 5308416 | tf_op jit(solution)/shard_map/reduce_scatter | solution.py:1323
  330.1 29.1 %collective-permute-start.28 = (bf16[384,1024]{1,0:T(8,128)(2,1)}, bf16[384,1024]{1,0:T(8,128)(2,1)S(1)}, u32[]{:S(2)}, u32[]{:S(2)}) collective-permute-start(bf16[384,1024]{1,0:T(8,128)(2,1)} %get-tuple-element.337), channel_id=1, source_target_pairs={{0,8},{8,0},{16,24},{24,16},{1,9},{9,1},{17,25},{25,17},{2,10},{10... | collective-permute-start | bytes 2359304 | tf_op jit(solution)/shard_map/ppermute | solution.py:1054
  330.6 28.6 %collective-permute-start.29 = (bf16[384,1024]{1,0:T(8,128)(2,1)}, bf16[384,1024]{1,0:T(8,128)(2,1)S(1)}, u32[]{:S(2)}, u32[]{:S(2)}) collective-permute-start(bf16[384,1024]{1,0:T(8,128)(2,1)} %get-tuple-element.338), channel_id=1, source_target_pairs={{0,16},{8,24},{16,0},{24,8},{1,17},{9,25},{17,1},{25,9},{2,18},{10... | collective-permute-start | bytes 2359304 | tf_op jit(solution)/shard_map/ppermute | solution.py:1054
  337.0 46.3 %collective-permute-start.31 = (bf16[768,1024]{1,0:T(8,128)(2,1)}, bf16[768,1024]{1,0:T(8,128)(2,1)}, u32[]{:S(2)}, u32[]{:S(2)}) collective-permute-start(bf16[768,1024]{1,0:T(8,128)(2,1)} %combine.11), channel_id=1, source_target_pairs={{0,16},{8,24},{16,0},{24,8},{1,17},{9,25},{17,1},{25,9},{2,18},{10... | collective-permute-start | bytes 4718600 | tf_op jit(solution)/shard_map/ppermute | solution.py:1054
  342.4 40.9 %collective-permute-start.30 = (bf16[768,1024]{1,0:T(8,128)(2,1)}, bf16[768,1024]{1,0:T(8,128)(2,1)S(1)}, u32[]{:S(2)}, u32[]{:S(2)}) collective-permute-start(bf16[768,1024]{1,0:T(8,128)(2,1)} %combine.10), channel_id=1, source_target_pairs={{0,8},{8,0},{16,24},{24,16},{1,9},{9,1},{17,25},{25,17},{2,10},{10... | collective-permute-start | bytes 4718600 | tf_op jit(solution)/shard_map/ppermute | solution.py:1054
  407.5 28.8 %collective-permute-start.35 = (bf16[240,1024]{1,0:T(8,128)(2,1)S(1)}, bf16[240,1024]{1,0:T(8,128)(2,1)}, u32[]{:S(2)}, u32[]{:S(2)}) collective-permute-start(bf16[240,1024]{1,0:T(8,128)(2,1)S(1)} %copy-done.68), channel_id=1, source_target_pairs={{0,8},{8,0},{16,24},{24,16},{1,9},{9,1},{17,25},{25,17},{2,10},{10... | collective-permute-start | bytes 1474568 | tf_op jit(solution)/shard_map/ppermute | solution.py:1054
  408.7 27.6 %collective-permute-start.36 = (bf16[240,1024]{1,0:T(8,128)(2,1)S(1)}, bf16[240,1024]{1,0:T(8,128)(2,1)}, u32[]{:S(2)}, u32[]{:S(2)}) collective-permute-start(bf16[240,1024]{1,0:T(8,128)(2,1)S(1)} %copy-done.67), channel_id=1, source_target_pairs={{0,16},{8,24},{16,0},{24,8},{1,17},{9,25},{17,1},{25,9},{2,18},{10... | collective-permute-start | bytes 1474568 | tf_op jit(solution)/shard_map/ppermute | solution.py:1054
  409.9 26.4 %collective-permute-start.37 = (bf16[240,1024]{1,0:T(8,128)(2,1)S(1)}, bf16[240,1024]{1,0:T(8,128)(2,1)}, u32[]{:S(2)}, u32[]{:S(2)}) collective-permute-start(bf16[240,1024]{1,0:T(8,128)(2,1)S(1)} %copy-done.65), channel_id=1, source_target_pairs={{0,24},{8,16},{16,8},{24,0},{1,25},{9,17},{17,9},{25,1},{2,26},{10... | collective-permute-start | bytes 1474568 | tf_op jit(solution)/shard_map/ppermute | solution.py:1054
  442.0 33.6 %collective-permute-start.40 = (bf16[768,1024]{1,0:T(8,128)(2,1)}, bf16[768,1024]{1,0:T(8,128)(2,1)S(1)}, u32[]{:S(2)}, u32[]{:S(2)}) collective-permute-start(bf16[768,1024]{1,0:T(8,128)(2,1)} %combine.15), channel_id=1, source_target_pairs={{0,16},{8,24},{16,0},{24,8},{1,17},{9,25},{17,1},{25,9},{2,18},{10... | collective-permute-start | bytes 4718600 | tf_op jit(solution)/shard_map/ppermute | solution.py:1054
  449.3 31.8 %collective-permute-start.39 = (bf16[768,1024]{1,0:T(8,128)(2,1)}, bf16[768,1024]{1,0:T(8,128)(2,1)S(1)}, u32[]{:S(2)}, u32[]{:S(2)}) collective-permute-start(bf16[768,1024]{1,0:T(8,128)(2,1)} %combine.14), channel_id=1, source_target_pairs={{0,8},{8,0},{16,24},{24,16},{1,9},{9,1},{17,25},{25,17},{2,10},{10... | collective-permute-start | bytes 4718600 | tf_op jit(solution)/shard_map/ppermute | solution.py:1054
  485.6 24.4 %collective-permute-start.38 = (bf16[2,2,112,1024]{3,2,1,0:T(8,128)(2,1)}, bf16[2,2,112,1024]{3,2,1,0:T(8,128)(2,1)}, u32[]{:S(2)}, u32[]{:S(2)}) collective-permute-start(bf16[2,2,112,1024]{3,2,1,0:T(8,128)(2,1)} %get-tuple-element.412), channel_id=1, source_target_pairs={{0,24},{8,16},{16,8},{24,0},{1,25},{9,17},{17,9},{25,1},{2,26},{10... | collective-permute-start | bytes 2752520 | tf_op jit(solution)/shard_map/ppermute | solution.py:1054
  (101 other events, 843.0 us)
Sparse Core Ops, SparseCore 0:
  12.7 175.9 all-gather.8
  190.3 84.3 all-gather.10
  276.4 82.7 all-gather.6
  361.3 53.4 reduce-scatter.2
  417.0 53.3 reduce-scatter.4

commit v4 on v3

--- a/solution.py
+++ b/solution.py
@@ -699,8 +699,43 @@
     part_refs, tail_refs = refs[:parts], refs[parts : parts + peers]
     at = parts + peers
     old_grads = refs[at : at + older]
-    out_ref, grad_ref, product_ref, dq_ref, dk_ref, dv_ref, hold_ref = refs[at + 2 * older :]
-    length, width = x_ref.shape
+    out_ref, grad_ref, product_ref, dq_ref, dk_ref, dv_ref, hold_ref = refs[
+        at + 2 * older : at + 2 * older + 7
+    ]
+    here, sems = refs[at + 2 * older + 7 : -1], refs[-1]
+    length, width = lse_ref.shape[0], x_ref.shape[1]
+    rows_here = pl.ds(step * length, length)
+    late_refs = here[parts + peers :]
+    oth_here, exit_here, qkv_here, res_here, cot_here, q_here, k_here, v_here, x_here = late_refs[:9]
+    att_here, moe_here = late_refs[9:]
+    copies = [
+        *zip(tail_refs, here[parts:]),
+        *[(a.at[rows_here], b) for a, b in zip(part_refs, here)],
+        (oth_ref.at[5:9], oth_here.at[5:9]),
+        (res_ref, res_here),
+        (cot_ref.at[rows_here], cot_here),
+        (exit_ref, exit_here),
+        (q_ref, q_here),
+        (k_ref, k_here),
+        (v_ref, v_here),
+        (oth_ref.at[0:4], oth_here.at[0:4]),
+        (qkv_ref, qkv_here),
+        (x_ref.at[rows_here], x_here),
+        (att_ref, att_here),
+        (moe_ref, moe_here),
+    ]
+    copies = [pltpu.make_async_copy(a, b, sems.at[i]) for i, (a, b) in enumerate(copies)]
+    for copy in copies:
+        copy.start()
+    waiting = iter(copies)
+
+    def await_next(count):
+        for _ in range(count):
+            next(waiting).wait()
+
+    part_refs, tail_refs = here[:parts], here[parts : parts + peers]
+    oth_ref, exit_ref, qkv_ref, res_ref, cot_ref = oth_here, exit_here, qkv_here, res_here, cot_here
+    q_ref, k_ref, v_ref, x_ref, att_ref, moe_ref = q_here, k_here, v_here, x_here, att_here, moe_here
     experts = gate_ref.shape[1]
     own = experts // peers
     capacity = (tail_refs[0].shape[0] - EXTRA) // last
@@ -710,9 +745,11 @@
 
     hits = last_hits(rank_ref, peers * last, capacity)
     hot = jnp.concatenate([jnp.where(h, 1.0, 0.0).astype(bf16) for h in hits], axis=0)
+    await_next(peers)
     tails = jnp.concatenate([ref[: last * capacity] for ref in tail_refs], axis=0)
     upstream = tn(hot, tails)
     for ref in part_refs:
+        await_next(1)
         upstream = upstream + ref[...].astype(f32)
     for k in range(peers):
         group = pl.ds(pl.multiple_of((me_ref[0] ^ k) * own, own), own)
@@ -725,6 +762,7 @@
     select = jnp.concatenate([select, jnp.zeros((LANES - experts, length), f32)], axis=0)
     logit_grad = select.T.astype(bf16)
 
+    await_next(3)
     route_lora_grad = (nt(logit_grad, rout_ref[...]) * mask).astype(bf16)
     upstream = upstream + nt(logit_grad, oth_ref[8]) + nt(route_lora_grad, oth_ref[7])
     residual = res_ref[...]
@@ -736,8 +774,10 @@
     merge_out = oth_ref[6]
     merge_in = take_rows(oth_ref[5], query_order(), HD)
     out_lora_grad = (nn(att_grad, merge_out) * mask).astype(bf16)
+    await_next(1)
     head_grad = (nt(att_grad, exit_ref[...]) + nt(out_lora_grad, merge_in)).astype(bf16)
 
+    await_next(3)
     shut = shut_of(row_ref[0])
     logs = lse_ref[...]
     for g in range(NGROUPS):
@@ -786,6 +826,7 @@
         dk_ref[:, g * SPAN : (g + 1) * SPAN] = rope(dk, cos, sin, -1.0).astype(bf16)
         dv_ref[:, g * SPAN : (g + 1) * SPAN] = jnp.concatenate(dvs, axis=0).T.astype(bf16)
 
+    await_next(5)
     dq, dk, dv = dq_ref[...], dk_ref[...], dv_ref[...]
     q_out = take_rows(oth_ref[3], query_halves(), HALF)
     k_out = take_rows(kout_ref[...], key_halves(), HALF)
@@ -868,17 +909,28 @@
     def whole(a):
         return pl.BlockSpec(a.shape, lambda i: (0,) * a.ndim)
 
+    far = pl.BlockSpec(memory_space=pl.ANY)
+    qkv, exit_full, other = weights[:3]
+    res, q, k, v, lse, att = saved[:6]
     qw, kw = H * HD, KVH * HD
+    here = [((length, width), bf16)] * len(parts) + [(a.shape, bf16) for a in tails]
+    here += [((9,) + other.shape[1:], bf16), (exit_full.shape, bf16), (qkv.shape, bf16)]
+    here += [(res.shape, f32), ((length, width), bf16), (q.shape, bf16), (k.shape, bf16)]
+    here += [(v.shape, bf16), ((length, width), bf16), (att.shape, bf16), (moe.shape, bf16)]
     ahead = 7 + len(weights) + len(saved) + 2 + len(parts) + peers
     return pl.pallas_call(
         functools.partial(attn_backward_kernel, step, peers, last, len(parts), len(older) // 2),
         grid=(1,),
-        in_specs=[pl.BlockSpec(memory_space=pltpu.SMEM), by_row(hidden), by_row(cotangent)]
+        in_specs=[pl.BlockSpec(memory_space=pltpu.SMEM), far, far]
         + [by_step(a) for a in (rows, mask)]
-        + [whole(a) for a in (cos, sin, *weights, *saved)]
-        + [whole(moe), by_step(rank)]
-        + [by_row(a) for a in parts]
-        + [whole(a) for a in tails]
+        + [whole(a) for a in (cos, sin)]
+        + [far] * 3
+        + [whole(a) for a in weights[3:]]
+        + [far] * 4
+        + [whole(lse), far]
+        + [whole(a) for a in saved[6:]]
+        + [far, by_step(rank)]
+        + [far] * (len(parts) + peers)
         + ([whole(older[0]), pl.BlockSpec(memory_space=pl.ANY)] if older else []),
         out_specs=[by_row(hidden), whole(grads)],
         out_shape=[jax.ShapeDtypeStruct(hidden.shape, bf16), grads],
@@ -888,6 +940,8 @@
             pltpu.VMEM((length, kw), bf16),
             pltpu.VMEM((length, kw), bf16),
             pltpu.VMEM((LANES, max(width, qw)), f32),
+            *[pltpu.VMEM(*a) for a in here],
+            pltpu.SemaphoreType.DMA((len(here) + 1,)),
         ],
         compiler_params=pltpu.CompilerParams(vmem_limit_bytes=VMEM),
         cost_estimate=pl.CostEstimate(
@@ -914,7 +968,7 @@
     out_ref[...] = (res_ref[...] + total).astype(bf16)
 
 
-def add_mixture(step, total, residual, rank, own, far, parts, older):
+def add_mixture(step, total, residual, rank, own, far, early, parts, older):
     length, width = residual.shape
 
     def by_step(a):
@@ -927,7 +981,8 @@
         mixture_kernel,
         grid=(1,),
         in_specs=[whole(residual), by_step(rank), by_step(own), by_step(far)]
-        + [pl.BlockSpec((length, width), lambda i: (step, 0))] * len(parts)
+        + [pl.BlockSpec((length, width), lambda i: (step, 0))]
+        + [whole(a) for a in parts]
         + [pl.BlockSpec(memory_space=pl.ANY)] * len(older),
         out_specs=pl.BlockSpec((length, width), lambda i: (step, 0)),
         out_shape=jax.ShapeDtypeStruct((total * length, width), bf16),
@@ -935,9 +990,9 @@
         cost_estimate=pl.CostEstimate(
             flops=2 * length * 256 * width, bytes_accessed=16 * length * width, transcendentals=0
         ),
-        input_output_aliases={4 + len(parts): 0} if older else {},
+        input_output_aliases={5 + len(parts): 0} if older else {},
         name="mixture",
-    )(residual, rank, own, far, *parts, *older)
+    )(residual, rank, own, far, early, *parts, *older)
 
 
 def finish_experts_kernel(chunks, *refs):
@@ -1301,9 +1356,14 @@
     )
     tails, filled = [], []
 
+
+    def mixes_of(m, rows):
+        return combine(slots, [(k, rows[k], m) for k in (1, 2)], apart=True, add=(1 - m, passed_mixes[m], 0))
+
     for m in micro:
         if m == micro_count - 1:
-            chunk, back_home = lax.optimization_barrier((chunk, back_home))
+            mixes = mixes_of(0, {k: rows_of(k) + [filled[k]] for k in (1, 2)})
+            chunk, back_home, mixes = lax.optimization_barrier((chunk, back_home, mixes))
         out = expert_chunk(
             [slots[m]], chunk, masks[m : m + 1], first, inner_width, first - head,
             local_experts - head, grads, [products[m]], m > 0, (micro_count, m), filled,
@@ -1328,25 +1388,20 @@
     older = []
     for m in micro:
         if m == micro_count - 1:
-            back_last[m], head_sum, older, mix_rows = lax.optimization_barrier(
-                (back_last[m], head_sum, older, mix_rows)
+            mix_rows, older = lax.optimization_barrier((mix_rows, older))
+            then = mixes_of(1, mix_rows)
+            back_last[m], head_sum, older, mixes, then = lax.optimization_barrier(
+                (back_last[m], head_sum, older, mixes, then)
             )
-            mixes = [
-                combine(slots, [(k, mix_rows[k], i) for i in micro], add=(2 - k, passed_mixes[2 - k], 0))
-                for k in (1, 2)
-            ]
-            mix_home = [exchange(a, k) for k, a in zip((1, 2), mixes)]
-            back_last[m], mixes, far_last = lax.optimization_barrier(
-                (back_last[m], mixes, filled[3])
-            )
-            far_last = exchange(far_last, 3)
+            mix_home = [[exchange(a, k) for k, a in zip((1, 2), pair)] for pair in (mixes, then)]
         grad_input, attn_grads = attn_backward(
             m, last, me, layer_entering_state, exit_cotangent, section_rows, own_mask,
             cos_table, sin_table, weights, saved[m], sent[m][0], rank_last, [own_back, *back_home], back_last[m],
             older,
         )
         older = [attn_grads, grad_input]
-    attn_grads, mix_home = lax.optimization_barrier((attn_grads, mix_home))
+    attn_grads, mix_home, far_last = lax.optimization_barrier((attn_grads, mix_home, filled[3]))
+    far_last = exchange(far_last, 3)
 
     if shard_count == SHARDS:
         received = lax.all_to_all(attn_grads, "fsdp", split_axis=0, concat_axis=0, tiled=True)
@@ -1362,8 +1417,7 @@
     for m in micro:
         block_out = [
             add_mixture(
-                m, micro_count, saved[m][0], rank_far, filled[0], far_last, [own_mix, *mix_home],
-                block_out,
+                m, micro_count, saved[m][0], rank_far, filled[0], far_last, own_mix, mix_home[m], block_out,
             )
         ]
     return (*block_out, grad_input, *attn_out, *expert_out)

time: 537 us -> 532 us (level)
    ppermute x36 -> x38, waiting for transfers between devices: 87.4 us -> 81.5 us  [exchange(): return lax.ppermute(a, 'dp', [(i, i ^ k) for i in range(size)])]
    ppermute x36 -> x38, starting transfers between devices: 44 us -> 45.7 us  [exchange(): return lax.ppermute(a, 'dp', [(i, i ^ k) for i in range(size)])]
    unnamed x176 -> x186, local copies, waits for them, and re-layouts: 14.3 us -> 15.9 us
  transfers between devices with their start and end apart: 50 -> 52, of which waited for: 21 -> 21; matrix products, arithmetic and copies ran while one was open for 5% -> 5% of each run, Pallas kernels for 56% -> 56%
where the time goes in v4:
time: 532 us; the launch traced here: 527 us
  Pallas kernels  295 us (55%)
  waiting for transfers between devices  116 us (22%)
  starting transfers between devices  58 us (11%)
  local copies, waits for them, and re-layouts  31.2 us (6%)
  between operations  15.3 us (3%)
  other arithmetic  10.8 us (2%)
    pallas_call x4, Pallas kernels, expert_chunk(): pl.pallas_call(functools.partial(expert_kernel, first, micro, len(held),...  119 us
    ppermute x38, waiting for transfers between devices, exchange(): return lax.ppermute(a, 'dp', [(i, i ^ k) for i in range(size)])  81.5 us
    pallas_call x2, Pallas kernels, attn_backward(): pl.pallas_call(functools.partial(attn_backward_kernel, step, peers, last,...  48.1 us
    ppermute x38, starting transfers between devices, exchange(): return lax.ppermute(a, 'dp', [(i, i ^ k) for i in range(size)])  45.7 us
    pallas_call x8, Pallas kernels, combine(): pl.pallas_call(functools.partial(combine_kernel, chunks, len(jobs), added...  38.6 us
    pallas_call x2, Pallas kernels, attn_forward(): pl.pallas_call(attn_forward_kernel, grid=(1,), in_specs=[pl.BlockSpec(mem...  36.1 us
    pallas_call x2, Pallas kernels, dispatch(): pl.pallas_call(functools.partial(dispatch_kernel, peers, capacity), grid=...  27.2 us
    unnamed x186, local copies, waits for them, and re-layouts  15.9 us
  transfers between devices with their start and end apart: 52, of which 21 were waited for; matrix products, arithmetic and copies ran while one was open for 5% of the time, Pallas kernels for 56%

profile of v4, /device:TPU:0, one launch (start us, length us, event | category | flops | bytes accessed | tf_op | source)
XLA Modules:
  0.0 526.6 jit_solution(4767614974494348855)
XLA Ops:
  42.3 13.9 %collective-permute-done.2 = bf16[1152,128]{1,0:T(8,128)(2,1)} collective-permute-done((bf16[1152,128]{1,0:T(8,128)(2,1)}, bf16[1152,128]{1,0:T(8,128)(2,1)}, u32[]{:S(2)}, u32[]{:S(2)}) %collective-permute-start.2) | collective-permute-done | bytes 294944 | tf_op jit(solution)/shard_map/ppermute | solution.py:1250
  66.6 23.9 %collective-permute-done.7.refs_2_ = bf16[4,1152,128]{2,1,0:T(8,128)(2,1)S(1)} collective-permute-done((bf16[4,1152,128]{2,1,0:T(8,128)(2,1)S(1)}, bf16[4,1152,128]{2,1,0:T(8,128)(2,1)S(1)}, u32[]{:S(2)}, u32[]{:S(2)}) %collective-permute-start.7) | collective-permute-done | bytes 1179680 | tf_op jit(solution)/shard_map/ppermute | solution.py:1109
  94.3 9.0 %collective-permute-done.8.refs_3_ = bf16[2,1152,128]{2,1,0:T(8,128)(2,1)S(1)} collective-permute-done((bf16[2,1152,128]{2,1,0:T(8,128)(2,1)S(1)}, bf16[2,1152,128]{2,1,0:T(8,128)(2,1)S(1)}, u32[]{:S(2)}, u32[]{:S(2)}) %collective-permute-start.8) | collective-permute-done | bytes 589856 | tf_op jit(solution)/shard_map/ppermute | solution.py:1109
  109.9 9.6 %unpack.1 = (bf16[1024,2048]{1,0:T(8,128)(2,1)}, bf16[1024,1024]{1,0:T(8,128)(2,1)}, bf16[12,1024,128]{2,1,0:T(8,128)(2,1)}) custom-call(s32[5]{0:T(128)} %pad_add_fusion.me_ref, bf16[4,1152,128]{2,1,0:T(8,128)(2,1)} %copy-done.1, bf16[4,1152,128]{2,1,0:T(8,128)(2,1)} %copy-done.4, bf16[4,1152,128]{2,1,0:T(8,128)(2,1)} %copy-done.3, ...), custom_call_target="tpu_custom_call" | custom-call | tf_op jit(solution)/shard_map/unpack/pallas_call | solution.py:553
  122.6 18.2 %attention_forward.2 = (f32[384,1024]{1,0:T(8,128)}, bf16[384,1024]{1,0:T(8,128)(2,1)}, bf16[384,512]{1,0:T(8,128)(2,1)}, bf16[384,512]{1,0:T(8,128)(2,1)}, f32[...) custom-call(s32[5]{0:T(128)} %pad_add_fusion.me_ref, ...), custom_call_target="tpu_custom_call" | custom-call | flops 5234491392 | bytes 20971520 | tf_op jit(solution)/shard_map/attention_forward/pallas_call | solution.py:671
  145.9 17.8 %attention_forward.3 = (f32[384,1024]{1,0:T(8,128)}, bf16[384,1024]{1,0:T(8,128)(2,1)}, bf16[384,512]{1,0:T(8,128)(2,1)}, bf16[384,512]{1,0:T(8,128)(2,1)}, f32[...) custom-call(s32[5]{0:T(128)} %pad_add_fusion.me_ref, ...), custom_call_target="tpu_custom_call" | custom-call | flops 5234491392 | bytes 20971520 | tf_op jit(solution)/shard_map/attention_forward/pallas_call | solution.py:671
  166.6 7.5 %collective-permute-done.21.refs_4_ = bf16[192,1024]{1,0:T(8,128)(2,1)S(1)} collective-permute-done((bf16[192,1024]{1,0:T(8,128)(2,1)S(1)}, bf16[192,1024]{1,0:T(8,128)(2,1)S(1)}, u32[]{:S(2)}, u32[]{:S(2)}) %collective-permute-start.21) | collective-permute-done | bytes 393248 | tf_op jit(solution)/shard_map/ppermute | solution.py:1109
  177.2 13.7 %dispatch.2 = (bf16[4,8,112,1024]{3,2,1,0:T(8,128)(2,1)}, bf16[4,8,112,1024]{3,2,1,0:T(8,128)(2,1)}, f32[4,8,112,128]{3,2,1,0:T(8,128)}, f32[4,8,384]{2,1,0:T(8,128)}, f32[4,384,128]{2,1,0:T(8,128)}) custom-call(bf16[416,1024]{1,0:T(8,128)(2,1)} %get-tuple-element.289.refs_0_.moe_ref, bf16[416,1024]{1,0:T(8,128)(2,1)} %copy-done.39, ...), custom_call_target="tpu_custom_call" | custom-call | flops 5637144576 | bytes 29360128 | tf_op jit(solution)/shard_map/dispatch/pallas_call | solution.py:163
  197.4 6.0 %collective-permute-done.25.refs_4_ = bf16[192,1024]{1,0:T(8,128)(2,1)S(1)} collective-permute-done((bf16[192,1024]{1,0:T(8,128)(2,1)S(1)}, bf16[192,1024]{1,0:T(8,128)(2,1)S(1)}, u32[]{:S(2)}, u32[]{:S(2)}) %collective-permute-start.25) | collective-permute-done | bytes 393248 | tf_op jit(solution)/shard_map/ppermute | solution.py:1109
  205.0 13.5 %dispatch.3 = (bf16[4,8,112,1024]{3,2,1,0:T(8,128)(2,1)}, bf16[4,8,112,1024]{3,2,1,0:T(8,128)(2,1)}, f32[4,8,112,128]{3,2,1,0:T(8,128)}, f32[4,8,384]{2,1,0:T(8,128)}, f32[4,384,128]{2,1,0:T(8,128)}) custom-call(bf16[416,1024]{1,0:T(8,128)(2,1)} %get-tuple-element.292.refs_0_.moe_ref, bf16[416,1024]{1,0:T(8,128)(2,1)} %copy-done.40, ...), custom_call_target="tpu_custom_call" | custom-call | flops 5637144576 | bytes 29360128 | tf_op jit(solution)/shard_map/dispatch/pallas_call | solution.py:163
  219.1 52.9 %experts.4 = (bf16[2,4,112,1024]{3,2,1,0:T(8,128)(2,1)}, bf16[2,4,112,1024]{3,2,1,0:T(8,128)(2,1)}, bf16[2,4,112,1024]{3,2,1,0:T(8,128)(2,1)}, bf16[2,4,112,1024...) custom-call(f32[4,8,384]{2,1,0:T(8,128)} %get-tuple-element.322.refs, ...), custom_call_target="tpu_custom_call" | custom-call | flops 35840000000 | bytes 81264640 | tf_op jit(solution)/shard_map/experts/pallas_call | solution.py:342
  274.8 29.8 %experts.5 = (bf16[2,2,112,1024]{3,2,1,0:T(8,128)(2,1)}, bf16[2,2,112,1024]{3,2,1,0:T(8,128)(2,1)}, bf16[2,2,112,1024]{3,2,1,0:T(8,128)(2,1)}, bf16[2,2,112,1024...) custom-call(f32[4,8,384]{2,1,0:T(8,128)} %get-tuple-element.322.refs, ...), custom_call_target="tpu_custom_call" | custom-call | flops 17920000000 | bytes 40632320 | tf_op jit(solution)/shard_map/experts/pallas_call | solution.py:342
  316.3 12.6 %collective-permute-done.26.refs_6_ = bf16[384,1024]{1,0:T(8,128)(2,1)S(1)} collective-permute-done((bf16[384,1024]{1,0:T(8,128)(2,1)}, bf16[384,1024]{1,0:T(8,128)(2,1)S(1)}, u32[]{:S(2)}, u32[]{:S(2)}) %collective-permute-start.26) | collective-permute-done | bytes 786464 | tf_op jit(solution)/shard_map/ppermute | solution.py:1109
  332.2 4.9 combine.11
  337.6 4.8 combine.10
  353.8 5.4 %all-gather.7.cloned.1.call-done = bf16[16,2112,128]{2,1,0:T(8,128)(2,1)} async-done(((bf16[2,2112,128]{2,1,0:T(8,128)(2,1)}), bf16[16,2112,128]{2,1,0:T(8,128)(2,1)}) %all-gather.7.cloned.1.call-update) | async-done | bytes 8650768 | tf_op jit(solution)/shard_map/all_gather | solution.py:1197
  359.2 17.8 %experts.6 = (bf16[2,2,112,1024]{3,2,1,0:T(8,128)(2,1)}, bf16[2,2,112,1024]{3,2,1,0:T(8,128)(2,1)}, bf16[2,2,112,1024]{3,2,1,0:T(8,128)(2,1)}, bf16[2,2,112,1024...) custom-call(f32[4,8,384]{2,1,0:T(8,128)} %get-tuple-element.322.refs, ...), custom_call_target="tpu_custom_call", output_to_operand_aliasing={{8}: (7, {})} | custom-call | flops 8960000000 | bytes 33292288 | tf_op jit(solution)/shard_map/experts/pallas_call | solution.py:342
  377.1 5.5 %combine.14 = (bf16[384,1024]{1,0:T(8,128)(2,1)}, bf16[384,1024]{1,0:T(8,128)(2,1)}) custom-call(f32[4,384,128]{2,1,0:T(8,128)} %get-tuple-element.320.refs_0_.refs_1_, f32[4,384,128]{2,1,0:T(8,128)} %get-tuple-element.320.refs_0_.refs_1_, bf16[2,4,112,1024]{3,2,1,0:T(8,128)(2,1)} %get-tuple-element.425.refs_2_, ...), custom_call_target="tpu_custom_call" | custom-call | flops 1409286144 | bytes 5505024 | tf_op jit(solution)/shard_map/combine/pallas_call | solution.py:426
  386.9 18.3 %experts.7 = (bf16[2,2,112,1024]{3,2,1,0:T(8,128)(2,1)}, bf16[2,2,112,1024]{3,2,1,0:T(8,128)(2,1)}, bf16[2,2,112,1024]{3,2,1,0:T(8,128)(2,1)}, bf16[2,2,112,1024...) custom-call(f32[4,8,384]{2,1,0:T(8,128)} %get-tuple-element.310.refs, ...), custom_call_target="tpu_custom_call", output_to_operand_aliasing={{8}: (7, {}), {0}: (8, {}), {1}: (9, {}), {2}: (10, {}), {3... | custom-call | flops 8960000000 | bytes 33292288 | tf_op jit(solution)/shard_map/experts/pallas_call | solution.py:342
  412.4 23.9 %attention_backward.2 = (bf16[768,1024]{1,0:T(8,128)(2,1)}, bf16[8,144,128]{2,1,0:T(8,128)(2,1)}) custom-call(s32[5]{0:T(128)} %pad_add_fusion.me_ref, bf16[768,1024]{1,0:T(8,128)(2,1)} %x_ref.7, bf16[768,1024]{1,0:T(8,128)(2,1)} %cot_ref.3, s32[2,1,384]{2,1,0:T(1,128)} %broadcast_in_dim.30.row_ref, f32[2,1,128]{2,1,0:T(1,128)} %copy-done.58, ...), custom_call_target="tpu_custom_call" | custom-call | flops 7851737088 | bytes 31457280 | tf_op jit(solution)/shard_map/attention_backward/pallas_call | solution.py:921
  436.3 5.4 %combine.15 = (bf16[384,1024]{1,0:T(8,128)(2,1)}, bf16[384,1024]{1,0:T(8,128)(2,1)}) custom-call(f32[4,384,128]{2,1,0:T(8,128)} %get-tuple-element.321.refs_1_.refs_0_, f32[4,384,128]{2,1,0:T(8,128)} %get-tuple-element.321.refs_1_.refs_0_, bf16[2,4,112,1024]{3,2,1,0:T(8,128)(2,1)} %get-tuple-element.425.refs_2_, ...), custom_call_target="tpu_custom_call" | custom-call | flops 1409286144 | bytes 5505024 | tf_op jit(solution)/shard_map/combine/pallas_call | solution.py:426
  445.9 24.3 %attention_backward.3 = (bf16[768,1024]{1,0:T(8,128)(2,1)}, bf16[8,288,128]{2,1,0:T(8,128)(2,1)}) custom-call(s32[5]{0:T(128)} %pad_add_fusion.me_ref, bf16[768,1024]{1,0:T(8,128)(2,1)} %x_ref.7, bf16[768,1024]{1,0:T(8,128)(2,1)} %cot_ref.3, s32[2,1,384]{2,1,0:T(1,128)} %broadcast_in_dim.30.row_ref, ...), custom_call_target="tpu_custom_call", output_to_operand_aliasing={{0}: (34, {})} | custom-call | flops 7851737088 | bytes 31457280 | tf_op jit(solution)/shard_map/attention_backward/pallas_call | solution.py:921
  470.2 5.8 %collective-permute-done.40.refs_1_ = bf16[384,1024]{1,0:T(8,128)(2,1)} collective-permute-done((bf16[384,1024]{1,0:T(8,128)(2,1)}, bf16[384,1024]{1,0:T(8,128)(2,1)}, u32[]{:S(2)}, u32[]{:S(2)}) %collective-permute-start.40) | collective-permute-done | bytes 786464 | tf_op jit(solution)/shard_map/ppermute | solution.py:1109
  484.7 12.7 %all-to-all-done.g_ref = bf16[8,288,128]{2,1,0:T(8,128)(2,1)S(1)} async-done(((bf16[8,288,128]{2,1,0:T(8,128)(2,1)}), bf16[8,288,128]{2,1,0:T(8,128)(2,1)S(1)}, u32[]{:S(2)}, u32[]{:S(2)}) %all-to-all-start) | async-done | bytes 589856 | tf_op jit(solution)/shard_map/all_to_all | solution.py:1407
  (364 shorter events, 153.8 us)
Async XLA Ops:
  7.2 211.3 %all-gather.9.cloned.1.call-start = ((), (), s32[]{:S(2)}) async-start(), calls=%async_computation.6 | async-start | bytes 19464192 | tf_op jit(solution)/shard_map/all_gather | solution.py:1197
  12.6 262.2 %all-gather.11.cloned.1.call-start = ((), (), s32[]{:S(2)}) async-start(), calls=%async_computation.7 | async-start | bytes 9732096 | tf_op jit(solution)/shard_map/all_gather | solution.py:1197
  22.8 34.6 %collective-permute-start.3 = (bf16[384,1024]{1,0:T(8,128)(2,1)}, bf16[384,1024]{1,0:T(8,128)(2,1)}, u32[]{:S(2)}, u32[]{:S(2)}) collective-permute-start(bf16[384,1024]{1,0:T(8,128)(2,1)} %get-tuple-element.295.refs_5_), channel_id=1, source_target_pairs={{0,8},{8,0},{16,24},{24,16},{1,9},{9,1},{17,25},{25,17},{2,10},{10... | collective-permute-start | bytes 2359304 | tf_op jit(solution)/shard_map/ppermute | solution.py:1109
  24.3 35.6 %collective-permute-start.4 = (bf16[384,1024]{1,0:T(8,128)(2,1)}, bf16[384,1024]{1,0:T(8,128)(2,1)}, u32[]{:S(2)}, u32[]{:S(2)}) collective-permute-start(bf16[384,1024]{1,0:T(8,128)(2,1)} %get-tuple-element.295.refs_5_), channel_id=1, source_target_pairs={{0,16},{8,24},{16,0},{24,8},{1,17},{9,25},{17,1},{25,9},{2,18},{10... | collective-permute-start | bytes 2359304 | tf_op jit(solution)/shard_map/ppermute | solution.py:1109
  25.8 34.1 %collective-permute-start.5 = (bf16[384,1024]{1,0:T(8,128)(2,1)}, bf16[384,1024]{1,0:T(8,128)(2,1)}, u32[]{:S(2)}, u32[]{:S(2)}) collective-permute-start(bf16[384,1024]{1,0:T(8,128)(2,1)} %get-tuple-element.295.refs_5_), channel_id=1, source_target_pairs={{0,24},{8,16},{16,8},{24,0},{1,25},{9,17},{17,9},{25,1},{2,26},{10... | collective-permute-start | bytes 2359304 | tf_op jit(solution)/shard_map/ppermute | solution.py:1109
  62.0 297.2 %all-gather.7.cloned.1.call-start = ((), (), s32[]{:S(2)}) async-start(), calls=%async_computation.5 | async-start | bytes 9732096 | tf_op jit(solution)/shard_map/all_gather | solution.py:1197
  64.2 377.6 %reduce-scatter.3.cloned.1.call-start = ((), (), s32[]{:S(2)}) async-start(), calls=%async_computation.3 | async-start | bytes 5308416 | tf_op jit(solution)/shard_map/reduce_scatter | solution.py:1334
  64.5 26.1 %collective-permute-start.7 = (bf16[4,1152,128]{2,1,0:T(8,128)(2,1)S(1)}, bf16[4,1152,128]{2,1,0:T(8,128)(2,1)S(1)}, u32[]{:S(2)}, u32[]{:S(2)}) collective-permute-start(bf16[4,1152,128]{2,1,0:T(8,128)(2,1)S(1)} %pad_maximum_fusion.refs_0_), channel_id=1, source_target_pairs={{0,16},{8,24},{16,0},{24,8},{1,17},{9,25},{17,1},{25,9},{2,18},{10... | collective-permute-start | bytes 3538952 | tf_op jit(solution)/shard_map/ppermute | solution.py:1109
  66.6 38.8 %collective-permute-start.10 = (bf16[4,1152,128]{2,1,0:T(8,128)(2,1)S(1)}, bf16[4,1152,128]{2,1,0:T(8,128)(2,1)S(1)}, u32[]{:S(2)}, u32[]{:S(2)}) collective-permute-start(bf16[4,1152,128]{2,1,0:T(8,128)(2,1)S(1)} %pad_maximum_fusion.refs_0_), channel_id=1, source_target_pairs={{0,1},{1,0},{2,3},{3,2},{4,5},{5,4},{6,7},{7,6},{8,9},{9,8},{10,11... | collective-permute-start | bytes 3538952 | tf_op jit(solution)/shard_map/ppermute | solution.py:1264
  105.4 35.5 %collective-permute-start.15 = (bf16[384,1024]{1,0:T(8,128)(2,1)}, bf16[384,1024]{1,0:T(8,128)(2,1)S(1)}, u32[]{:S(2)}, u32[]{:S(2)}) collective-permute-start(bf16[384,1024]{1,0:T(8,128)(2,1)} %get-tuple-element.306.refs_5_), channel_id=1, source_target_pairs={{0,8},{8,0},{16,24},{24,16},{1,9},{9,1},{17,25},{25,17},{2,10},{10... | collective-permute-start | bytes 2359304 | tf_op jit(solution)/shard_map/ppermute | solution.py:1109
  106.0 36.4 %collective-permute-start.16 = (bf16[384,1024]{1,0:T(8,128)(2,1)}, bf16[384,1024]{1,0:T(8,128)(2,1)S(1)}, u32[]{:S(2)}, u32[]{:S(2)}) collective-permute-start(bf16[384,1024]{1,0:T(8,128)(2,1)} %get-tuple-element.306.refs_5_), channel_id=1, source_target_pairs={{0,16},{8,24},{16,0},{24,8},{1,17},{9,25},{17,1},{25,9},{2,18},{10... | collective-permute-start | bytes 2359304 | tf_op jit(solution)/shard_map/ppermute | solution.py:1109
  107.5 34.9 %collective-permute-start.17 = (bf16[384,1024]{1,0:T(8,128)(2,1)}, bf16[384,1024]{1,0:T(8,128)(2,1)}, u32[]{:S(2)}, u32[]{:S(2)}) collective-permute-start(bf16[384,1024]{1,0:T(8,128)(2,1)} %get-tuple-element.306.refs_5_), channel_id=1, source_target_pairs={{0,24},{8,16},{16,8},{24,0},{1,25},{9,17},{17,9},{25,1},{2,26},{10... | collective-permute-start | bytes 2359304 | tf_op jit(solution)/shard_map/ppermute | solution.py:1109
  272.1 209.5 %reduce-scatter.5.cloned.1.call-start = ((), (), s32[]{:S(2)}) async-start(), calls=%async_computation.4 | async-start | bytes 5308416 | tf_op jit(solution)/shard_map/reduce_scatter | solution.py:1383
  330.1 29.1 %collective-permute-start.28 = (bf16[384,1024]{1,0:T(8,128)(2,1)}, bf16[384,1024]{1,0:T(8,128)(2,1)S(1)}, u32[]{:S(2)}, u32[]{:S(2)}) collective-permute-start(bf16[384,1024]{1,0:T(8,128)(2,1)} %get-tuple-element.347), channel_id=1, source_target_pairs={{0,8},{8,0},{16,24},{24,16},{1,9},{9,1},{17,25},{25,17},{2,10},{10... | collective-permute-start | bytes 2359304 | tf_op jit(solution)/shard_map/ppermute | solution.py:1109
  330.7 28.5 %collective-permute-start.29 = (bf16[384,1024]{1,0:T(8,128)(2,1)}, bf16[384,1024]{1,0:T(8,128)(2,1)S(1)}, u32[]{:S(2)}, u32[]{:S(2)}) collective-permute-start(bf16[384,1024]{1,0:T(8,128)(2,1)} %get-tuple-element.348), channel_id=1, source_target_pairs={{0,16},{8,24},{16,0},{24,8},{1,17},{9,25},{17,1},{25,9},{2,18},{10... | collective-permute-start | bytes 2359304 | tf_op jit(solution)/shard_map/ppermute | solution.py:1109
  337.1 46.2 %collective-permute-start.31 = (bf16[768,1024]{1,0:T(8,128)(2,1)}, bf16[768,1024]{1,0:T(8,128)(2,1)}, u32[]{:S(2)}, u32[]{:S(2)}) collective-permute-start(bf16[768,1024]{1,0:T(8,128)(2,1)} %combine.11), channel_id=1, source_target_pairs={{0,16},{8,24},{16,0},{24,8},{1,17},{9,25},{17,1},{25,9},{2,18},{10... | collective-permute-start | bytes 4718600 | tf_op jit(solution)/shard_map/ppermute | solution.py:1109
  342.5 40.8 %collective-permute-start.30 = (bf16[768,1024]{1,0:T(8,128)(2,1)}, bf16[768,1024]{1,0:T(8,128)(2,1)S(1)}, u32[]{:S(2)}, u32[]{:S(2)}) collective-permute-start(bf16[768,1024]{1,0:T(8,128)(2,1)} %combine.10), channel_id=1, source_target_pairs={{0,8},{8,0},{16,24},{24,16},{1,9},{9,1},{17,25},{25,17},{2,10},{10... | collective-permute-start | bytes 4718600 | tf_op jit(solution)/shard_map/ppermute | solution.py:1109
  408.9 32.8 %collective-permute-start.35 = (bf16[240,1024]{1,0:T(8,128)(2,1)S(1)}, bf16[240,1024]{1,0:T(8,128)(2,1)S(1)}, u32[]{:S(2)}, u32[]{:S(2)}) collective-permute-start(bf16[240,1024]{1,0:T(8,128)(2,1)S(1)} %copy-done.70), channel_id=1, source_target_pairs={{0,8},{8,0},{16,24},{24,16},{1,9},{9,1},{17,25},{25,17},{2,10},{10... | collective-permute-start | bytes 1474568 | tf_op jit(solution)/shard_map/ppermute | solution.py:1109
  410.1 31.7 %collective-permute-start.36 = (bf16[240,1024]{1,0:T(8,128)(2,1)S(1)}, bf16[240,1024]{1,0:T(8,128)(2,1)}, u32[]{:S(2)}, u32[]{:S(2)}) collective-permute-start(bf16[240,1024]{1,0:T(8,128)(2,1)S(1)} %copy-done.68), channel_id=1, source_target_pairs={{0,16},{8,24},{16,0},{24,8},{1,17},{9,25},{17,1},{25,9},{2,18},{10... | collective-permute-start | bytes 1474568 | tf_op jit(solution)/shard_map/ppermute | solution.py:1109
  411.0 30.8 %collective-permute-start.37 = (bf16[240,1024]{1,0:T(8,128)(2,1)S(1)}, bf16[240,1024]{1,0:T(8,128)(2,1)}, u32[]{:S(2)}, u32[]{:S(2)}) collective-permute-start(bf16[240,1024]{1,0:T(8,128)(2,1)S(1)} %copy-done.67), channel_id=1, source_target_pairs={{0,24},{8,16},{16,8},{24,0},{1,25},{9,17},{17,9},{25,1},{2,26},{10... | collective-permute-start | bytes 1474568 | tf_op jit(solution)/shard_map/ppermute | solution.py:1109
  441.8 28.4 %collective-permute-start.38 = (bf16[384,1024]{1,0:T(8,128)(2,1)}, bf16[384,1024]{1,0:T(8,128)(2,1)S(1)}, u32[]{:S(2)}, u32[]{:S(2)}) collective-permute-start(bf16[384,1024]{1,0:T(8,128)(2,1)} %get-tuple-element.441), channel_id=1, source_target_pairs={{0,8},{8,0},{16,24},{24,16},{1,9},{9,1},{17,25},{25,17},{2,10},{10... | collective-permute-start | bytes 2359304 | tf_op jit(solution)/shard_map/ppermute | solution.py:1109
  443.0 27.2 %collective-permute-start.39 = (bf16[384,1024]{1,0:T(8,128)(2,1)S(1)}, bf16[384,1024]{1,0:T(8,128)(2,1)}, u32[]{:S(2)}, u32[]{:S(2)}) collective-permute-start(bf16[384,1024]{1,0:T(8,128)(2,1)S(1)} %copy-done.63), channel_id=1, source_target_pairs={{0,16},{8,24},{16,0},{24,8},{1,17},{9,25},{17,1},{25,9},{2,18},{10... | collective-permute-start | bytes 2359304 | tf_op jit(solution)/shard_map/ppermute | solution.py:1109
  443.9 32.2 %collective-permute-start.40 = (bf16[384,1024]{1,0:T(8,128)(2,1)}, bf16[384,1024]{1,0:T(8,128)(2,1)}, u32[]{:S(2)}, u32[]{:S(2)}) collective-permute-start(bf16[384,1024]{1,0:T(8,128)(2,1)} %get-tuple-element.443), channel_id=1, source_target_pairs={{0,8},{8,0},{16,24},{24,16},{1,9},{9,1},{17,25},{25,17},{2,10},{10... | collective-permute-start | bytes 2359304 | tf_op jit(solution)/shard_map/ppermute | solution.py:1109
  445.4 31.7 %collective-permute-start.41 = (bf16[384,1024]{1,0:T(8,128)(2,1)}, bf16[384,1024]{1,0:T(8,128)(2,1)}, u32[]{:S(2)}, u32[]{:S(2)}) collective-permute-start(bf16[384,1024]{1,0:T(8,128)(2,1)} %get-tuple-element.444), channel_id=1, source_target_pairs={{0,16},{8,24},{16,0},{24,8},{1,17},{9,25},{17,1},{25,9},{2,18},{10... | collective-permute-start | bytes 2359304 | tf_op jit(solution)/shard_map/ppermute | solution.py:1109
  (108 other events, 944.9 us)
Sparse Core Ops, SparseCore 0:
  12.7 175.9 all-gather.8
  190.4 84.3 all-gather.10
  276.4 82.7 all-gather.6
  361.3 53.4 reduce-scatter.2
  417.0 53.3 reduce-scatter.4
